TPU v7x, 32 devices: a whole 2x2x4 slice. The times are simulated.
32 devices in a mesh: frame: 8 (over y, x, core), head: 4 (over z).
Axes of the slice: x: 2, y: 2, z: 4, core: 2. Of those that a mesh axis runs over, the one named last changes fastest.
Arguments:
- queries: bfloat16 [16, 512, 3072], P('frame', None, 'head'), may hold values from -24 to 24
- keys: bfloat16 [16, 512, 3072], P('frame', None, 'head'), may hold values from -24 to 24
- values: bfloat16 [16, 512, 3072], P('frame', None, 'head'), may hold values from -6 to 6
- ref_keys: bfloat16 [512, 3072], P('frame', 'head'), may hold values from -24 to 24
- ref_values: bfloat16 [512, 3072], P('frame', 'head'), may hold values from -6 to 6
- rate_scale: float32 [24], P('head'), may hold values from 0.05 to 2
- rate_reach: float32 [24], P('head'), may hold values from 0.1 to 4
- window_start: int32 [16], replicated, may hold values from 0 to 15, as said below
- out_weight: bfloat16 [3072, 3072], P('head'), may hold values from -0.15625 to 0.15625
- conv_taps: float32 [3, 3072], P(None, 'head'), may hold values from -3 to 3
- cotangent: bfloat16 [16, 512, 3072], P('frame', None, 'head'), may hold values from -6 to 6
Outputs:
- block_out: bfloat16 [16, 512, 3072], P('frame', None, 'head')
- grad_queries: bfloat16 [16, 512, 3072], P('frame', None, 'head')
- grad_keys: bfloat16 [16, 512, 3072], P('frame', None, 'head')
- grad_values: bfloat16 [16, 512, 3072], P('frame', None, 'head')
- grad_ref_keys: float32 [512, 3072], P('frame', 'head')
- grad_ref_values: float32 [512, 3072], P('frame', 'head')
- grad_out_weight: float32 [3072, 3072], P('head', 'frame')
- grad_conv_taps: float32 [3, 3072], P(None, 'head')
Inputs may be any that keep to these rules, and one draw needn't show every extreme that they name: window_start[f] <= f for every frame f.
All inputs are finite; a program needn't handle non-finite values.
Results may differ from a plain program's by a relative error of at most 0.015.
Values may be sent and summed in bfloat16 or wider, within the bound.
No kernel may reach another device: no remote copies, remote signals or barrier semaphores. Data moves between devices by JAX's collectives and lax.ppermute only.
A program may use at most 128 MiB of HBM per device.

v0:
```python
import jax
import jax.numpy as jnp
from jax import lax
from jax.sharding import PartitionSpec as P

HEAD_DIM = 128


def shifted(value, axis, steps):
    count = lax.axis_size(axis)
    initial, last = (max(0, -steps), min(count, count - steps))
    return lax.ppermute(value, axis, [(source, source + steps) for source in range(initial, last)])


def kerple_bias(rate_scale, rate_reach, starts):
    count = starts.shape[0]
    places = jnp.arange(count, dtype=jnp.int32)
    distance = jnp.abs(places[:, None] - places[None, :]).astype(jnp.float32)
    penalty = -rate_scale[:, None, None] * jnp.log1p(rate_reach[:, None, None] * distance[None])
    allowed = (places[None, :] <= places[:, None]) & (places[None, :] >= starts[:, None])
    return (penalty, allowed)


def temporal_attend(query_all, key_all, value_all, penalty, allowed):
    frame_count, positions, channels = query_all.shape
    head_count = channels // HEAD_DIM
    query_heads = query_all.reshape(frame_count, positions, head_count, HEAD_DIM)
    key_heads = key_all.reshape(frame_count, positions, head_count, HEAD_DIM)
    value_heads = value_all.reshape(frame_count, positions, head_count, HEAD_DIM)
    scores = (
        jnp.einsum("fphd,gphd->hpfg", query_heads, key_heads) * HEAD_DIM ** (-0.5)
        + penalty[:, None]
    )
    scores = jnp.where(allowed[None, None], scores, -jnp.inf)
    weights = jax.nn.softmax(scores, axis=-1)
    result = jnp.einsum("hpfg,gphd->fphd", weights, value_heads)
    return result.reshape(frame_count, positions, channels)


def ref_attend(query_all, ref_key_all, ref_value_all):
    frame_count, positions, channels = query_all.shape
    head_count = channels // HEAD_DIM
    key_heads = ref_key_all.reshape(ref_key_all.shape[0], head_count, HEAD_DIM)
    value_heads = ref_value_all.reshape(ref_value_all.shape[0], head_count, HEAD_DIM)

    def one_frame(query_frame):
        query_heads = query_frame.reshape(positions, head_count, HEAD_DIM)
        scores = jnp.einsum("shd,thd->hst", query_heads, key_heads) * HEAD_DIM ** (-0.5)
        weights = jax.nn.softmax(scores, axis=-1)
        return jnp.einsum("hst,thd->shd", weights, value_heads).reshape(positions, channels)

    return lax.map(jax.checkpoint(one_frame), query_all)


def causal_mix(extended, taps, frame_count):
    lead = taps.shape[0] - 1
    result = taps[0] * extended[lead : lead + frame_count]
    for offset in range(1, taps.shape[0]):
        result = result + taps[offset] * extended[lead - offset : lead - offset + frame_count]
    return result


def anti_mix(extended, taps, frame_count):
    result = taps[0] * extended[0:frame_count]
    for offset in range(1, taps.shape[0]):
        result = result + taps[offset] * extended[offset : offset + frame_count]
    return result


def tap_products(grad_out, extended, tap_count):
    lead = tap_count - 1
    frame_count = grad_out.shape[0]
    terms = []
    for offset in range(tap_count):
        terms.append(
            jnp.sum(grad_out * extended[lead - offset : lead - offset + frame_count], axis=(0, 1))
        )
    return jnp.stack(terms)


def per_device(
    queries,
    keys,
    values,
    ref_keys,
    ref_values,
    rate_scale,
    rate_reach,
    window_start,
    out_weight,
    conv_taps,
    cotangent,
):
    frame_local, spatial, channels = queries.shape
    width = out_weight.shape[1]
    lead = conv_taps.shape[0] - 1
    penalty, allowed = kerple_bias(rate_scale, rate_reach, window_start)
    query_pos, key_pos, value_pos = (
        lax.all_to_all(queries, "frame", split_axis=1, concat_axis=0, tiled=True),
        lax.all_to_all(keys, "frame", split_axis=1, concat_axis=0, tiled=True),
        lax.all_to_all(values, "frame", split_axis=1, concat_axis=0, tiled=True),
    )

    def temporal_part(query_all, key_all, value_all):
        return temporal_attend(query_all, key_all, value_all, penalty, allowed)

    temporal_out, temporal_pull = jax.vjp(
        temporal_part,
        query_pos.astype(jnp.float32),
        key_pos.astype(jnp.float32),
        value_pos.astype(jnp.float32),
    )
    temporal_back = lax.all_to_all(temporal_out, "frame", split_axis=0, concat_axis=1, tiled=True)
    ref_key_all, ref_value_all = (
        lax.all_gather(ref_keys, "frame", axis=0, tiled=True),
        lax.all_gather(ref_values, "frame", axis=0, tiled=True),
    )
    ref_out, ref_pull = jax.vjp(
        ref_attend,
        queries.astype(jnp.float32),
        ref_key_all.astype(jnp.float32),
        ref_value_all.astype(jnp.float32),
    )
    attended = (temporal_back + ref_out).astype(jnp.bfloat16)
    row_count = frame_local * spatial
    attended_rows = attended.reshape(row_count, channels)
    partial_terms = jnp.dot(attended_rows, out_weight, preferred_element_type=jnp.float32).reshape(
        frame_local, spatial, width
    )
    mixed = lax.psum_scatter(partial_terms, "head", scatter_dimension=2, tiled=True).astype(
        jnp.bfloat16
    )
    earlier = shifted(mixed, "frame", 1)
    past = jnp.concatenate([earlier.astype(jnp.float32), mixed.astype(jnp.float32)], 0)
    block_out = causal_mix(past, conv_taps, frame_local).astype(jnp.bfloat16)
    grad_out = cotangent.astype(jnp.float32)
    later = shifted(cotangent, "frame", -1)
    future = jnp.concatenate([grad_out, later.astype(jnp.float32)], 0)
    grad_mixed = anti_mix(future, conv_taps, frame_local).astype(jnp.bfloat16)
    grad_taps = lax.psum(tap_products(grad_out, past, lead + 1), "frame")
    grad_wide = lax.all_gather(grad_mixed, "head", axis=2, tiled=True).reshape(row_count, width)
    grad_attended = lax.dot_general(
        grad_wide, out_weight, (((1,), (1,)), ((), ())), preferred_element_type=jnp.float32
    ).astype(jnp.bfloat16)
    weight_terms = lax.dot_general(
        attended_rows, grad_wide, (((0,), (0,)), ((), ())), preferred_element_type=jnp.float32
    )
    grad_weight = lax.psum_scatter(
        weight_terms.astype(jnp.bfloat16), "frame", scatter_dimension=1, tiled=True
    ).astype(jnp.float32)
    grad_local = grad_attended.reshape(frame_local, spatial, channels)
    grad_pos = lax.all_to_all(grad_local, "frame", split_axis=1, concat_axis=0, tiled=True)
    temporal_grads = temporal_pull(grad_pos.astype(jnp.float32))
    query_back, key_back, value_back = (
        lax.all_to_all(temporal_grads[0], "frame", split_axis=0, concat_axis=1, tiled=True),
        lax.all_to_all(temporal_grads[1], "frame", split_axis=0, concat_axis=1, tiled=True),
        lax.all_to_all(temporal_grads[2], "frame", split_axis=0, concat_axis=1, tiled=True),
    )
    ref_query_grad, ref_key_grad, ref_value_grad = ref_pull(grad_local.astype(jnp.float32))
    ref_key_share, ref_value_share = (
        lax.psum_scatter(
            ref_key_grad.astype(jnp.bfloat16), "frame", scatter_dimension=0, tiled=True
        ).astype(jnp.float32),
        lax.psum_scatter(
            ref_value_grad.astype(jnp.bfloat16), "frame", scatter_dimension=0, tiled=True
        ).astype(jnp.float32),
    )
    return (
        block_out,
        (query_back + ref_query_grad).astype(jnp.bfloat16),
        key_back.astype(jnp.bfloat16),
        value_back.astype(jnp.bfloat16),
        ref_key_share,
        ref_value_share,
        grad_weight,
        grad_taps,
    )


def solution(mesh):
    placed = (
        P("frame", None, "head"),
        P("frame", None, "head"),
        P("frame", None, "head"),
        P("frame", "head"),
        P("frame", "head"),
        P("head"),
        P("head"),
        P(),
        P("head", None),
        P(None, "head"),
        P("frame", None, "head"),
    )
    return jax.shard_map(
        per_device,
        mesh=mesh,
        in_specs=placed,
        out_specs=(
            P("frame", None, "head"),
            P("frame", None, "head"),
            P("frame", None, "head"),
            P("frame", None, "head"),
            P("frame", "head"),
            P("frame", "head"),
            P("head", "frame"),
            P(None, "head"),
        ),
        check_vma=False,
    )
```

profile of v0, /device:TPU:0, one launch (start us, length us, event | category | flops | bytes accessed | tf_op | source)
XLA Modules:
  0.0 819.9 jit_solution(5690581162147018194)
XLA Ops:
  11.5 5.2 all-to-all-start
  19.4 18.3 %all-to-all-done = bf16[2,512,768]{2,0,1:T(2,128)(2,1)S(1)} async-done(((bf16[2,512,768]{2,0,1:T(2,128)(2,1)}), bf16[2,512,768]{2,0,1:T(2,128)(2,1)S(1)}, u32[]{:S(2)}, u32[]{:S(2)}) %all-to-all-start) | async-done | bytes 1572896 | tf_op jit(solution)/shard_map/all_to_all | solution.py:99
  46.3 16.7 %all-to-all-done.1 = bf16[2,512,768]{2,0,1:T(2,128)(2,1)} async-done(((bf16[2,512,768]{2,0,1:T(2,128)(2,1)}), bf16[2,512,768]{2,0,1:T(2,128)(2,1)}, u32[]{:S(2)}, u32[]{:S(2)}) %all-to-all-start.1) | async-done | bytes 1572896 | tf_op jit(solution)/shard_map/all_to_all | solution.py:100
  68.9 24.8 %all_gather.9 = bf16[512,768]{1,0:T(8,128)(2,1)S(1)} all-gather(bf16[64,768]{1,0:T(8,128)(2,1)S(1)} %copy-done.21), channel_id=1, replica_groups=mesh['frame'=8,'head'=4] {'frame'}, dimensions={0}, use_global_device_ids=true | all-gather | bytes 884736 | tf_op jit(solution)/shard_map/all_gather | solution.py:115
  97.2 9.2 %all_gather.10 = bf16[512,768]{1,0:T(8,128)(2,1)S(1)} all-gather(bf16[64,768]{1,0:T(8,128)(2,1)S(1)} %copy-done.22), channel_id=1, replica_groups=mesh['frame'=8,'head'=4] {'frame'}, dimensions={0}, use_global_device_ids=true | all-gather | bytes 884736 | tf_op jit(solution)/shard_map/all_gather | solution.py:116
  121.9 9.1 %fusion.62 = (f32[6,64,16]{2,1,0:T(8,128)S(1)}, f32[6,64,16,16]{2,3,1,0:T(8,128)}) fusion(f32[6,16,16]{1,2,0:T(8,128)S(1)} %log-plus-one_multiply_fusion, pred[16,16]{0,1:T(8,128)(4,1)S(1)} %fusion.56, bf16[16,64,6,128]{3,2,1,0:T(8,128)(2,1)} %reshape.182, bf16[16,64,6,128]{3,2,1,0:T(8,128)(2,1)} %reshape.181), kind=kOutput, calls=%fused_computation.97 | convolution fusion | flops 25657360 | bytes 3569920 | tf_op jit(solution)/shard_map/jvp()/sub | solution.py:35
  148.8 17.9 %while.29 = (s32[]{:T(128)}, f32[2,512,768]{2,1,0:T(8,128)}, bf16[2,512,768]{1,2,0:T(8,128)(2,1)}, bf16[512,6,128]{2,0,1:T(8,128)(2,1)}, bf16[512,6,128]{0,2,1:T(8,128)(2,1)}, /*index=5*/s32[]{:T(128)}) while((s32[]{:T(128)}, f32[2,512,768]{2,1,0:T(8,128)}, bf16[2,512,768]{1,2,0:T(8,128)(2,1)}, bf16[512,6,128]{2,0,1:T(8,128)(2,1)}, ...), condition=%wide.region_5.6_spmd, body=%wide.region_2.5_spmd.sunk | while | flops 817883136 | bytes 30732872 | solution.py:52
  166.7 18.0 %all-to-all-done.3 = f32[16,64,768]{2,1,0:T(8,128)} async-done(((f32[16,64,768]{2,1,0:T(8,128)}), f32[16,64,768]{2,1,0:T(8,128)}, u32[]{:S(2)}, u32[]{:S(2)}) %all-to-all-start.3) | async-done | bytes 3145760 | tf_op jit(solution)/shard_map/all_to_all | solution.py:113
  189.2 8.0 fusion.16
  199.8 208.7 %reduce-scatter.11.cloned.1.call-done = f32[2,512,768]{2,1,0:T(8,128)} async-done(((f32[2,512,3072]{2,1,0:T(8,128)}), f32[2,512,768]{2,1,0:T(8,128)}) %reduce-scatter.11.cloned.1.call-update) | async-done | bytes 3145744 | tf_op jit(solution)/shard_map/reduce_scatter | solution.py:130
  422.4 131.1 %all-gather.2.cloned.1.call-done = bf16[2,512,3072]{2,1,0:T(8,128)(2,1)} async-done(((bf16[2,512,768]{2,1,0:T(8,128)(2,1)}), bf16[2,512,3072]{2,1,0:T(8,128)(2,1)}) %all-gather.2.cloned.1.call-update) | async-done | bytes 6291472 | tf_op jit(solution)/shard_map/all_gather | solution.py:141
  553.5 8.8 %convolution_convert_fusion = bf16[1024,768]{1,0:T(8,128)(2,1)S(1)} fusion(bf16[1024,3072]{1,0:T(8,128)(2,1)} %bitcast.184, bf16[768,3072]{1,0:T(8,128)(2,1)} %param.23), kind=kOutput, calls=%fused_computation.64 | convolution fusion | flops 4832624640 | bytes 12582912 | tf_op jit(solution)/shard_map/dot_general | solution.py:142
  565.9 57.4 %while.30 = (s32[]{:T(128)}, f32[512,6,128]{2,0,1:T(8,128)}, f32[512,6,128]{0,2,1:T(8,128)}, f32[2,512,768]{2,1,0:T(8,128)}, bf16[2,512,768]{1,2,0:T(8,128)(2,1)...) while((s32[]{:T(128)}, f32[512,6,128]{2,0,1:T(8,128)}, ...), condition=%wide.region_12.13_spmd.clone, body=%wide.region_8.0_spmd.clone.sunk | while | flops 2054160384 | bytes 152002816 | solution.py:52
  582.3 6.0 bitcast_add_fusion.7
  588.3 5.9 bitcast_add_fusion.6
  610.6 6.4 bitcast_add_fusion.7
  616.9 6.4 bitcast_add_fusion.6
  635.6 9.6 %bitcast_convert_fusion = bf16[768,3072]{1,0:T(8,128)(2,1)} fusion(bf16[2,512,768]{2,1,0:T(8,128)(2,1)} %copy-done.18, bf16[2,512,3072]{2,1,0:T(8,128)(2,1)} %all-gather.2.cloned.1.call-done), kind=kOutput, calls=%fused_computation.28 | convolution fusion | flops 4834197504 | bytes 12582912 | tf_op jit(solution)/shard_map/dot_general | solution.py:145
  645.2 6.6 copy.182
  661.8 6.6 fusion.28
  691.3 15.1 %all-to-all-done.6 = bf16[16,64,768]{2,1,0:T(8,128)(2,1)} async-done(((bf16[16,64,768]{2,1,0:T(8,128)(2,1)}), bf16[16,64,768]{2,1,0:T(8,128)(2,1)}, u32[]{:S(2)}, u32[]{:S(2)}) %all-to-all-start.6) | async-done | bytes 1572896 | tf_op jit(solution)/shard_map/all_to_all | solution.py:156
  719.6 5.0 reshape.192
  724.6 7.2 all-to-all-done.7
  735.5 62.7 %psum.7 = f32[3,768]{1,0:T(4,128)} all-reduce(f32[3,768]{1,0:T(4,128)S(1)} %pad_maximum_fusion.2), channel_id=1, replica_groups=mesh['frame'=8,'head'=4] {'frame'}, use_global_device_ids=true, to_apply=%region_19.20 | all-reduce | flops 2304 | bytes 18432 | tf_op jit(solution)/shard_map/psum | solution.py:140
  (209 shorter events, 209.6 us)
Async XLA Ops:
  11.5 26.2 %all-to-all-start = ((bf16[2,512,768]{2,0,1:T(2,128)(2,1)}), bf16[2,512,768]{2,0,1:T(2,128)(2,1)S(1)}, u32[]{:S(2)}, u32[]{:S(2)}) async-start(bf16[2,512,768]{2,0,1:T(2,128)(2,1)} %copy.122), calls=%async_computation | async-start | bytes 3145728 | tf_op jit(solution)/shard_map/all_to_all | solution.py:99
  37.7 25.3 %all-to-all-start.1 = ((bf16[2,512,768]{2,0,1:T(2,128)(2,1)}), bf16[2,512,768]{2,0,1:T(2,128)(2,1)}, u32[]{:S(2)}, u32[]{:S(2)}) async-start(bf16[2,512,768]{2,0,1:T(2,128)(2,1)} %copy.124), calls=%async_computation.1 | async-start | bytes 3145728 | tf_op jit(solution)/shard_map/all_to_all | solution.py:100
  42.0 25.3 %copy-start.11 = (bf16[2,512,768]{2,1,0:T(8,128)(2,1)S(1)}, bf16[2,512,768]{2,1,0:T(8,128)(2,1)}, u32[]{:S(2)}) copy-start(bf16[2,512,768]{2,1,0:T(8,128)(2,1)} %param.15) | copy-start | bytes 4718596
  46.3 22.6 %copy-start.31 = (f32[6]{0:T(128)S(1)}, f32[6]{0:T(128)}, u32[]{:S(2)}) copy-start(f32[6]{0:T(128)} %param.20) | copy-start | bytes 76
  46.3 22.6 %copy-start.21 = (bf16[64,768]{1,0:T(8,128)(2,1)S(1)}, bf16[64,768]{1,0:T(8,128)(2,1)}, u32[]{:S(2)}) copy-start(bf16[64,768]{1,0:T(8,128)(2,1)} %param.18) | copy-start | bytes 294916
  63.0 52.7 %all-to-all-start.2 = ((bf16[2,512,768]{2,0,1:T(2,128)(2,1)}), bf16[2,512,768]{2,0,1:T(2,128)(2,1)}, u32[]{:S(2)}, u32[]{:S(2)}) async-start(bf16[2,512,768]{2,0,1:T(2,128)(2,1)} %copy.128), calls=%async_computation.2 | async-start | bytes 3145728 | tf_op jit(solution)/shard_map/all_to_all | solution.py:101
  67.3 29.8 %copy-start.22 = (bf16[64,768]{1,0:T(8,128)(2,1)S(1)}, bf16[64,768]{1,0:T(8,128)(2,1)}, u32[]{:S(2)}) copy-start(bf16[64,768]{1,0:T(8,128)(2,1)} %param.19) | copy-start | bytes 294916
  68.9 38.6 %copy-start.30 = (s32[16]{0:T(128)S(1)}, s32[16]{0:T(128)}, u32[]{:S(2)}) copy-start(s32[16]{0:T(128)} %param.22) | copy-start | bytes 196
  68.9 38.6 %copy-start.29 = (f32[6]{0:T(128)S(1)}, f32[6]{0:T(128)}, u32[]{:S(2)}) copy-start(f32[6]{0:T(128)} %param.21) | copy-start | bytes 76
  107.6 14.3 %copy-start.27 = (pred[16,16]{0,1:T(8,128)(4,1)}, pred[16,16]{0,1:T(8,128)(4,1)S(1)}, u32[]{:S(2)}) copy-start(pred[16,16]{0,1:T(8,128)(4,1)S(1)} %fusion.56) | copy-start | bytes 772
  121.9 11.5 %copy-start.5 = (bf16[16,64,6,128]{3,2,1,0:T(8,128)(2,1)}, bf16[16,64,6,128]{3,2,1,0:T(8,128)(2,1)S(1)}, u32[]{:S(2)}) copy-start(bf16[16,64,6,128]{3,2,1,0:T(8,128)(2,1)S(1)} %reshape.183) | copy-start | bytes 4718596
  142.4 42.3 %all-to-all-start.3 = ((f32[16,64,768]{2,1,0:T(8,128)}), f32[16,64,768]{2,1,0:T(8,128)}, u32[]{:S(2)}, u32[]{:S(2)}) async-start(f32[16,64,768]{2,1,0:T(8,128)} %reshape.184), calls=%async_computation.3 | async-start | bytes 6291456 | tf_op jit(solution)/shard_map/all_to_all | solution.py:113
  146.8 261.8 %reduce-scatter.11.cloned.1.call-start = ((), (), s32[]{:S(2)}) async-start(), calls=%async_computation.12 | async-start | bytes 15728640 | tf_op jit(solution)/shard_map/reduce_scatter | solution.py:130
  197.2 356.3 %all-gather.2.cloned.1.call-start = ((), (), s32[]{:S(2)}) async-start(), calls=%async_computation.13 | async-start | bytes 7864320 | tf_op jit(solution)/shard_map/all_gather | solution.py:141
  198.6 214.5 %collective-permute-start.1 = (bf16[2,512,768]{2,1,0:T(8,128)(2,1)S(1)}, bf16[2,512,768]{2,1,0:T(8,128)(2,1)S(1)}, u32[]{:S(2)}, u32[]{:S(2)}) collective-permute-start(bf16[2,512,768]{2,1,0:T(8,128)(2,1)S(1)} %copy-done.14), channel_id=1, source_target_pairs={{4,0},{8,4},{12,8},{16,12},{20,16},{24,20},{28,24},{5,1},{9,5},{13... | collective-permute-start | bytes 4718600 | tf_op jit(solution)/shard_map/ppermute | solution.py:12
  410.9 4.8 collective-permute-start
  420.0 378.2 %reduce-scatter.13.cloned.1.call-start = ((), (), s32[]{:S(2)}) async-start(), calls=%async_computation.14 | async-start | bytes 884736
  629.1 26.8 %all-to-all-start.4 = ((bf16[2,512,768]{2,0,1:T(2,128)(2,1)}), bf16[2,512,768]{2,0,1:T(2,128)(2,1)S(1)}, u32[]{:S(2)}, u32[]{:S(2)}) async-start(bf16[2,512,768]{2,0,1:T(2,128)(2,1)} %copy.139), calls=%async_computation.5 | async-start | bytes 3145728 | tf_op jit(solution)/shard_map/all_to_all | solution.py:152
  632.8 167.3 %reduce-scatter.15.cloned.1.call-start = ((), (), s32[]{:S(2)}) async-start(), calls=%async_computation.15 | async-start | bytes 884736
  635.6 175.2 %reduce-scatter.17.cloned.1.call-start = ((), (), s32[]{:S(2)}) async-start(), calls=%async_computation.16 | async-start | bytes 5308416
  677.9 28.5 %all-to-all-start.6 = ((bf16[16,64,768]{2,1,0:T(8,128)(2,1)}), bf16[16,64,768]{2,1,0:T(8,128)(2,1)}, u32[]{:S(2)}, u32[]{:S(2)}) async-start(bf16[16,64,768]{2,1,0:T(8,128)(2,1)} %reshape.193), calls=%async_computation.7 | async-start | bytes 3145728 | tf_op jit(solution)/shard_map/all_to_all | solution.py:156
  686.8 23.9 %copy-start.8 = (f32[6,64,16,16]{2,3,1,0:T(8,128)S(1)}, f32[6,64,16,16]{2,3,1,0:T(8,128)}, u32[]{:S(2)}) copy-start(f32[6,64,16,16]{2,3,1,0:T(8,128)} %get-tuple-element.349) | copy-start | bytes 1179652
  706.4 25.3 %all-to-all-start.7 = ((bf16[16,64,768]{2,1,0:T(8,128)(2,1)}), bf16[16,64,768]{2,1,0:T(8,128)(2,1)}, u32[]{:S(2)}, u32[]{:S(2)}) async-start(bf16[16,64,768]{2,1,0:T(8,128)(2,1)} %reshape.194), calls=%async_computation.8 | async-start | bytes 3145728 | tf_op jit(solution)/shard_map/all_to_all | solution.py:157
  731.8 75.5 %all-to-all-start.5 = ((f32[16,64,768]{2,1,0:T(8,128)}), f32[16,64,768]{2,1,0:T(8,128)S(1)}, u32[]{:S(2)}, u32[]{:S(2)}) async-start(f32[16,64,768]{2,1,0:T(8,128)} %reshape.192), calls=%async_computation.6 | async-start | bytes 6291456 | tf_op jit(solution)/shard_map/all_to_all | solution.py:155
  (32 other events, 169.1 us)
Sparse Core Ops, SparseCore 0:
  197.3 211.2 reduce-scatter.10
  420.1 133.3 all-gather.1
  626.4 35.3 reduce-scatter.12
  665.4 41.6 reduce-scatter.14
  710.4 81.5 reduce-scatter.16
where the time goes:
time: 829 us; the launch traced here: 820 us
  waiting for transfers between devices  422 us (51%)
  local copies, waits for them, and re-layouts  125 us (15%)
  matrix products  106 us (13%)
  blocking collectives  96.7 us (12%)
  starting transfers between devices  37.5 us (5%)
  other arithmetic  18.4 us (2%)
  between operations  14.5 us (2%)
    reduce_scatter x1, waiting for transfers between devices, per_device(): lax.psum_scatter(partial_terms, 'head', scatter_dimension=2, tiled=True)  209 us
    all_gather x1, waiting for transfers between devices, per_device(): lax.all_gather(grad_mixed, 'head', axis=2, tiled=True)  131 us
    psum x1, blocking collectives, per_device(): grad_taps = lax.psum(tap_products(grad_out, past, lead + 1), 'frame')  62.7 us
    unnamed x75, local copies, waits for them, and re-layouts  33.9 us
    dot_general x8, matrix products, one_frame(): jnp.einsum('shd,thd->hst', query_heads, key_heads) * HEAD_DIM ** (-0.5)  28.4 us
    all_gather x1, blocking collectives, per_device(): lax.all_gather(ref_keys, 'frame', axis=0, tiled=True)  24.8 us
    dot_general x6, matrix products, one_frame(): jnp.einsum('hst,thd->shd', weights, value_heads)  24.5 us
    all_to_all x1, waiting for transfers between devices, per_device(): lax.all_to_all(queries, 'frame', split_axis=1, concat_axis=0, tiled=True)  18.3 us
  transfers between devices with their start and end apart: 15, of which 9 were waited for; matrix products, arithmetic and copies ran while one was open for 15% of the time, Pallas kernels for 0%

commit v1 on v0

v1 whole, which is shorter than its diff:
```python
import jax
import jax.numpy as jnp
from jax import lax
from jax.experimental import pallas as pl
from jax.experimental.pallas import tpu as pltpu
from jax.sharding import PartitionSpec as P

HEAD_DIM = 128
SCALE = HEAD_DIM ** (-0.5)
LOG2E = 1.4426950408889634
BLOCK = 16
HIDDEN = -1e30
CHUNKS = 1
BF16 = jnp.bfloat16
F32 = jnp.float32
ANY = pl.BlockSpec(memory_space=pl.ANY)
SMEM = pl.BlockSpec(memory_space=pltpu.SMEM)
LIMIT = pltpu.CompilerParams(vmem_limit_bytes=48 * 2**20)


def dot(a, b):
    return lax.dot_general(a, b, (((1,), (0,)), ((), ())), preferred_element_type=F32)


def dot_nt(a, b):
    return lax.dot_general(a, b, (((1,), (1,)), ((), ())), preferred_element_type=F32)


def dot_tn(a, b):
    return lax.dot_general(a, b, (((0,), (0,)), ((), ())), preferred_element_type=F32)


def run_copies(copies):
    for copy in copies:
        copy.start()
    for copy in copies:
        copy.wait()


def pack(arrays, me, count):
    frames, spatial, channels = arrays[0].shape
    held = spatial // count
    part = held // CHUNKS
    total = len(arrays)

    def kernel(me_ref, *refs):
        sources, pieces, sems = refs[:total], refs[total:-1], refs[-1]
        copies = []
        for chunk in range(CHUNKS):
            for s in range(count):
                start = pl.multiple_of((me_ref[0] ^ s) * held + chunk * part, part)
                for a in range(total):
                    copies.append(
                        pltpu.make_async_copy(
                            sources[a].at[:, pl.ds(start, part), :],
                            pieces[chunk * count + s].at[a],
                            sems.at[len(copies)],
                        )
                    )
        run_copies(copies)

    flat = pl.pallas_call(
        kernel,
        in_specs=[SMEM] + [ANY] * total,
        out_specs=[ANY] * (CHUNKS * count),
        out_shape=[jax.ShapeDtypeStruct((total, frames, part, channels), BF16)] * (CHUNKS * count),
        scratch_shapes=[pltpu.SemaphoreType.DMA((CHUNKS * count * total,))],
        cost_estimate=pl.CostEstimate(
            flops=0, bytes_accessed=4 * total * arrays[0].size, transcendentals=0
        ),
    )(me, *arrays)
    return [flat[c * count : (c + 1) * count] for c in range(CHUNKS)]


def unpack(pieces, me, count):
    total, frames, part, channels = pieces[0][0].shape
    held = part * CHUNKS
    flat = [piece for chunk in pieces for piece in chunk]

    def kernel(me_ref, *refs):
        sources, results, sems = refs[: len(flat)], refs[len(flat) : -1], refs[-1]
        copies = []
        for chunk in range(CHUNKS):
            for s in range(count):
                start = pl.multiple_of((me_ref[0] ^ s) * held + chunk * part, part)
                for a in range(total):
                    copies.append(
                        pltpu.make_async_copy(
                            sources[chunk * count + s].at[a],
                            results[a].at[:, pl.ds(start, part), :],
                            sems.at[len(copies)],
                        )
                    )
        run_copies(copies)

    return pl.pallas_call(
        kernel,
        in_specs=[SMEM] + [ANY] * len(flat),
        out_specs=[ANY] * total,
        out_shape=[jax.ShapeDtypeStruct((frames, held * count, channels), BF16)] * total,
        scratch_shapes=[pltpu.SemaphoreType.DMA((len(flat) * total,))],
        cost_estimate=pl.CostEstimate(
            flops=0, bytes_accessed=4 * len(flat) * flat[0].size, transcendentals=0
        ),
    )(me, *flat)


def swap(value, s):
    count = lax.axis_size("frame")
    return lax.ppermute(value, "frame", [(i, i ^ s) for i in range(count)])


def exchange(pieces):
    return [pieces[0]] + [swap(pieces[s], s) for s in range(1, len(pieces))]


def collect(own, count):
    even = [own] + [swap(own, s) for s in range(2, count, 2)]
    odd = swap(jnp.stack(even), 1)
    return [even[s // 2] if s % 2 == 0 else odd[s // 2] for s in range(count)]


def reduce_pieces(even, odd):
    near = swap(odd.astype(BF16), 1).astype(F32)
    sums = even + near
    total = sums[0]
    for t in range(1, even.shape[0]):
        total = total + swap(sums[t].astype(BF16), 2 * t).astype(F32)
    return total


def temporal_bias(rate_scale, rate_reach, starts, me, count):
    frames = starts.shape[0]
    local = frames // count
    places = ((me ^ jnp.arange(count, dtype=jnp.int32))[:, None] * local + jnp.arange(local)).reshape(frames)
    distance = jnp.abs(places[:, None] - places[None, :]).astype(F32)
    penalty = -rate_scale[:, None, None] * jnp.log1p(rate_reach[:, None, None] * distance[None])
    allowed = (places[:, None] <= places[None, :]) & (places[:, None] >= starts[places][None, :])
    small = jnp.where(allowed[None], penalty * LOG2E, HIDDEN)
    same = jnp.eye(BLOCK, dtype=jnp.bool_)
    wide = jnp.where(same[None, None, :, None, :], small[:, :, None, :, None], HIDDEN)
    return wide.reshape(rate_scale.shape[0], frames * BLOCK, frames * BLOCK)


def weights_of(scores):
    raised = jnp.exp2(scores - jnp.max(scores, axis=0, keepdims=True))
    return raised, 1.0 / jnp.sum(raised, axis=0, keepdims=True)


def block_rows(refs, index, at):
    parts = []
    for ref in refs:
        value = ref[index, :, at, :]
        parts.append(value.reshape(value.shape[0] * value.shape[1], HEAD_DIM))
    return jnp.concatenate(parts, axis=0)


def attend(video, refs, bias):
    count = len(video)
    _, frames, part, channels = video[0].shape
    tokens = refs[0].shape[1]
    heads = channels // HEAD_DIM
    rows = bias.shape[1]

    def kernel(*args):
        video_refs, kv_refs, bias_ref, out_ref = args[:count], args[count : 2 * count], args[-2], args[-1]
        ref_key = jnp.concatenate([r[0] for r in kv_refs], axis=0)
        ref_value_t = jnp.concatenate([r[1] for r in kv_refs], axis=0).T
        for b in range(part // BLOCK):
            at = slice(b * BLOCK, (b + 1) * BLOCK)
            query, key, value = (block_rows(video_refs, a, at) for a in range(3))
            raised, inverse = weights_of(dot_nt(key, query) * (SCALE * LOG2E) + bias_ref[0])
            total = dot(value.T, raised.astype(BF16)) * inverse
            raised, inverse = weights_of(dot_nt(ref_key, query) * (SCALE * LOG2E))
            total = total + dot(ref_value_t, raised.astype(BF16)) * inverse
            out_ref[:, :, at, :] = total.T.astype(BF16).reshape(count, frames, BLOCK, HEAD_DIM)

    all_rows = count * frames * part
    return pl.pallas_call(
        kernel,
        grid=(heads,),
        in_specs=[pl.BlockSpec((3, frames, part, HEAD_DIM), lambda h: (0, 0, 0, h))] * count
        + [pl.BlockSpec((2, tokens, HEAD_DIM), lambda h: (0, 0, h))] * count
        + [pl.BlockSpec((1, rows, rows), lambda h: (h, 0, 0))],
        out_specs=pl.BlockSpec((count, frames, part, HEAD_DIM), lambda h: (0, 0, 0, h)),
        out_shape=jax.ShapeDtypeStruct((count, frames, part, channels), BF16),
        compiler_params=LIMIT,
        cost_estimate=pl.CostEstimate(
            flops=4 * all_rows * channels * (rows + tokens * count),
            bytes_accessed=8 * all_rows * channels,
            transcendentals=all_rows * heads * (rows + tokens * count),
        ),
    )(*video, *refs, bias)


def attend_back(video, refs, bias, grad):
    count = len(video)
    _, frames, part, channels = video[0].shape
    tokens = refs[0].shape[1]
    heads = channels // HEAD_DIM
    rows = bias.shape[1]

    def kernel(*args):
        video_refs, kv_refs, bias_ref, grad_ref = (
            args[:count],
            args[count : 2 * count],
            args[2 * count],
            args[2 * count + 1],
        )
        outs = args[2 * count + 2 : 3 * count + 2]
        out_ref_key, out_ref_value = args[3 * count + 2 :]
        ref_key = jnp.concatenate([r[0] for r in kv_refs], axis=0)
        ref_value = jnp.concatenate([r[1] for r in kv_refs], axis=0)
        ref_key_t = ref_key.T

        def back(scores, value, grad_rows):
            raised, inverse = weights_of(scores)
            weights = raised * inverse
            pulled = dot_nt(value, grad_rows)
            centre = jnp.sum(weights * pulled, axis=0, keepdims=True)
            return weights.astype(BF16), (weights * (pulled - centre)).astype(BF16)

        sum_key = jnp.zeros((tokens * count, HEAD_DIM), F32)
        sum_value = jnp.zeros((tokens * count, HEAD_DIM), F32)
        for b in range(part // BLOCK):
            at = slice(b * BLOCK, (b + 1) * BLOCK)
            query, key, value = (block_rows(video_refs, a, at) for a in range(3))
            grad_rows = grad_ref[:, :, at, :].reshape(rows, HEAD_DIM)
            weights, slopes = back(
                dot_nt(key, query) * (SCALE * LOG2E) + bias_ref[0], value, grad_rows
            )
            grad_value = dot(weights, grad_rows)
            grad_key = dot(slopes, query) * SCALE
            grad_query_t = dot(key.T, slopes)
            weights, slopes = back(dot_nt(ref_key, query) * (SCALE * LOG2E), ref_value, grad_rows)
            sum_value = sum_value + dot(weights, grad_rows)
            sum_key = sum_key + dot(slopes, query)
            grad_query = (grad_query_t + dot(ref_key_t, slopes)).T * SCALE
            for a, result in enumerate((grad_query, grad_key, grad_value)):
                split = result.astype(BF16).reshape(count, frames, BLOCK, HEAD_DIM)
                for s in range(count):
                    outs[s][a, :, at, :] = split[s]
        for s in range(count):
            here = slice(s * tokens, (s + 1) * tokens)
            out_ref_key[s] = sum_key[here] * SCALE
            out_ref_value[s] = sum_value[here]

    all_rows = count * frames * part
    results = pl.pallas_call(
        kernel,
        grid=(heads,),
        in_specs=[pl.BlockSpec((3, frames, part, HEAD_DIM), lambda h: (0, 0, 0, h))] * count
        + [pl.BlockSpec((2, tokens, HEAD_DIM), lambda h: (0, 0, h))] * count
        + [
            pl.BlockSpec((1, rows, rows), lambda h: (h, 0, 0)),
            pl.BlockSpec((count, frames, part, HEAD_DIM), lambda h: (0, 0, 0, h)),
        ],
        out_specs=[pl.BlockSpec((3, frames, part, HEAD_DIM), lambda h: (0, 0, 0, h))] * count
        + [pl.BlockSpec((count, tokens, HEAD_DIM), lambda h: (0, 0, h))] * 2,
        out_shape=[jax.ShapeDtypeStruct((3, frames, part, channels), BF16)] * count
        + [jax.ShapeDtypeStruct((count, tokens, channels), F32)] * 2,
        compiler_params=LIMIT,
        cost_estimate=pl.CostEstimate(
            flops=10 * all_rows * channels * (rows + tokens * count),
            bytes_accessed=16 * all_rows * channels,
            transcendentals=all_rows * heads * (rows + tokens * count),
        ),
    )(*video, *refs, bias, grad)
    return results[:count], results[count], results[count + 1]


def mix_back(pieces, taps, me):
    count = len(pieces)
    _, frames, part, channels = pieces[0].shape
    reach = taps.shape[0]
    full = count * frames

    def kernel(me_ref, taps_ref, *refs):
        out_ref, line = refs[-2], refs[-1]
        for s in range(count):
            for u in range(frames):
                line[(me_ref[0] ^ s) * frames + u] = refs[s][0, u].astype(F32)
        for k in range(reach - 1):
            line[full + k] = jnp.zeros((part, HEAD_DIM), F32)
        for s in range(count):
            for u in range(frames):
                place = (me_ref[0] ^ s) * frames + u
                total = taps_ref[0:1, :] * line[place]
                for k in range(1, reach):
                    total = total + taps_ref[k : k + 1, :] * line[place + k]
                out_ref[s, u] = total.astype(BF16)

    return pl.pallas_call(
        kernel,
        grid=(channels // HEAD_DIM,),
        in_specs=[SMEM, pl.BlockSpec((reach, HEAD_DIM), lambda h: (0, h))]
        + [pl.BlockSpec((1, frames, part, HEAD_DIM), lambda h: (0, 0, 0, h))] * count,
        out_specs=pl.BlockSpec((count, frames, part, HEAD_DIM), lambda h: (0, 0, 0, h)),
        out_shape=jax.ShapeDtypeStruct((count, frames, part, channels), BF16),
        scratch_shapes=[pltpu.VMEM((full + reach - 1, part, HEAD_DIM), F32)],
        compiler_params=LIMIT,
        cost_estimate=pl.CostEstimate(
            flops=6 * full * part * channels, bytes_accessed=4 * full * part * channels, transcendentals=0
        ),
    )(me, taps, *pieces)


def mix(terms, pieces, taps, me):
    count = len(pieces)
    _, frames, part, channels = pieces[0].shape
    reach = taps.shape[0]
    lead = reach - 1
    full = count * frames
    total_terms = len(terms)

    def kernel(me_ref, taps_ref, *refs):
        term_refs, cot_refs = refs[:total_terms], refs[total_terms : total_terms + count]
        outs, taps_out, line = refs[total_terms + count : -2], refs[-2], refs[-1]
        for k in range(lead):
            line[k] = jnp.zeros((part, HEAD_DIM), F32)
        for s in range(count):
            for u in range(frames):
                value = term_refs[0][s, u].astype(F32)
                for term in term_refs[1:]:
                    value = value + term[s, u].astype(F32)
                line[(me_ref[0] ^ s) * frames + u + lead] = value.astype(BF16).astype(F32)
        sums = [jnp.zeros((part, HEAD_DIM), F32) for _ in range(reach)]
        for s in range(count):
            for u in range(frames):
                place = (me_ref[0] ^ s) * frames + u + lead
                cot = cot_refs[s][0, u].astype(F32)
                total = jnp.zeros((part, HEAD_DIM), F32)
                for k in range(reach):
                    past = line[place - k]
                    total = total + taps_ref[k : k + 1, :] * past
                    sums[k] = sums[k] + cot * past
                outs[s][0, u] = total.astype(BF16)
        for k in range(reach):
            taps_out[k : k + 1, :] = jnp.sum(sums[k], axis=0, keepdims=True)

    results = pl.pallas_call(
        kernel,
        grid=(channels // HEAD_DIM,),
        in_specs=[SMEM, pl.BlockSpec((reach, HEAD_DIM), lambda h: (0, h))]
        + [pl.BlockSpec((count, frames, part, HEAD_DIM), lambda h: (0, 0, 0, h))] * total_terms
        + [pl.BlockSpec((1, frames, part, HEAD_DIM), lambda h: (0, 0, 0, h))] * count,
        out_specs=[pl.BlockSpec((1, frames, part, HEAD_DIM), lambda h: (0, 0, 0, h))] * count
        + [pl.BlockSpec((reach, HEAD_DIM), lambda h: (0, h))],
        out_shape=[jax.ShapeDtypeStruct((1, frames, part, channels), BF16)] * count
        + [jax.ShapeDtypeStruct((reach, channels), F32)],
        scratch_shapes=[pltpu.VMEM((full + lead, part, HEAD_DIM), F32)],
        compiler_params=LIMIT,
        cost_estimate=pl.CostEstimate(
            flops=12 * full * part * channels, bytes_accessed=10 * full * part * channels, transcendentals=0
        ),
    )(me, taps, *terms, *pieces)
    return results[:count], results[count]


def per_device(
    queries,
    keys,
    values,
    ref_keys,
    ref_values,
    rate_scale,
    rate_reach,
    window_start,
    out_weight,
    conv_taps,
    cotangent,
):
    frames, spatial, channels = queries.shape
    width = out_weight.shape[1]
    count, depth = lax.axis_size("frame"), lax.axis_size("head")
    place, level = lax.axis_index("frame"), lax.axis_index("head")
    me = place.reshape(1).astype(jnp.int32)
    part = spatial // count // CHUNKS
    rows = count * frames * part
    shape = (count, frames, part, channels)

    def weight_block(j):
        return lax.dynamic_slice_in_dim(out_weight, jnp.clip(j, 0, depth - 1) * channels, channels, 1)

    cot = [exchange(chunk) for chunk in pack([cotangent], me, count)]
    video = [exchange(chunk) for chunk in pack([queries, keys, values], me, count)]
    refs = collect(jnp.stack([ref_keys, ref_values]), count)
    bias = temporal_bias(rate_scale, rate_reach, window_start, place, count)

    blocks = []
    for c in range(CHUNKS):
        own = mix_back(cot[c], conv_taps, me).reshape(rows, channels)
        arrived = [(own, level)]
        up = down = own
        for s in range(1, depth):
            up = lax.ppermute(up, "head", [(i, i + 1) for i in range(s - 1, depth - 1)])
            down = lax.ppermute(down, "head", [(i, i - 1) for i in range(1, depth - s + 1)])
            if 2 * s < depth:
                arrived += [(up, level - s), (down, level + s)]
            else:
                arrived.append((jnp.where(level >= s, up, down), jnp.where(level >= s, level - s, level + s)))
        blocks.append(arrived)

    attended = [attend(video[c], refs, bias).reshape(rows, channels) for c in range(CHUNKS)]

    out_pieces, taps_sum = [], 0.0
    for c in range(CHUNKS):
        shares = dot(attended[c], out_weight).astype(BF16)

        def share(j):
            return lax.dynamic_slice_in_dim(shares, jnp.clip(j, 0, depth - 1) * channels, channels, 1)

        up = down = None
        for s in range(1, depth):
            far = depth - s
            send_up, send_down = share(level + far), share(level - far)
            if s > 1:
                send_up = (send_up.astype(F32) + up.astype(F32)).astype(BF16)
                send_down = (send_down.astype(F32) + down.astype(F32)).astype(BF16)
            up = lax.ppermute(send_up, "head", [(i, i + 1) for i in range(depth - far)])
            down = lax.ppermute(send_down, "head", [(i, i - 1) for i in range(far, depth)])
        terms = [t.reshape(shape) for t in (share(level), up, down)]
        pieces, taps_part = mix(terms, cot[c], conv_taps, me)
        out_pieces.append(exchange(pieces))
        taps_sum = taps_sum + taps_part

    slots = jnp.zeros((3 * depth - 2, channels, channels), F32)
    for step in range(len(blocks[0])):
        term = sum(dot_tn(attended[c], blocks[c][step][0]) for c in range(CHUNKS))
        slots = lax.dynamic_update_slice_in_dim(slots, term[None], blocks[0][step][1] + depth - 1, 0)
    columns = width // count
    per_block = channels // columns

    def weight_piece(s):
        target = place ^ s
        return lax.dynamic_slice(
            slots,
            (depth - 1 + target // per_block, 0, (target % per_block) * columns),
            (1, channels, columns),
        )[0]

    grad_weight = reduce_pieces(
        jnp.stack([weight_piece(s) for s in range(0, count, 2)]),
        jnp.stack([weight_piece(s) for s in range(1, count, 2)]),
    )

    grad_pieces, ref_key_sum, ref_value_sum = [], 0.0, 0.0
    for c in range(CHUNKS):
        total = sum(dot_nt(block, weight_block(j)) for block, j in blocks[c])
        pieces, ref_key_part, ref_value_part = attend_back(
            video[c], refs, bias, total.astype(BF16).reshape(shape)
        )
        grad_pieces.append(exchange(pieces))
        ref_key_sum = ref_key_sum + ref_key_part
        ref_value_sum = ref_value_sum + ref_value_part

    ref_sum = jnp.stack([ref_key_sum, ref_value_sum], axis=1)
    ref_grads = reduce_pieces(ref_sum[0::2], ref_sum[1::2])

    step = 1
    while step < count:
        taps_sum = taps_sum + swap(taps_sum, step)
        step *= 2

    (block_out,) = unpack(out_pieces, me, count)
    grad_queries, grad_keys, grad_values = unpack(grad_pieces, me, count)
    return (
        block_out,
        grad_queries,
        grad_keys,
        grad_values,
        ref_grads[0],
        ref_grads[1],
        grad_weight,
        taps_sum,
    )


def solution(mesh):
    video = P("frame", None, "head")
    tokens = P("frame", "head")
    return jax.shard_map(
        per_device,
        mesh=mesh,
        in_specs=(
            video,
            video,
            video,
            tokens,
            tokens,
            P("head"),
            P("head"),
            P(),
            P("head", None),
            P(None, "head"),
            video,
        ),
        out_specs=(video, video, video, video, tokens, tokens, P("head", "frame"), P(None, "head")),
        check_vma=False,
    )
```

time: 829 us -> 791 us (0.954)
  Pallas kernels: 0 us -> 437 us
  waiting for transfers between devices: 422 us -> 105 us
  blocking collectives: 96.7 us -> 0 us
  local copies, waits for them, and re-layouts: 125 us -> 47.3 us
  starting transfers between devices: 37.5 us -> 112 us
  matrix products: 106 us -> 44.7 us
  other arithmetic: 18.4 us -> 32.3 us
  between operations: 14.5 us -> 2.31 us
    pallas_call x0 -> x8, Pallas kernels: none -> 437 us  [the longest x2 193 us: unpack(): pl.pallas_call(kernel, in_specs=[SMEM] + [ANY] * len(flat), out_specs=[AN...]
    reduce_scatter x1 -> x0, waiting for transfers between devices: 209 us -> none  [per_device(): lax.psum_scatter(partial_terms, 'head', scatter_dimension=2, tiled=True)]
    all_gather x1 -> x0, waiting for transfers between devices: 131 us -> none  [per_device(): lax.all_gather(grad_mixed, 'head', axis=2, tiled=True)]
    ppermute x2 -> x55, starting transfers between devices: 3.17 us -> 112 us  [the longest x3 53.1 us: per_device(): up = lax.ppermute(send_up, 'head', [(i, i + 1) for i in range(depth - far)])]
    ppermute x2 -> x55, waiting for transfers between devices: 2.38 us -> 105 us  [the longest x43 93.8 us: swap(): return lax.ppermute(value, 'frame', [(i, i ^ s) for i in range(count)])]
    all_to_all x8 -> x0, waiting for transfers between devices: 79.3 us -> none  [the longest x1 18.3 us: per_device(): lax.all_to_all(queries, 'frame', split_axis=1, concat_axis=0, tiled=True)]
    psum x1 -> x0, blocking collectives: 62.7 us -> none  [per_device(): grad_taps = lax.psum(tap_products(grad_out, past, lead + 1), 'frame')]
    dot_general x22 -> x11, matrix products: 97.1 us -> 44.7 us  [the longest x5 20.2 us: dot_tn(): lax.dot_general(a, b, (((0,), (0,)), ((), ())), preferred_element_type=F32)]
  transfers between devices with their start and end apart: 15 -> 55, of which waited for: 9 -> 18; matrix products, arithmetic and copies ran while one was open for 15% -> 14% of each run, Pallas kernels for 0% -> 56%
where the time goes in v1:
time: 791 us; the launch traced here: 781 us
  Pallas kernels  437 us (55%)
  starting transfers between devices  112 us (14%)
  waiting for transfers between devices  105 us (13%)
  local copies, waits for them, and re-layouts  47.3 us (6%)
  matrix products  44.7 us (6%)
  other arithmetic  32.3 us (4%)
    pallas_call x2, Pallas kernels, unpack(): pl.pallas_call(kernel, in_specs=[SMEM] + [ANY] * len(flat), out_specs=[AN...  193 us
    pallas_call x2, Pallas kernels, pack(): pl.pallas_call(kernel, in_specs=[SMEM] + [ANY] * total, out_specs=[ANY] *...  193 us
    ppermute x43, waiting for transfers between devices, swap(): return lax.ppermute(value, 'frame', [(i, i ^ s) for i in range(count)])  93.8 us
    ppermute x3, starting transfers between devices, per_device(): up = lax.ppermute(send_up, 'head', [(i, i + 1) for i in range(depth - far)])  53.1 us
    ppermute x43, starting transfers between devices, swap(): return lax.ppermute(value, 'frame', [(i, i ^ s) for i in range(count)])  42.4 us
    pallas_call x1, Pallas kernels, attend_back(): pl.pallas_call(kernel, grid=(heads,), in_specs=[pl.BlockSpec((3, frames,...  27.6 us
    dot_general x5, matrix products, dot_tn(): lax.dot_general(a, b, (((0,), (0,)), ((), ())), preferred_element_type=F32)  20.2 us
    dot_general x5, matrix products, dot_nt(): lax.dot_general(a, b, (((1,), (1,)), ((), ())), preferred_element_type=F32)  17.8 us
  transfers between devices with their start and end apart: 55, of which 18 were waited for; matrix products, arithmetic and copies ran while one was open for 14% of the time, Pallas kernels for 56%

profile of v1, /device:TPU:0, one launch (start us, length us, event | category | flops | bytes accessed | tf_op | source)
XLA Modules:
  0.0 780.9 jit_solution(5493193464100307654)
XLA Ops:
  6.2 144.3 %shard_map.170 = (bf16[3,2,64,768]{3,2,1,0:T(8,128)(2,1)}, bf16[3,2,64,768]{3,2,1,0:T(8,128)(2,1)}, bf16[3,2,64,768]{3,2,1,0:T(8,128)(2,1)}, bf16[3,2,64,768]{3,...) custom-call(s32[1]{0:T(128)} %bitcast.me_ref, ...), custom_call_target="tpu_custom_call" | custom-call | bytes 9437184 | tf_op jit(solution)/shard_map/pallas_call | solution.py:62
  152.8 48.8 %shard_map.172 = (bf16[1,2,64,768]{3,2,1,0:T(8,128)(2,1)}, bf16[1,2,64,768]{3,2,1,0:T(8,128)(2,1)}, bf16[1,2,64,768]{3,2,1,0:T(8,128)(2,1)}, bf16[1,2,64,768]{3,...) custom-call(s32[1]{0:T(128)} %bitcast.me_ref, ...), custom_call_target="tpu_custom_call" | custom-call | bytes 3145728 | tf_op jit(solution)/shard_map/pallas_call | solution.py:62
  217.2 6.6 collective-permute-done.21.refs_8_.refs_5_
  226.7 4.7 collective-permute-done.23.refs_10_.refs_7_
  235.9 5.4 broadcast_in_dim.71
  241.3 9.7 %broadcast_in_dim.72 = f32[6,256,256]{2,1,0:T(8,128)} reshape(f32[6,16,16,16,16]{4,3,2,1,0:T(8,128)} %broadcast_in_dim.71) | data formatting | bytes 3145728 | tf_op jit(solution)/shard_map/jit(_where)/broadcast_in_dim | solution.py:141
  258.2 4.9 collective-permute-start.31
  263.1 10.2 %collective-permute-done.3.args_4_ = bf16[3,2,64,768]{3,2,1,0:T(8,128)(2,1)} collective-permute-done((bf16[3,2,64,768]{3,2,1,0:T(8,128)(2,1)}, bf16[3,2,64,768]{3,2,1,0:T(8,128)(2,1)}, u32[]{:S(2)}, u32[]{:S(2)}) %collective-permute-start.3) | collective-permute-done | bytes 589856 | tf_op jit(solution)/shard_map/ppermute | solution.py:110
  274.5 10.9 %collective-permute-done.4.args_5_ = bf16[3,2,64,768]{3,2,1,0:T(8,128)(2,1)} collective-permute-done((bf16[3,2,64,768]{3,2,1,0:T(8,128)(2,1)}, bf16[3,2,64,768]{3,2,1,0:T(8,128)(2,1)}, u32[]{:S(2)}, u32[]{:S(2)}) %collective-permute-start.4) | collective-permute-done | bytes 589856 | tf_op jit(solution)/shard_map/ppermute | solution.py:110
  285.6 17.0 %shard_map.171 = bf16[8,2,64,768]{3,2,1,0:T(8,128)(2,1)} custom-call(bf16[3,2,64,768]{3,2,1,0:T(8,128)(2,1)S(1)} %copy-done.34, bf16[3,2,64,768]{3,2,1,0:T(8,128)(2,1)S(1)} %copy-done.36, bf16[3,2,64,768]{3,2,1,0:T(8,128)(2,1)S(1)} %copy-done.38, bf16[3,2,64,768]{3,2,1,0:T(8,128)(2,1)} %collective-permute-done.2.args_3_, ...), custom_call_target="tpu_custom_call" | custom-call | flops 2415919104 | bytes 6291456 | tf_op jit(solution)/shard_map/pallas_call | solution.py:179
  302.7 6.7 convolution_convert_fusion
  319.8 4.6 collective-permute-start.11
  332.4 10.0 %broadcast_in_dim.74 = f32[10,768,768]{2,1,0:T(8,128)} broadcast(f32[]{:T(128)} %constant.164.clone.1), dimensions={} | broadcast | bytes 23592964 | tf_op jit(solution)/shard_map/broadcast_in_dim | solution.py:427
  359.6 5.2 collective-permute-done.34
  373.1 43.9 %collective-permute-start.12 = (bf16[1024,768]{1,0:T(8,128)(2,1)S(1)}, bf16[1024,768]{1,0:T(8,128)(2,1)S(1)}, u32[]{:S(2)}, u32[]{:S(2)}) collective-permute-start(bf16[1024,768]{1,0:T(8,128)(2,1)S(1)} %get-tuple-element.97), channel_id=1, source_target_pairs={{0,1},{1,2},{4,5},{5,6},{8,9},{9,10},{12,13},{13,14},{16,17},{17,1... | collective-permute-start | bytes 4718600 | tf_op jit(solution)/shard_map/ppermute | solution.py:420
  432.8 5.7 collective-permute-done.12
  449.2 27.6 %shard_map.176 = (bf16[3,2,64,768]{3,2,1,0:T(8,128)(2,1)S(1)}, bf16[3,2,64,768]{3,2,1,0:T(8,128)(2,1)S(1)}, bf16[3,2,64,768]{3,2,1,0:T(8,128)(2,1)S(1)}, bf16[3,...) custom-call(bf16[3,2,64,768]{3,2,1,0:T(8,128)(2,1)} %get-tuple-eleme, ...), custom_call_target="tpu_custom_call" | custom-call | flops 6039797760 | bytes 12582912 | tf_op jit(solution)/shard_map/pallas_call | solution.py:249
  483.9 5.2 shard_map.173
  504.8 5.2 collective-permute-done.38.refs_2_
  511.5 10.4 %collective-permute-done.39.refs_3_ = bf16[3,2,64,768]{3,2,1,0:T(8,128)(2,1)S(1)} collective-permute-done((bf16[3,2,64,768]{3,2,1,0:T(8,128)(2,1)}, bf16[3,2,64,768]{3,2,1,0:T(8,128)(2,1)S(1)}, u32[]{:S(2)}, u32[]{:S(2)}) %collective-permute-start.39) | collective-permute-done | bytes 589856 | tf_op jit(solution)/shard_map/ppermute | solution.py:110
  526.0 22.2 %collective-permute-done.53 = f32[3,768]{1,0:T(4,128)S(1)} collective-permute-done((f32[3,768]{1,0:T(4,128)S(1)}, f32[3,768]{1,0:T(4,128)S(1)}, u32[]{:S(2)}, u32[]{:S(2)}) %collective-permute-start.53) | collective-permute-done | bytes 9248 | tf_op jit(solution)/shard_map/ppermute | solution.py:110
  565.1 144.3 %shard_map.177 = (bf16[2,512,768]{2,1,0:T(8,128)(2,1)}, bf16[2,512,768]{2,1,0:T(8,128)(2,1)}, bf16[2,512,768]{2,1,0:T(8,128)(2,1)}) custom-call(s32[1]{0:T(128)} %bitcast.me_ref, bf16[3,2,64,768]{3,2,1,0:T(8,128)(2,1)} %copy-done.39, bf16[3,2,64,768]{3,2,1,0:T(8,128)(2,1)} %copy-done.67, bf16[3,2,64,768]{3,2,1,0:T(8,128)(2,1)} %copy-done.68, ...), custom_call_target="tpu_custom_call" | custom-call | bytes 9437184 | tf_op jit(solution)/shard_map/pallas_call | solution.py:96
  711.0 8.2 %collective-permute-done.27.refs_4_ = bf16[1,2,64,768]{3,2,1,0:T(8,128)(2,1)S(1)} collective-permute-done((bf16[1,2,64,768]{3,2,1,0:T(8,128)(2,1)S(1)}, bf16[1,2,64,768]{3,2,1,0:T(8,128)(2,1)S(1)}, u32[]{:S(2)}, u32[]{:S(2)}) %collective-permute-start.27) | collective-permute-done | bytes 196640 | tf_op jit(solution)/shard_map/ppermute | solution.py:110
  728.8 48.8 %shard_map.174 = bf16[2,512,768]{2,1,0:T(8,128)(2,1)} custom-call(s32[1]{0:T(128)} %bitcast.me_ref, bf16[1,2,64,768]{3,2,1,0:T(8,128)(2,1)} %copy-done.40, bf16[1,2,64,768]{3,2,1,0:T(8,128)(2,1)} %copy-done.80, bf16[1,2,64,768]{3,2,1,0:T(8,128)(2,1)} %collective-permute-done.25.refs_2_, bf16[1,2,64,768]{3,2,1,0:T(8,128)(2,1)} %collective-permute-done.26.refs_3_, ...), custom_call_target="tpu_custom_call" | custom-call | bytes 3145728 | tf_op jit(solution)/shard_map/pallas_call | solution.py:96
  (344 shorter events, 168.0 us)
Async XLA Ops:
  1.6 200.1 %collective-permute-start.9 = (bf16[2,64,768]{2,1,0:T(8,128)(2,1)S(1)}, bf16[2,64,768]{2,1,0:T(8,128)(2,1)S(1)}, u32[]{:S(2)}, u32[]{:S(2)}) collective-permute-start(bf16[2,64,768]{2,1,0:T(8,128)(2,1)S(1)} %get-tuple-element.114.args_8_), channel_id=1, source_target_pairs={{0,24},{4,28},{8,16},{12,20},{16,8},{20,12},{24,0},{28,4},{1,25},{... | collective-permute-start | bytes 589832 | tf_op jit(solution)/shard_map/ppermute | solution.py:110
  5.6 196.4 %collective-permute-start.8 = (bf16[2,64,768]{2,1,0:T(8,128)(2,1)S(1)}, bf16[2,64,768]{2,1,0:T(8,128)(2,1)S(1)}, u32[]{:S(2)}, u32[]{:S(2)}) collective-permute-start(bf16[2,64,768]{2,1,0:T(8,128)(2,1)S(1)} %get-tuple-element.114.args_8_), channel_id=1, source_target_pairs={{0,16},{4,20},{8,24},{12,28},{16,0},{20,4},{24,8},{28,12},{1,17},{... | collective-permute-start | bytes 589832 | tf_op jit(solution)/shard_map/ppermute | solution.py:110
  6.1 196.1 %collective-permute-start.7 = (bf16[2,64,768]{2,1,0:T(8,128)(2,1)S(1)}, bf16[2,64,768]{2,1,0:T(8,128)(2,1)S(1)}, u32[]{:S(2)}, u32[]{:S(2)}) collective-permute-start(bf16[2,64,768]{2,1,0:T(8,128)(2,1)S(1)} %get-tuple-element.114.args_8_), channel_id=1, source_target_pairs={{0,8},{4,12},{8,0},{12,4},{16,24},{20,28},{24,16},{28,20},{1,9},{5... | collective-permute-start | bytes 589832 | tf_op jit(solution)/shard_map/ppermute | solution.py:110
  150.5 82.5 %collective-permute-start = (bf16[3,2,64,768]{3,2,1,0:T(8,128)(2,1)}, bf16[3,2,64,768]{3,2,1,0:T(8,128)(2,1)S(1)}, u32[]{:S(2)}, u32[]{:S(2)}) collective-permute-start(bf16[3,2,64,768]{3,2,1,0:T(8,128)(2,1)} %get-tuple-element.47), channel_id=1, source_target_pairs={{0,4},{4,0},{8,12},{12,8},{16,20},{20,16},{24,28},{28,24},{1,5},{5... | collective-permute-start | bytes 1769480 | tf_op jit(solution)/shard_map/ppermute | solution.py:110
  150.6 83.0 %collective-permute-start.1 = (bf16[3,2,64,768]{3,2,1,0:T(8,128)(2,1)}, bf16[3,2,64,768]{3,2,1,0:T(8,128)(2,1)S(1)}, u32[]{:S(2)}, u32[]{:S(2)}) collective-permute-start(bf16[3,2,64,768]{3,2,1,0:T(8,128)(2,1)} %get-tuple-element.48), channel_id=1, source_target_pairs={{0,8},{4,12},{8,0},{12,4},{16,24},{20,28},{24,16},{28,20},{1,9},{5... | collective-permute-start | bytes 1769480 | tf_op jit(solution)/shard_map/ppermute | solution.py:110
  233.0 52.5 %collective-permute-start.4 = (bf16[3,2,64,768]{3,2,1,0:T(8,128)(2,1)}, bf16[3,2,64,768]{3,2,1,0:T(8,128)(2,1)}, u32[]{:S(2)}, u32[]{:S(2)}) collective-permute-start(bf16[3,2,64,768]{3,2,1,0:T(8,128)(2,1)} %get-tuple-element.51), channel_id=1, source_target_pairs={{0,20},{4,16},{8,28},{12,24},{16,4},{20,0},{24,12},{28,8},{1,21},{... | collective-permute-start | bytes 1769480 | tf_op jit(solution)/shard_map/ppermute | solution.py:110
  233.6 51.9 %collective-permute-start.5 = (bf16[3,2,64,768]{3,2,1,0:T(8,128)(2,1)}, bf16[3,2,64,768]{3,2,1,0:T(8,128)(2,1)}, u32[]{:S(2)}, u32[]{:S(2)}) collective-permute-start(bf16[3,2,64,768]{3,2,1,0:T(8,128)(2,1)} %get-tuple-element.52), channel_id=1, source_target_pairs={{0,24},{4,28},{8,16},{12,20},{16,8},{20,12},{24,0},{28,4},{1,25},{... | collective-permute-start | bytes 1769480 | tf_op jit(solution)/shard_map/ppermute | solution.py:110
  235.1 50.4 %collective-permute-start.6 = (bf16[3,2,64,768]{3,2,1,0:T(8,128)(2,1)}, bf16[3,2,64,768]{3,2,1,0:T(8,128)(2,1)}, u32[]{:S(2)}, u32[]{:S(2)}) collective-permute-start(bf16[3,2,64,768]{3,2,1,0:T(8,128)(2,1)} %get-tuple-element.53), channel_id=1, source_target_pairs={{0,28},{4,24},{8,20},{12,16},{16,12},{20,8},{24,4},{28,0},{1,29},{... | collective-permute-start | bytes 1769480 | tf_op jit(solution)/shard_map/ppermute | solution.py:110
  258.2 66.2 %collective-permute-start.31 = (bf16[1024,768]{1,0:T(8,128)(2,1)S(1)}, bf16[1024,768]{1,0:T(8,128)(2,1)}, u32[]{:S(2)}, u32[]{:S(2)}) collective-permute-start(bf16[1024,768]{1,0:T(8,128)(2,1)S(1)} %bitcast.96), channel_id=1, source_target_pairs={{0,1},{1,2},{2,3},{4,5},{5,6},{6,7},{8,9},{9,10},{10,11},{12,13},{... | collective-permute-start | bytes 4718600 | tf_op jit(solution)/shard_map/ppermute | solution.py:396
  273.3 53.0 %collective-permute-start.32 = (bf16[1024,768]{1,0:T(8,128)(2,1)S(1)}, bf16[1024,768]{1,0:T(8,128)(2,1)}, u32[]{:S(2)}, u32[]{:S(2)}) collective-permute-start(bf16[1024,768]{1,0:T(8,128)(2,1)S(1)} %bitcast.97), channel_id=1, source_target_pairs={{1,0},{2,1},{3,2},{5,4},{6,5},{7,6},{9,8},{10,9},{11,10},{13,12},{... | collective-permute-start | bytes 4718600 | tf_op jit(solution)/shard_map/ppermute | solution.py:397
  319.8 49.2 %collective-permute-start.11 = (bf16[1024,768]{1,0:T(8,128)(2,1)}, bf16[1024,768]{1,0:T(8,128)(2,1)}, u32[]{:S(2)}, u32[]{:S(2)}) collective-permute-start(bf16[1024,768]{1,0:T(8,128)(2,1)} %get-tuple-element.99), channel_id=1, source_target_pairs={{0,1},{4,5},{8,9},{12,13},{16,17},{20,21},{24,25},{28,29}} | collective-permute-start | bytes 4718600 | tf_op jit(solution)/shard_map/ppermute | solution.py:420
  358.8 66.7 %collective-permute-start.35 = (bf16[1024,768]{1,0:T(8,128)(2,1)}, bf16[1024,768]{1,0:T(8,128)(2,1)S(1)}, u32[]{:S(2)}, u32[]{:S(2)}) collective-permute-start(bf16[1024,768]{1,0:T(8,128)(2,1)} %collective-permute-done.33), channel_id=1, source_target_pairs={{2,3},{6,7},{10,11},{14,15},{18,19},{22,23},{26,27},{30,31}} | collective-permute-start | bytes 4718600 | tf_op jit(solution)/shard_map/ppermute | solution.py:396
  364.8 60.7 %collective-permute-start.36 = (bf16[1024,768]{1,0:T(8,128)(2,1)}, bf16[1024,768]{1,0:T(8,128)(2,1)S(1)}, u32[]{:S(2)}, u32[]{:S(2)}) collective-permute-start(bf16[1024,768]{1,0:T(8,128)(2,1)} %collective-permute-done.34), channel_id=1, source_target_pairs={{1,0},{5,4},{9,8},{13,12},{17,16},{21,20},{25,24},{29,28}} | collective-permute-start | bytes 4718600 | tf_op jit(solution)/shard_map/ppermute | solution.py:397
  373.1 65.4 %collective-permute-start.12 = (bf16[1024,768]{1,0:T(8,128)(2,1)S(1)}, bf16[1024,768]{1,0:T(8,128)(2,1)S(1)}, u32[]{:S(2)}, u32[]{:S(2)}) collective-permute-start(bf16[1024,768]{1,0:T(8,128)(2,1)S(1)} %get-tuple-element.97), channel_id=1, source_target_pairs={{0,1},{1,2},{4,5},{5,6},{8,9},{9,10},{12,13},{13,14},{16,17},{17,1... | collective-permute-start | bytes 4718600 | tf_op jit(solution)/shard_map/ppermute | solution.py:420
  424.2 58.5 %collective-permute-start.16 = (bf16[1024,768]{1,0:T(8,128)(2,1)}, bf16[1024,768]{1,0:T(8,128)(2,1)}, u32[]{:S(2)}, u32[]{:S(2)}) collective-permute-start(bf16[1024,768]{1,0:T(8,128)(2,1)} %get-tuple-element.96), channel_id=1, source_target_pairs={{1,0},{2,1},{3,2},{5,4},{6,5},{7,6},{9,8},{10,9},{11,10},{13,12},{... | collective-permute-start | bytes 4718600 | tf_op jit(solution)/shard_map/ppermute | solution.py:421
  432.8 92.7 %collective-permute-start.48 = (bf16[4,768,384]{2,1,0:T(8,128)(2,1)}, bf16[4,768,384]{2,1,0:T(8,128)(2,1)}, u32[]{:S(2)}, u32[]{:S(2)}) collective-permute-start(bf16[4,768,384]{2,1,0:T(8,128)(2,1)} %pad_maximum_fusion.1), channel_id=1, source_target_pairs={{0,4},{4,0},{8,12},{12,8},{16,20},{20,16},{24,28},{28,24},{1,5},{5... | collective-permute-start | bytes 7077896 | tf_op jit(solution)/shard_map/ppermute | solution.py:110
  440.3 42.5 %collective-permute-start.13 = (bf16[1024,768]{1,0:T(8,128)(2,1)}, bf16[1024,768]{1,0:T(8,128)(2,1)S(1)}, u32[]{:S(2)}, u32[]{:S(2)}) collective-permute-start(bf16[1024,768]{1,0:T(8,128)(2,1)} %add_convert_fusion.3), channel_id=1, source_target_pairs={{0,1},{1,2},{2,3},{4,5},{5,6},{6,7},{8,9},{9,10},{10,11},{12,13},{... | collective-permute-start | bytes 4718600 | tf_op jit(solution)/shard_map/ppermute | solution.py:420
  504.7 48.9 %collective-permute-start.41 = (bf16[3,2,64,768]{3,2,1,0:T(8,128)(2,1)S(1)}, bf16[3,2,64,768]{3,2,1,0:T(8,128)(2,1)S(1)}, u32[]{:S(2)}, u32[]{:S(2)}) collective-permute-start(bf16[3,2,64,768]{3,2,1,0:T(8,128)(2,1)S(1)} %copy-done.45), channel_id=1, source_target_pairs={{0,20},{4,16},{8,28},{12,24},{16,4},{20,0},{24,12},{28,8},{1,21},{... | collective-permute-start | bytes 1769480 | tf_op jit(solution)/shard_map/ppermute | solution.py:110
  510.0 44.2 %collective-permute-start.42 = (bf16[3,2,64,768]{3,2,1,0:T(8,128)(2,1)S(1)}, bf16[3,2,64,768]{3,2,1,0:T(8,128)(2,1)S(1)}, u32[]{:S(2)}, u32[]{:S(2)}) collective-permute-start(bf16[3,2,64,768]{3,2,1,0:T(8,128)(2,1)S(1)} %copy-done.43), channel_id=1, source_target_pairs={{0,24},{4,28},{8,16},{12,20},{16,8},{20,12},{24,0},{28,4},{1,25},{... | collective-permute-start | bytes 1769480 | tf_op jit(solution)/shard_map/ppermute | solution.py:110
  554.3 155.0 %collective-permute-start.25 = (bf16[1,2,64,768]{3,2,1,0:T(8,128)(2,1)S(1)}, bf16[1,2,64,768]{3,2,1,0:T(8,128)(2,1)}, u32[]{:S(2)}, u32[]{:S(2)}) collective-permute-start(bf16[1,2,64,768]{3,2,1,0:T(8,128)(2,1)S(1)} %copy-done.59), channel_id=1, source_target_pairs={{0,8},{4,12},{8,0},{12,4},{16,24},{20,28},{24,16},{28,20},{1,9},{5... | collective-permute-start | bytes 589832 | tf_op jit(solution)/shard_map/ppermute | solution.py:110
  555.9 154.0 %collective-permute-start.26 = (bf16[1,2,64,768]{3,2,1,0:T(8,128)(2,1)S(1)}, bf16[1,2,64,768]{3,2,1,0:T(8,128)(2,1)}, u32[]{:S(2)}, u32[]{:S(2)}) collective-permute-start(bf16[1,2,64,768]{3,2,1,0:T(8,128)(2,1)S(1)} %copy-done.57), channel_id=1, source_target_pairs={{0,12},{4,8},{8,4},{12,0},{16,28},{20,24},{24,20},{28,16},{1,13},{... | collective-permute-start | bytes 589832 | tf_op jit(solution)/shard_map/ppermute | solution.py:110
  561.5 216.2 %collective-permute-start.51 = (bf16[768,384]{1,0:T(8,128)(2,1)S(1)}, bf16[768,384]{1,0:T(8,128)(2,1)}, u32[]{:S(2)}, u32[]{:S(2)}) collective-permute-start(bf16[768,384]{1,0:T(8,128)(2,1)S(1)} %get-tuple-element.102), channel_id=1, source_target_pairs={{0,24},{4,28},{8,16},{12,20},{16,8},{20,12},{24,0},{28,4},{1,25},{... | collective-permute-start | bytes 1769480 | tf_op jit(solution)/shard_map/ppermute | solution.py:110
  561.9 215.8 %collective-permute-start.50 = (bf16[768,384]{1,0:T(8,128)(2,1)S(1)}, bf16[768,384]{1,0:T(8,128)(2,1)}, u32[]{:S(2)}, u32[]{:S(2)}) collective-permute-start(bf16[768,384]{1,0:T(8,128)(2,1)S(1)} %get-tuple-element.103), channel_id=1, source_target_pairs={{0,16},{4,20},{8,24},{12,28},{16,0},{20,4},{24,8},{28,12},{1,17},{... | collective-permute-start | bytes 1769480 | tf_op jit(solution)/shard_map/ppermute | solution.py:110
  563.5 214.2 %collective-permute-start.49 = (bf16[768,384]{1,0:T(8,128)(2,1)S(1)}, bf16[768,384]{1,0:T(8,128)(2,1)}, u32[]{:S(2)}, u32[]{:S(2)}) collective-permute-start(bf16[768,384]{1,0:T(8,128)(2,1)S(1)} %get-tuple-element.101), channel_id=1, source_target_pairs={{0,8},{4,12},{8,0},{12,4},{16,24},{20,28},{24,16},{28,20},{1,9},{5... | collective-permute-start | bytes 1769480 | tf_op jit(solution)/shard_map/ppermute | solution.py:110
  (129 other events, 3238.5 us)

commit v2 on v1

v2 whole, which is shorter than its diff:
```python
import jax
import jax.numpy as jnp
from jax import lax
from jax.experimental import pallas as pl
from jax.experimental.pallas import tpu as pltpu
from jax.sharding import PartitionSpec as P

HEAD_DIM = 128
SCALE = HEAD_DIM ** (-0.5)
LOG2E = 1.4426950408889634
BLOCK = 16
HIDDEN = -1e30
CHUNKS = 1
BF16 = jnp.bfloat16
F32 = jnp.float32
ANY = pl.BlockSpec(memory_space=pl.ANY)
SMEM = pl.BlockSpec(memory_space=pltpu.SMEM)
LIMIT = pltpu.CompilerParams(vmem_limit_bytes=48 * 2**20)


def dot(a, b):
    return lax.dot_general(a, b, (((1,), (0,)), ((), ())), preferred_element_type=F32)


def dot_nt(a, b):
    return lax.dot_general(a, b, (((1,), (1,)), ((), ())), preferred_element_type=F32)


def dot_tn(a, b):
    return lax.dot_general(a, b, (((0,), (0,)), ((), ())), preferred_element_type=F32)


def swap(value, s):
    count = lax.axis_size("frame")
    return lax.ppermute(value, "frame", [(i, i ^ s) for i in range(count)])


def collect(own, count):
    even = jnp.stack([own] + [swap(own, s) for s in range(2, count, 2)])
    return even, swap(even, 1)


def reduce_pieces(even, odd):
    sums = even + swap(odd.astype(BF16), 1).astype(F32)
    total = sums[0]
    for t in range(1, even.shape[0]):
        total = total + swap(sums[t].astype(BF16), 2 * t).astype(F32)
    return total


def to_positions(arrays, count):
    frames, spatial, channels = arrays[0].shape
    split = [a.reshape(frames, count, 1, spatial // count, channels).transpose(1, 2, 0, 3, 4) for a in arrays]
    return jnp.concatenate(split, axis=1)


def travel(value):
    return lax.all_to_all(value, "frame", split_axis=0, concat_axis=0, tiled=True)


def to_frames(value):
    count, total, frames, part, channels = value.shape
    return value.transpose(1, 2, 0, 3, 4).reshape(total, frames, count * part, channels)


def temporal_bias(rate_scale, rate_reach, starts):
    places = jnp.arange(starts.shape[0], dtype=jnp.int32)
    distance = jnp.abs(places[:, None] - places[None, :]).astype(F32)
    penalty = -rate_scale[:, None, None] * jnp.log1p(rate_reach[:, None, None] * distance[None])
    allowed = (places[:, None] <= places[None, :]) & (places[:, None] >= starts[None, :])
    return jnp.repeat(jnp.where(allowed[None], penalty * LOG2E, HIDDEN), BLOCK, axis=2)


def widen(bias):
    frames, rows = bias.shape
    wide = jnp.broadcast_to(bias[:, None, :], (frames, BLOCK, rows)).reshape(rows, rows)
    key_place = lax.broadcasted_iota(jnp.int32, (rows, rows), 0) % BLOCK
    query_place = lax.broadcasted_iota(jnp.int32, (rows, rows), 1) % BLOCK
    return jnp.where(key_place == query_place, wide, HIDDEN)


def weights_of(scores):
    raised = jnp.exp2(scores - jnp.max(scores, axis=0, keepdims=True))
    return raised, 1.0 / jnp.sum(raised, axis=0, keepdims=True)


def stacked(ref, index):
    value = ref[:, index]
    return value.reshape(value.shape[0] * value.shape[1], HEAD_DIM)


def attend(video, even, odd, bias):
    count, _, frames, part, channels = video.shape
    tokens = even.shape[2]
    heads = channels // HEAD_DIM
    rows = count * frames * BLOCK

    def kernel(video_ref, even_ref, odd_ref, bias_ref, out_ref):
        ref_key = jnp.concatenate([stacked(even_ref, 0), stacked(odd_ref, 0)], axis=0)
        ref_value_t = jnp.concatenate([stacked(even_ref, 1), stacked(odd_ref, 1)], axis=0).T
        wide = widen(bias_ref[0])
        for b in range(part // BLOCK):
            at = slice(b * BLOCK, (b + 1) * BLOCK)
            query, key, value = (video_ref[:, a, :, at, :].reshape(rows, HEAD_DIM) for a in range(3))
            raised, inverse = weights_of(dot_nt(key, query) * (SCALE * LOG2E) + wide)
            total = dot(value.T, raised.astype(BF16)) * inverse
            raised, inverse = weights_of(dot_nt(ref_key, query) * (SCALE * LOG2E))
            total = total + dot(ref_value_t, raised.astype(BF16)) * inverse
            out_ref[:, :, at, :] = total.T.astype(BF16).reshape(count, frames, BLOCK, HEAD_DIM)

    all_rows = count * frames * part
    return pl.pallas_call(
        kernel,
        grid=(heads,),
        in_specs=[pl.BlockSpec((count, 3, frames, part, HEAD_DIM), lambda h: (0, 0, 0, 0, h))]
        + [pl.BlockSpec((count // 2, 2, tokens, HEAD_DIM), lambda h: (0, 0, 0, h))] * 2
        + [pl.BlockSpec((1, count * frames, rows), lambda h: (h, 0, 0))],
        out_specs=pl.BlockSpec((count, frames, part, HEAD_DIM), lambda h: (0, 0, 0, h)),
        out_shape=jax.ShapeDtypeStruct((count, frames, part, channels), BF16),
        compiler_params=LIMIT,
        cost_estimate=pl.CostEstimate(
            flops=4 * all_rows * channels * (rows + tokens * count),
            bytes_accessed=8 * all_rows * channels,
            transcendentals=all_rows * heads * (rows + tokens * count),
        ),
    )(video, even, odd, bias)


def attend_back(video, even, odd, bias, grad):
    count, _, frames, part, channels = video.shape
    tokens = even.shape[2]
    heads = channels // HEAD_DIM
    rows = count * frames * BLOCK
    half = tokens * count // 2

    def kernel(video_ref, even_ref, odd_ref, bias_ref, grad_ref, out_ref, even_out, odd_out):
        ref_key = jnp.concatenate([stacked(even_ref, 0), stacked(odd_ref, 0)], axis=0)
        ref_value = jnp.concatenate([stacked(even_ref, 1), stacked(odd_ref, 1)], axis=0)
        ref_key_t = ref_key.T
        wide = widen(bias_ref[0])

        def back(scores, value, grad_rows):
            raised, inverse = weights_of(scores)
            weights = raised * inverse
            pulled = dot_nt(value, grad_rows)
            centre = jnp.sum(weights * pulled, axis=0, keepdims=True)
            return weights.astype(BF16), (weights * (pulled - centre)).astype(BF16)

        sums = [jnp.zeros((2 * half, HEAD_DIM), F32) for _ in range(2)]
        for b in range(part // BLOCK):
            at = slice(b * BLOCK, (b + 1) * BLOCK)
            query, key, value = (video_ref[:, a, :, at, :].reshape(rows, HEAD_DIM) for a in range(3))
            grad_rows = grad_ref[:, :, at, :].reshape(rows, HEAD_DIM)
            weights, slopes = back(dot_nt(key, query) * (SCALE * LOG2E) + wide, value, grad_rows)
            grad_value = dot(weights, grad_rows)
            grad_key = dot(slopes, query) * SCALE
            grad_query_t = dot(key.T, slopes)
            weights, slopes = back(dot_nt(ref_key, query) * (SCALE * LOG2E), ref_value, grad_rows)
            sums[0] = sums[0] + dot(slopes, query)
            sums[1] = sums[1] + dot(weights, grad_rows)
            grad_query = (grad_query_t + dot(ref_key_t, slopes)).T * SCALE
            for a, result in enumerate((grad_query, grad_key, grad_value)):
                out_ref[:, a, :, at, :] = result.astype(BF16).reshape(count, frames, BLOCK, HEAD_DIM)
        sums[0] = sums[0] * SCALE
        for a in range(2):
            even_out[:, a] = sums[a][:half].reshape(count // 2, tokens, HEAD_DIM)
            odd_out[:, a] = sums[a][half:].reshape(count // 2, tokens, HEAD_DIM)

    all_rows = count * frames * part
    video_spec = pl.BlockSpec((count, 3, frames, part, HEAD_DIM), lambda h: (0, 0, 0, 0, h))
    ref_specs = [pl.BlockSpec((count // 2, 2, tokens, HEAD_DIM), lambda h: (0, 0, 0, h))] * 2
    return pl.pallas_call(
        kernel,
        grid=(heads,),
        in_specs=[
            video_spec,
            *ref_specs,
            pl.BlockSpec((1, count * frames, rows), lambda h: (h, 0, 0)),
            pl.BlockSpec((count, frames, part, HEAD_DIM), lambda h: (0, 0, 0, h)),
        ],
        out_specs=[video_spec, *ref_specs],
        out_shape=[jax.ShapeDtypeStruct(video.shape, BF16)]
        + [jax.ShapeDtypeStruct(even.shape, F32)] * 2,
        compiler_params=LIMIT,
        cost_estimate=pl.CostEstimate(
            flops=10 * all_rows * channels * (rows + tokens * count),
            bytes_accessed=16 * all_rows * channels,
            transcendentals=all_rows * heads * (rows + tokens * count),
        ),
    )(video, even, odd, bias, grad)


def mix_back(cot, taps):
    full, part, channels = cot.shape
    reach = taps.shape[0]

    def kernel(taps_ref, cot_ref, out_ref):
        line = [cot_ref[f].astype(F32) for f in range(full)]
        for f in range(full):
            total = taps_ref[0:1, :] * line[f]
            for k in range(1, min(reach, full - f)):
                total = total + taps_ref[k : k + 1, :] * line[f + k]
            out_ref[f] = total.astype(BF16)

    block = pl.BlockSpec((full, part, HEAD_DIM), lambda h: (0, 0, h))
    return pl.pallas_call(
        kernel,
        grid=(channels // HEAD_DIM,),
        in_specs=[pl.BlockSpec((reach, HEAD_DIM), lambda h: (0, h)), block],
        out_specs=block,
        out_shape=jax.ShapeDtypeStruct(cot.shape, BF16),
        compiler_params=LIMIT,
        cost_estimate=pl.CostEstimate(flops=6 * cot.size, bytes_accessed=4 * cot.size, transcendentals=0),
    )(taps, cot)


def mix(terms, cot, taps):
    full, part, channels = cot.shape
    reach = taps.shape[0]
    total_terms = len(terms)

    def kernel(taps_ref, *refs):
        cot_ref, out_ref, taps_out = refs[total_terms:]
        line = []
        sums = [jnp.zeros((part, HEAD_DIM), F32) for _ in range(reach)]
        for f in range(full):
            value = refs[0][f].astype(F32)
            for term in refs[1:total_terms]:
                value = value + term[f].astype(F32)
            line.append(value.astype(BF16).astype(F32))
            cot_line = cot_ref[f].astype(F32)
            total = jnp.zeros((part, HEAD_DIM), F32)
            for k in range(min(reach, f + 1)):
                total = total + taps_ref[k : k + 1, :] * line[f - k]
                sums[k] = sums[k] + cot_line * line[f - k]
            out_ref[f] = total.astype(BF16)
        for k in range(reach):
            taps_out[k : k + 1, :] = jnp.sum(sums[k], axis=0, keepdims=True)

    block = pl.BlockSpec((full, part, HEAD_DIM), lambda h: (0, 0, h))
    taps_block = pl.BlockSpec((reach, HEAD_DIM), lambda h: (0, h))
    return pl.pallas_call(
        kernel,
        grid=(channels // HEAD_DIM,),
        in_specs=[taps_block] + [block] * (total_terms + 1),
        out_specs=[block, taps_block],
        out_shape=[jax.ShapeDtypeStruct(cot.shape, BF16), jax.ShapeDtypeStruct(taps.shape, F32)],
        compiler_params=LIMIT,
        cost_estimate=pl.CostEstimate(flops=12 * cot.size, bytes_accessed=10 * cot.size, transcendentals=0),
    )(taps, *terms, cot)


def weight_terms(attended, blocks, level, count):
    depth = lax.axis_size("head")
    chunks = len(attended)
    rows, channels = attended[0].shape
    parts = count // depth
    columns = channels // parts
    offsets = sorted(blocks[0])

    def kernel(level_ref, *refs):
        held = refs[:chunks]
        sources = [
            {d: refs[chunks + c * len(offsets) + k] for k, d in enumerate(offsets)} for c in range(chunks)
        ]
        out_ref, buffer, turned, sems = refs[chunks + chunks * len(offsets) :]
        j = pl.program_id(0)

        def fetch(target, slot):
            for d in offsets:

                @pl.when(target - level_ref[0] == d)
                def _():
                    for c in range(chunks):
                        pltpu.make_async_copy(sources[c][d], buffer.at[slot, c], sems.at[slot, c]).start()

        @pl.when(j == 0)
        def _():
            fetch(j, 0)
            for c in range(chunks):
                turned[c] = held[c][...].T

        @pl.when(j + 1 < depth)
        def _():
            fetch(j + 1, (j + 1) % 2)

        total = None
        for c in range(chunks):
            pltpu.make_async_copy(sources[c][0], buffer.at[j % 2, c], sems.at[j % 2, c]).wait()
            term = dot(turned[c], buffer[j % 2, c])
            total = term if total is None else total + term
        for p in range(parts):
            out_ref[0, p] = total[:, p * columns : (p + 1) * columns].astype(BF16)

    flat = [blocks[c][d] for c in range(chunks) for d in offsets]
    return pl.pallas_call(
        kernel,
        grid=(depth,),
        in_specs=[SMEM]
        + [pl.BlockSpec((rows, channels), lambda j: (0, 0))] * chunks
        + [ANY] * len(flat),
        out_specs=pl.BlockSpec((1, parts, channels, columns), lambda j: (j, 0, 0, 0)),
        out_shape=jax.ShapeDtypeStruct((depth, parts, channels, columns), BF16),
        scratch_shapes=[
            pltpu.VMEM((2, chunks, rows, channels), BF16),
            pltpu.VMEM((chunks, channels, rows), BF16),
            pltpu.SemaphoreType.DMA((2, chunks)),
        ],
        compiler_params=LIMIT,
        cost_estimate=pl.CostEstimate(
            flops=2 * chunks * rows * channels * channels * depth,
            bytes_accessed=4 * chunks * rows * channels * depth,
            transcendentals=0,
        ),
    )(level.reshape(1).astype(jnp.int32), *attended, *flat)


def after(value, *others):
    return lax.optimization_barrier((value, *others))[0]


def per_device(
    queries,
    keys,
    values,
    ref_keys,
    ref_values,
    rate_scale,
    rate_reach,
    window_start,
    out_weight,
    conv_taps,
    cotangent,
):
    frames, spatial, channels = queries.shape
    width = out_weight.shape[1]
    count, depth = lax.axis_size("frame"), lax.axis_size("head")
    place, level = lax.axis_index("frame"), lax.axis_index("head")
    part = spatial // count // CHUNKS
    rows = count * frames * part
    line_shape = (count * frames, part, channels)

    def chunk_of(array, c):
        return lax.slice_in_dim(array, c * (spatial // CHUNKS), (c + 1) * (spatial // CHUNKS), axis=1)

    def weight_block(j):
        return lax.dynamic_slice_in_dim(out_weight, jnp.clip(j, 0, depth - 1) * channels, channels, 1)

    even, odd = collect(jnp.stack([ref_keys, ref_values]), count)
    bias = temporal_bias(rate_scale, rate_reach, window_start)

    cot, video = [], []
    for c in range(CHUNKS):
        packed = to_positions([chunk_of(cotangent, c)], count)
        if c > 0:
            packed = after(packed, video[-1])
        cot.append(travel(packed).reshape(line_shape))
        packed = to_positions([chunk_of(a, c) for a in (queries, keys, values)], count)
        video.append(travel(after(packed, cot[-1])))

    blocks, totals = [], []
    for c in range(CHUNKS):
        own = mix_back(cot[c], conv_taps).reshape(rows, channels)
        arrived = {0: own}
        total = dot_nt(own, weight_block(level))
        up = down = own
        for s in range(1, depth):
            up = lax.ppermute(up, "head", [(i, i + 1) for i in range(s - 1, depth - 1)])
            down = lax.ppermute(down, "head", [(i, i - 1) for i in range(1, depth - s + 1)])
            arrived[-s], arrived[s] = up, down
            if 2 * s < depth:
                total = total + dot_nt(up, weight_block(level - s)) + dot_nt(down, weight_block(level + s))
            else:
                below = level >= s
                total = total + dot_nt(
                    jnp.where(below, up, down), weight_block(jnp.where(below, level - s, level + s))
                )
        blocks.append(arrived)
        totals.append(total.astype(BF16).reshape(count, frames, part, channels))

    attended = [attend(video[c], even, odd, bias).reshape(rows, channels) for c in range(CHUNKS)]

    outs, taps_sum = [], 0.0
    for c in range(CHUNKS):
        shares = dot(attended[c], out_weight).astype(BF16)

        def share(j):
            return lax.dynamic_slice_in_dim(shares, jnp.clip(j, 0, depth - 1) * channels, channels, 1)

        up = down = None
        for s in range(1, depth):
            far = depth - s
            send_up, send_down = share(level + far), share(level - far)
            if s > 1:
                send_up = (send_up.astype(F32) + up.astype(F32)).astype(BF16)
                send_down = (send_down.astype(F32) + down.astype(F32)).astype(BF16)
            up = lax.ppermute(send_up, "head", [(i, i + 1) for i in range(depth - far)])
            down = lax.ppermute(send_down, "head", [(i, i - 1) for i in range(far, depth)])
        out, taps_part = mix([t.reshape(line_shape) for t in (share(level), up, down)], cot[c], conv_taps)
        outs.append(to_frames(travel(out.reshape(count, 1, frames, part, channels))))
        taps_sum = taps_sum + taps_part

    terms = weight_terms(attended, blocks, level, count)
    columns = terms.shape[3]
    by_chip = terms.reshape(count // 2, 2, channels, columns)
    core = place % 2
    near = swap(lax.dynamic_index_in_dim(by_chip, 1 - core, 1, keepdims=False), 1)
    sums = lax.dynamic_index_in_dim(by_chip, core, 1, keepdims=False).astype(F32) + near.astype(F32)
    groups = [list(range(k, count, 2)) for k in range(2)]
    far = lax.all_to_all(
        sums.astype(BF16), "frame", split_axis=0, concat_axis=0, axis_index_groups=groups, tiled=True
    )
    grad_weight = jnp.sum(far.astype(F32), axis=0)

    grads, ref_even, ref_odd = [], 0.0, 0.0
    for c in range(CHUNKS):
        back, even_part, odd_part = attend_back(video[c], even, odd, bias, totals[c])
        grads.append(to_frames(travel(back)))
        ref_even, ref_odd = ref_even + even_part, ref_odd + odd_part
    ref_grads = reduce_pieces(ref_even, ref_odd)

    step = 1
    while step < count:
        taps_sum = taps_sum + swap(taps_sum, step)
        step *= 2

    block_out = jnp.concatenate([out[0] for out in outs], axis=1)
    grad_queries, grad_keys, grad_values = (
        jnp.concatenate([grad[a] for grad in grads], axis=1) for a in range(3)
    )
    return (
        block_out,
        grad_queries,
        grad_keys,
        grad_values,
        ref_grads[0],
        ref_grads[1],
        grad_weight,
        taps_sum,
    )


def solution(mesh):
    video = P("frame", None, "head")
    tokens = P("frame", "head")
    return jax.shard_map(
        per_device,
        mesh=mesh,
        in_specs=(
            video,
            video,
            video,
            tokens,
            tokens,
            P("head"),
            P("head"),
            P(),
            P("head", None),
            P(None, "head"),
            video,
        ),
        out_specs=(video, video, video, video, tokens, tokens, P("head", "frame"), P(None, "head")),
        check_vma=False,
    )
```

time: 791 us -> 382 us (0.48)
  Pallas kernels: 437 us -> 58.8 us
  waiting for transfers between devices: 105 us -> 160 us
  starting transfers between devices: 112 us -> 59.8 us
  blocking collectives: 0 us -> 25.9 us
  local copies, waits for them, and re-layouts: 47.3 us -> 22.4 us
  matrix products: 44.7 us -> 29.3 us
  other arithmetic: 32.3 us -> 22 us
    pallas_call x8 -> x5, Pallas kernels: 437 us -> 58.8 us  [the longest x1 27 us: attend_back(): pl.pallas_call(kernel, grid=(heads,), in_specs=[video_spec, *ref_specs, p...]
    ppermute x43 -> x12, waiting for transfers between devices: 93.8 us -> 36.2 us  [swap(): return lax.ppermute(value, 'frame', [(i, i ^ s) for i in range(count)])]
    ppermute x3, waiting for transfers between devices: 5.75 us -> 59.9 us  [per_device(): up = lax.ppermute(send_up, 'head', [(i, i + 1) for i in range(depth - far)])]
    ppermute x3, waiting for transfers between devices: 5.21 us -> 42.4 us  [per_device(): lax.ppermute(down, 'head', [(i, i - 1) for i in range(1, depth - s + 1)])]
    ppermute x3, starting transfers between devices: 53.1 us -> 17.2 us  [per_device(): up = lax.ppermute(send_up, 'head', [(i, i + 1) for i in range(depth - far)])]
    ppermute x43 -> x12, starting transfers between devices: 42.4 us -> 8.66 us  [swap(): return lax.ppermute(value, 'frame', [(i, i ^ s) for i in range(count)])]
    all_to_all x0 -> x1, blocking collectives: none -> 25.9 us  [travel(): lax.all_to_all(value, 'frame', split_axis=0, concat_axis=0, tiled=True)]
    broadcast_in_dim x5 -> x1, local copies, waits for them, and re-layouts: 26.3 us -> 1.15 us  [temporal_bias(): jnp.repeat(jnp.where(allowed[None], penalty * LOG2E, HIDDEN), BLOCK, axis=2)]
  transfers between devices with their start and end apart: 55 -> 28, of which waited for: 18 -> 13; matrix products, arithmetic and copies ran while one was open for 14% -> 17% of each run, Pallas kernels for 56% -> 13%
where the time goes in v2:
time: 382 us; the launch traced here: 380 us
  waiting for transfers between devices  160 us (42%)
  starting transfers between devices  59.8 us (16%)
  Pallas kernels  58.8 us (15%)
  matrix products  29.3 us (8%)
  blocking collectives  25.9 us (7%)
  local copies, waits for them, and re-layouts  22.4 us (6%)
  other arithmetic  22 us (6%)
    ppermute x3, waiting for transfers between devices, per_device(): up = lax.ppermute(send_up, 'head', [(i, i + 1) for i in range(depth - far)])  59.9 us
    ppermute x3, waiting for transfers between devices, per_device(): lax.ppermute(down, 'head', [(i, i - 1) for i in range(1, depth - s + 1)])  42.4 us
    ppermute x12, waiting for transfers between devices, swap(): return lax.ppermute(value, 'frame', [(i, i ^ s) for i in range(count)])  36.2 us
    pallas_call x1, Pallas kernels, attend_back(): pl.pallas_call(kernel, grid=(heads,), in_specs=[video_spec, *ref_specs, p...  27 us
    all_to_all x1, blocking collectives, travel(): lax.all_to_all(value, 'frame', split_axis=0, concat_axis=0, tiled=True)  25.9 us
    dot_general x5, matrix products, dot_nt(): lax.dot_general(a, b, (((1,), (1,)), ((), ())), preferred_element_type=F32)  22 us
    ppermute x3, waiting for transfers between devices, per_device(): up = lax.ppermute(up, 'head', [(i, i + 1) for i in range(s - 1, depth - 1)])  21.8 us
    ppermute x3, starting transfers between devices, per_device(): up = lax.ppermute(send_up, 'head', [(i, i + 1) for i in range(depth - far)])  17.2 us
  transfers between devices with their start and end apart: 28, of which 13 were waited for; matrix products, arithmetic and copies ran while one was open for 17% of the time, Pallas kernels for 13%

profile of v2, /device:TPU:0, one launch (start us, length us, event | category | flops | bytes accessed | tf_op | source)
XLA Modules:
  0.0 379.7 jit_solution(1095492768146666519)
XLA Ops:
  2.2 25.9 %all_to_all.25 = bf16[8,1,2,64,768]{4,3,2,1,0:T(8,128)(2,1)S(1)} all-to-all(bf16[8,1,2,64,768]{4,3,2,1,0:T(8,128)(2,1)S(1)} %copy.39), channel_id=1, replica_groups=mesh['frame'=8,'head'=4] {'frame'}, dimensions={0} | all-to-all | bytes 3145728 | tf_op jit(solution)/shard_map/all_to_all | solution.py:58
  29.5 4.8 %collective-permute-start.10 = (bf16[1024,768]{1,0:T(8,128)(2,1)S(1)}, bf16[1024,768]{1,0:T(8,128)(2,1)}, u32[]{:S(2)}, u32[]{:S(2)}) collective-permute-start(bf16[1024,768]{1,0:T(8,128)(2,1)S(1)} %bitcast.71), channel_id=1, source_target_pairs={{0,1},{1,2},{2,3},{4,5},{5,6},{6,7},{8,9},{9,10},{10,11},{12,13},{... | collective-permute-start | bytes 4718600 | tf_op jit(solution)/shard_map/ppermute | solution.py:368
  39.5 4.7 %all-to-all-start.1 = ((bf16[8,3,2,64,768]{4,3,2,1,0:T(8,128)(2,1)}), bf16[8,3,2,64,768]{4,3,2,1,0:T(8,128)(2,1)}, u32[]{:S(2)}, u32[]{:S(2)}) async-start(bf16[8,3,2,64,768]{4,3,2,1,0:T(8,128)(2,1)} %pad_maximum_fusion), calls=%async_computation.1 | async-start | bytes 9437184 | tf_op jit(solution)/shard_map/all_to_all | solution.py:58
  44.3 21.8 %collective-permute-done.10.refs_3_ = bf16[1024,768]{1,0:T(8,128)(2,1)} collective-permute-done((bf16[1024,768]{1,0:T(8,128)(2,1)S(1)}, bf16[1024,768]{1,0:T(8,128)(2,1)}, u32[]{:S(2)}, u32[]{:S(2)}) %collective-permute-start.10) | collective-permute-done | bytes 1572896 | tf_op jit(solution)/shard_map/ppermute | solution.py:368
  73.5 34.6 %collective-permute-done.13.refs_6_ = bf16[1024,768]{1,0:T(8,128)(2,1)} collective-permute-done((bf16[1024,768]{1,0:T(8,128)(2,1)}, bf16[1024,768]{1,0:T(8,128)(2,1)}, u32[]{:S(2)}, u32[]{:S(2)}) %collective-permute-start.13) | collective-permute-done | bytes 1572896 | tf_op jit(solution)/shard_map/ppermute | solution.py:369
  113.1 4.2 %collective-permute-done = bf16[2,64,768]{2,1,0:T(8,128)(2,1)S(1)} collective-permute-done((bf16[2,64,768]{2,1,0:T(8,128)(2,1)S(1)}, bf16[2,64,768]{2,1,0:T(8,128)(2,1)S(1)}, u32[]{:S(2)}, u32[]{:S(2)}) %collective-permute-start) | collective-permute-done | bytes 196640 | tf_op jit(solution)/shard_map/ppermute | solution.py:35
  123.3 16.1 %shard_map.170 = bf16[8,2,64,768]{3,2,1,0:T(8,128)(2,1)S(1)} custom-call(bf16[8,3,2,64,768]{4,3,2,1,0:T(8,128)(2,1)} %all-to-all-done.1.video_ref, bf16[4,2,64,768]{3,2,1,0:T(8,128)(2,1)S(1)} %pad_maximum_fusion.1.even_ref, bf16[4,2,64,768]{3,2,1,0:T(8,128)(2,1)S(1)} %collective-permute-done.3.odd_ref, f32[6,16,256]{2,1,0:T(8,128)S(1)} %reshape.126.bias_ref), custom_call_target="tpu_custom_call" | custom-call | flops 2415919104 | bytes 6291456 | tf_op jit(solution)/shard_map/pallas_call | solution.py:112
  139.4 4.3 %collective-permute-done.15.refs_7_ = bf16[1024,768]{1,0:T(8,128)(2,1)} collective-permute-done((bf16[1024,768]{1,0:T(8,128)(2,1)}, bf16[1024,768]{1,0:T(8,128)(2,1)}, u32[]{:S(2)}, u32[]{:S(2)}) %collective-permute-start.15) | collective-permute-done | bytes 1572896 | tf_op jit(solution)/shard_map/ppermute | solution.py:369
  143.8 8.6 %shard_map.174 = bf16[4,2,768,384]{3,2,1,0:T(8,128)(2,1)} custom-call(s32[1]{0:T(128)} %bitcast.35.level_ref, bf16[1024,768]{1,0:T(8,128)(2,1)S(1)} %bitcast.76, bf16[1024,768]{1,0:T(8,128)(2,1)S(1)} %collective-permute-done.14.refs_1_, bf16[1024,768]{1,0:T(8,128)(2,1)} %collective-permute-done.12.refs_2_, ...), custom_call_target="tpu_custom_call" | custom-call | flops 4831838208 | bytes 12582912 | tf_op jit(solution)/shard_map/pallas_call | solution.py:296
  155.8 7.4 %convolution_convert_fusion = bf16[1024,3072]{1,0:T(8,128)(2,1)S(1)} fusion(bf16[1024,768]{1,0:T(8,128)(2,1)} %bitcast.77, bf16[768,3072]{1,0:T(8,128)(2,1)} %param.19), kind=kOutput, calls=%fused_computation | convolution fusion | flops 4834983936 | bytes 12582912 | tf_op jit(solution)/shard_map/dot_general | solution.py:22
  168.7 4.4 %fusion.12 = f32[1024,768]{1,0:T(8,128)} fusion(bf16[1024,768]{1,0:T(8,128)(2,1)S(1)} %bitcast.74, bf16[768,3072]{1,0:T(8,128)(2,1)} %param.19, s32[]{:T(128)S(6)} %select_n.69), kind=kOutput, calls=%fused_computation.26 | convolution fusion | flops 1207959552 | bytes 5898244 | tf_op jit(solution)/shard_map/dot_general | solution.py:26
  173.1 4.7 %fusion.10 = f32[1024,768]{1,0:T(8,128)} fusion(bf16[1024,768]{1,0:T(8,128)(2,1)} %collective-permute-done.10.refs_3_, bf16[768,3072]{1,0:T(8,128)(2,1)S(1)} %bitcast.92, s32[]{:T(128)S(6)} %select_n.73), kind=kOutput, calls=%fused_computation.24 | convolution fusion | flops 1207959552 | bytes 5898244 | tf_op jit(solution)/shard_map/dot_general | solution.py:26
  177.8 4.6 %fusion.8 = f32[1024,768]{1,0:T(8,128)} fusion(bf16[1024,768]{1,0:T(8,128)(2,1)} %collective-permute-done.11.refs_5_, bf16[768,3072]{1,0:T(8,128)(2,1)S(1)} %bitcast.92, s32[]{:T(128)S(6)} %select_n.70), kind=kOutput, calls=%fused_computation.22 | convolution fusion | flops 1207959552 | bytes 5898244 | tf_op jit(solution)/shard_map/dot_general | solution.py:26
  186.3 4.5 %all-to-all-start.4 = ((bf16[4,768,384]{2,1,0:T(8,128)(2,1)}), bf16[4,768,384]{2,1,0:T(8,128)(2,1)}, u32[]{:S(2)}, u32[]{:S(2)}) async-start(bf16[4,768,384]{2,1,0:T(8,128)(2,1)} %fusion), calls=%async_computation.4 | async-start | bytes 4718592 | tf_op jit(solution)/shard_map/all_to_all | solution.py:410
  203.2 4.9 %add_convert_fusion = bf16[1024,768]{1,0:T(8,128)(2,1)} fusion(f32[1024,768]{1,0:T(8,128)S(1)} %fusion.2, f32[1024,768]{1,0:T(8,128)S(1)} %copy-done.14, f32[1024,768]{1,0:T(8,128)S(1)} %copy-done.12, f32[1024,768]{1,0:T(8,128)S(1)} %copy-done.13, bf16[1024,768]{1,0:T(8,128)(2,1)S(1)} %collective-permute-done.14.refs_1_, ...), kind=kOutput, calls=%fused_computation.5 | convolution fusion | flops 1212678144 | bytes 18481156 | tf_op jit(solution)/shard_map/dot_general | solution.py:26
  208.1 27.0 %shard_map.173 = (bf16[8,3,2,64,768]{4,3,2,1,0:T(8,128)(2,1)}, f32[4,2,64,768]{3,2,1,0:T(8,128)S(1)}, f32[4,2,64,768]{3,2,1,0:T(8,128)S(1)}) custom-call(bf16[8,3,2,64,768]{4,3,2,1,0:T(8,128)(2,1)} %all-to-all-done.1.video_ref, bf16[4,2,64,768]{3,2,1,0:T(8,128)(2,1)S(1)} %copy-done.6, bf16[4,2,64,768]{3,2,1,0:T(8,128)(2,1)S(1)} %copy-done.9, ...), custom_call_target="tpu_custom_call" | custom-call | flops 6039797760 | bytes 12582912 | tf_op jit(solution)/shard_map/pallas_call | solution.py:172
  236.3 4.6 %all-to-all-start.3 = ((bf16[8,3,2,64,768]{4,3,2,1,0:T(8,128)(2,1)}), bf16[8,3,2,64,768]{4,3,2,1,0:T(8,128)(2,1)}, u32[]{:S(2)}, u32[]{:S(2)}) async-start(bf16[8,3,2,64,768]{4,3,2,1,0:T(8,128)(2,1)} %get-tuple-element.16), calls=%async_computation.3 | async-start | bytes 9437184 | tf_op jit(solution)/shard_map/all_to_all | solution.py:58
  244.5 6.0 %collective-permute-start.5 = (bf16[1024,768]{1,0:T(8,128)(2,1)S(1)}, bf16[1024,768]{1,0:T(8,128)(2,1)S(1)}, u32[]{:S(2)}, u32[]{:S(2)}) collective-permute-start(bf16[1024,768]{1,0:T(8,128)(2,1)S(1)} %get-tuple-element.23), channel_id=1, source_target_pairs={{0,1},{1,2},{4,5},{5,6},{8,9},{9,10},{12,13},{13,14},{16,17},{17,1... | collective-permute-start | bytes 4718600 | tf_op jit(solution)/shard_map/ppermute | solution.py:397
  251.8 30.7 %collective-permute-done.5 = bf16[1024,768]{1,0:T(8,128)(2,1)S(1)} collective-permute-done((bf16[1024,768]{1,0:T(8,128)(2,1)S(1)}, bf16[1024,768]{1,0:T(8,128)(2,1)S(1)}, u32[]{:S(2)}, u32[]{:S(2)}) %collective-permute-start.5) | collective-permute-done | bytes 1572896 | tf_op jit(solution)/shard_map/ppermute | solution.py:397
  284.4 7.6 %collective-permute-start.6 = (bf16[1024,768]{1,0:T(8,128)(2,1)S(1)}, bf16[1024,768]{1,0:T(8,128)(2,1)S(1)}, u32[]{:S(2)}, u32[]{:S(2)}) collective-permute-start(bf16[1024,768]{1,0:T(8,128)(2,1)S(1)} %add_convert_fusion.3), channel_id=1, source_target_pairs={{0,1},{1,2},{2,3},{4,5},{5,6},{6,7},{8,9},{9,10},{10,11},{12,13},{... | collective-permute-start | bytes 4718600 | tf_op jit(solution)/shard_map/ppermute | solution.py:397
  296.1 29.2 %collective-permute-done.6 = bf16[1024,768]{1,0:T(8,128)(2,1)S(1)} collective-permute-done((bf16[1024,768]{1,0:T(8,128)(2,1)S(1)}, bf16[1024,768]{1,0:T(8,128)(2,1)S(1)}, u32[]{:S(2)}, u32[]{:S(2)}) %collective-permute-start.6) | collective-permute-done | bytes 1572896 | tf_op jit(solution)/shard_map/ppermute | solution.py:397
  325.3 5.8 %shard_map.171 = (bf16[16,64,768]{2,1,0:T(8,128)(2,1)}, f32[3,768]{1,0:T(4,128)S(1)}) custom-call(f32[3,768]{1,0:T(4,128)S(1)} %copy-done.7, bf16[16,64,768]{2,1,0:T(8,128)(2,1)S(1)} %bitcast.70, bf16[16,64,768]{2,1,0:T(8,128)(2,1)S(1)} %bitcast.75, bf16[16,64,768]{2,1,0:T(8,128)(2,1)} %bitcast.90, bf16[16,64,768]{2,1,0:T(8,128)(2,1)} %bitcast.69), custom_call_target="tpu_custom_call" | custom-call | flops 9437184 | bytes 7864320 | tf_op jit(solution)/shard_map/pallas_call | solution.py:242
  338.5 21.2 %collective-permute-done.17 = bf16[2,64,768]{2,1,0:T(8,128)(2,1)S(1)} collective-permute-done((bf16[2,64,768]{2,1,0:T(8,128)(2,1)S(1)}, bf16[2,64,768]{2,1,0:T(8,128)(2,1)S(1)}, u32[]{:S(2)}, u32[]{:S(2)}) %collective-permute-start.17) | collective-permute-done | bytes 196640 | tf_op jit(solution)/shard_map/ppermute | solution.py:35
  359.7 4.6 %collective-permute-done.19 = bf16[2,64,768]{2,1,0:T(8,128)(2,1)S(1)} collective-permute-done((bf16[2,64,768]{2,1,0:T(8,128)(2,1)S(1)}, bf16[2,64,768]{2,1,0:T(8,128)(2,1)S(1)}, u32[]{:S(2)}, u32[]{:S(2)}) %collective-permute-start.19) | collective-permute-done | bytes 196640 | tf_op jit(solution)/shard_map/ppermute | solution.py:35
  (136 shorter events, 86.3 us)
Async XLA Ops:
  29.5 36.6 %collective-permute-start.10 = (bf16[1024,768]{1,0:T(8,128)(2,1)S(1)}, bf16[1024,768]{1,0:T(8,128)(2,1)}, u32[]{:S(2)}, u32[]{:S(2)}) collective-permute-start(bf16[1024,768]{1,0:T(8,128)(2,1)S(1)} %bitcast.71), channel_id=1, source_target_pairs={{0,1},{1,2},{2,3},{4,5},{5,6},{6,7},{8,9},{9,10},{10,11},{12,13},{... | collective-permute-start | bytes 4718600 | tf_op jit(solution)/shard_map/ppermute | solution.py:368
  34.2 37.2 %collective-permute-start.11 = (bf16[1024,768]{1,0:T(8,128)(2,1)S(1)}, bf16[1024,768]{1,0:T(8,128)(2,1)}, u32[]{:S(2)}, u32[]{:S(2)}) collective-permute-start(bf16[1024,768]{1,0:T(8,128)(2,1)S(1)} %bitcast.72), channel_id=1, source_target_pairs={{1,0},{2,1},{3,2},{5,4},{6,5},{7,6},{9,8},{10,9},{11,10},{13,12},{... | collective-permute-start | bytes 4718600 | tf_op jit(solution)/shard_map/ppermute | solution.py:369
  39.5 83.8 %all-to-all-start.1 = ((bf16[8,3,2,64,768]{4,3,2,1,0:T(8,128)(2,1)}), bf16[8,3,2,64,768]{4,3,2,1,0:T(8,128)(2,1)}, u32[]{:S(2)}, u32[]{:S(2)}) async-start(bf16[8,3,2,64,768]{4,3,2,1,0:T(8,128)(2,1)} %pad_maximum_fusion), calls=%async_computation.1 | async-start | bytes 9437184 | tf_op jit(solution)/shard_map/all_to_all | solution.py:58
  66.1 6.6 %collective-permute-start.12 = (bf16[1024,768]{1,0:T(8,128)(2,1)}, bf16[1024,768]{1,0:T(8,128)(2,1)}, u32[]{:S(2)}, u32[]{:S(2)}) collective-permute-start(bf16[1024,768]{1,0:T(8,128)(2,1)} %collective-permute-done.10.refs_3_), channel_id=1, source_target_pairs={{1,2},{2,3},{5,6},{6,7},{9,10},{10,11},{13,14},{14,15},{17,18},{18... | collective-permute-start | bytes 4718600 | tf_op jit(solution)/shard_map/ppermute | solution.py:368
  71.4 36.6 %collective-permute-start.13 = (bf16[1024,768]{1,0:T(8,128)(2,1)}, bf16[1024,768]{1,0:T(8,128)(2,1)}, u32[]{:S(2)}, u32[]{:S(2)}) collective-permute-start(bf16[1024,768]{1,0:T(8,128)(2,1)} %collective-permute-done.11.refs_5_), channel_id=1, source_target_pairs={{1,0},{2,1},{5,4},{6,5},{9,8},{10,9},{13,12},{14,13},{17,16},{18,1... | collective-permute-start | bytes 4718600 | tf_op jit(solution)/shard_map/ppermute | solution.py:369
  72.7 66.7 %collective-permute-start.14 = (bf16[1024,768]{1,0:T(8,128)(2,1)}, bf16[1024,768]{1,0:T(8,128)(2,1)S(1)}, u32[]{:S(2)}, u32[]{:S(2)}) collective-permute-start(bf16[1024,768]{1,0:T(8,128)(2,1)} %collective-permute-done.12.refs_2_), channel_id=1, source_target_pairs={{2,3},{6,7},{10,11},{14,15},{18,19},{22,23},{26,27},{30,31}} | collective-permute-start | bytes 4718600 | tf_op jit(solution)/shard_map/ppermute | solution.py:368
  108.0 35.7 %collective-permute-start.15 = (bf16[1024,768]{1,0:T(8,128)(2,1)}, bf16[1024,768]{1,0:T(8,128)(2,1)}, u32[]{:S(2)}, u32[]{:S(2)}) collective-permute-start(bf16[1024,768]{1,0:T(8,128)(2,1)} %collective-permute-done.13.refs_6_), channel_id=1, source_target_pairs={{1,0},{5,4},{9,8},{13,12},{17,16},{21,20},{25,24},{29,28}} | collective-permute-start | bytes 4718600 | tf_op jit(solution)/shard_map/ppermute | solution.py:369
  109.4 7.9 %collective-permute-start = (bf16[2,64,768]{2,1,0:T(8,128)(2,1)S(1)}, bf16[2,64,768]{2,1,0:T(8,128)(2,1)S(1)}, u32[]{:S(2)}, u32[]{:S(2)}) collective-permute-start(bf16[2,64,768]{2,1,0:T(8,128)(2,1)S(1)} %get-tuple-element.36), channel_id=1, source_target_pairs={{0,8},{4,12},{8,0},{12,4},{16,24},{20,28},{24,16},{28,20},{1,9},{5... | collective-permute-start | bytes 589832 | tf_op jit(solution)/shard_map/ppermute | solution.py:35
  111.6 8.8 %collective-permute-start.1 = (bf16[2,64,768]{2,1,0:T(8,128)(2,1)S(1)}, bf16[2,64,768]{2,1,0:T(8,128)(2,1)S(1)}, u32[]{:S(2)}, u32[]{:S(2)}) collective-permute-start(bf16[2,64,768]{2,1,0:T(8,128)(2,1)S(1)} %get-tuple-element.36), channel_id=1, source_target_pairs={{0,16},{4,20},{8,24},{12,28},{16,0},{20,4},{24,8},{28,12},{1,17},{... | collective-permute-start | bytes 589832 | tf_op jit(solution)/shard_map/ppermute | solution.py:35
  111.9 8.5 %collective-permute-start.2 = (bf16[2,64,768]{2,1,0:T(8,128)(2,1)S(1)}, bf16[2,64,768]{2,1,0:T(8,128)(2,1)S(1)}, u32[]{:S(2)}, u32[]{:S(2)}) collective-permute-start(bf16[2,64,768]{2,1,0:T(8,128)(2,1)S(1)} %get-tuple-element.36), channel_id=1, source_target_pairs={{0,24},{4,28},{8,16},{12,20},{16,8},{20,12},{24,0},{28,4},{1,25},{... | collective-permute-start | bytes 589832 | tf_op jit(solution)/shard_map/ppermute | solution.py:35
  155.8 26.6 %collective-permute-start.20 = (bf16[4,768,384]{2,1,0:T(8,128)(2,1)}, bf16[4,768,384]{2,1,0:T(8,128)(2,1)}, u32[]{:S(2)}, u32[]{:S(2)}) collective-permute-start(bf16[4,768,384]{2,1,0:T(8,128)(2,1)} %dynamic-slice_bitcast_fusion), channel_id=1, source_target_pairs={{0,4},{4,0},{8,12},{12,8},{16,20},{20,16},{24,28},{28,24},{1,5},{5... | collective-permute-start | bytes 7077896 | tf_op jit(solution)/shard_map/ppermute | solution.py:35
  166.7 31.0 %collective-permute-start.7 = (bf16[1024,768]{1,0:T(8,128)(2,1)}, bf16[1024,768]{1,0:T(8,128)(2,1)}, u32[]{:S(2)}, u32[]{:S(2)}) collective-permute-start(bf16[1024,768]{1,0:T(8,128)(2,1)} %get-tuple-element.24), channel_id=1, source_target_pairs={{3,2},{7,6},{11,10},{15,14},{19,18},{23,22},{27,26},{31,30}} | collective-permute-start | bytes 4718600 | tf_op jit(solution)/shard_map/ppermute | solution.py:398
  186.3 50.0 %all-to-all-start.4 = ((bf16[4,768,384]{2,1,0:T(8,128)(2,1)}), bf16[4,768,384]{2,1,0:T(8,128)(2,1)}, u32[]{:S(2)}, u32[]{:S(2)}) async-start(bf16[4,768,384]{2,1,0:T(8,128)(2,1)} %fusion), calls=%async_computation.4 | async-start | bytes 4718592 | tf_op jit(solution)/shard_map/all_to_all | solution.py:410
  194.2 46.6 %collective-permute-start.4 = (bf16[1024,768]{1,0:T(8,128)(2,1)}, bf16[1024,768]{1,0:T(8,128)(2,1)}, u32[]{:S(2)}, u32[]{:S(2)}) collective-permute-start(bf16[1024,768]{1,0:T(8,128)(2,1)} %get-tuple-element.25), channel_id=1, source_target_pairs={{0,1},{4,5},{8,9},{12,13},{16,17},{20,21},{24,25},{28,29}} | collective-permute-start | bytes 4718600 | tf_op jit(solution)/shard_map/ppermute | solution.py:397
  201.2 39.7 %collective-permute-start.8 = (bf16[1024,768]{1,0:T(8,128)(2,1)}, bf16[1024,768]{1,0:T(8,128)(2,1)}, u32[]{:S(2)}, u32[]{:S(2)}) collective-permute-start(bf16[1024,768]{1,0:T(8,128)(2,1)} %add_convert_fusion.2), channel_id=1, source_target_pairs={{2,1},{3,2},{6,5},{7,6},{10,9},{11,10},{14,13},{15,14},{18,17},{19... | collective-permute-start | bytes 4718600 | tf_op jit(solution)/shard_map/ppermute | solution.py:398
  236.3 94.8 %all-to-all-start.3 = ((bf16[8,3,2,64,768]{4,3,2,1,0:T(8,128)(2,1)}), bf16[8,3,2,64,768]{4,3,2,1,0:T(8,128)(2,1)}, u32[]{:S(2)}, u32[]{:S(2)}) async-start(bf16[8,3,2,64,768]{4,3,2,1,0:T(8,128)(2,1)} %get-tuple-element.16), calls=%async_computation.3 | async-start | bytes 9437184 | tf_op jit(solution)/shard_map/all_to_all | solution.py:58
  244.5 38.0 %collective-permute-start.5 = (bf16[1024,768]{1,0:T(8,128)(2,1)S(1)}, bf16[1024,768]{1,0:T(8,128)(2,1)S(1)}, u32[]{:S(2)}, u32[]{:S(2)}) collective-permute-start(bf16[1024,768]{1,0:T(8,128)(2,1)S(1)} %get-tuple-element.23), channel_id=1, source_target_pairs={{0,1},{1,2},{4,5},{5,6},{8,9},{9,10},{12,13},{13,14},{16,17},{17,1... | collective-permute-start | bytes 4718600 | tf_op jit(solution)/shard_map/ppermute | solution.py:397
  250.5 45.6 %collective-permute-start.9 = (bf16[1024,768]{1,0:T(8,128)(2,1)S(1)}, bf16[1024,768]{1,0:T(8,128)(2,1)S(1)}, u32[]{:S(2)}, u32[]{:S(2)}) collective-permute-start(bf16[1024,768]{1,0:T(8,128)(2,1)S(1)} %get-tuple-element.22), channel_id=1, source_target_pairs={{1,0},{2,1},{3,2},{5,4},{6,5},{7,6},{9,8},{10,9},{11,10},{13,12},{... | collective-permute-start | bytes 4718600 | tf_op jit(solution)/shard_map/ppermute | solution.py:398
  284.4 40.9 %collective-permute-start.6 = (bf16[1024,768]{1,0:T(8,128)(2,1)S(1)}, bf16[1024,768]{1,0:T(8,128)(2,1)S(1)}, u32[]{:S(2)}, u32[]{:S(2)}) collective-permute-start(bf16[1024,768]{1,0:T(8,128)(2,1)S(1)} %add_convert_fusion.3), channel_id=1, source_target_pairs={{0,1},{1,2},{2,3},{4,5},{5,6},{6,7},{8,9},{9,10},{10,11},{12,13},{... | collective-permute-start | bytes 4718600 | tf_op jit(solution)/shard_map/ppermute | solution.py:397
  331.1 47.4 %all-to-all-start.2 = ((bf16[8,1,2,64,768]{4,3,2,1,0:T(8,128)(2,1)}), bf16[8,1,2,64,768]{4,3,2,1,0:T(8,128)(2,1)S(1)}, u32[]{:S(2)}, u32[]{:S(2)}) async-start(bf16[8,1,2,64,768]{4,3,2,1,0:T(8,128)(2,1)} %bitcast.20), calls=%async_computation.2 | async-start | bytes 3145728 | tf_op jit(solution)/shard_map/all_to_all | solution.py:58
  334.9 24.8 %collective-permute-start.17 = (bf16[2,64,768]{2,1,0:T(8,128)(2,1)S(1)}, bf16[2,64,768]{2,1,0:T(8,128)(2,1)S(1)}, u32[]{:S(2)}, u32[]{:S(2)}) collective-permute-start(bf16[2,64,768]{2,1,0:T(8,128)(2,1)S(1)} %get-tuple-element.30), channel_id=1, source_target_pairs={{0,8},{4,12},{8,0},{12,4},{16,24},{20,28},{24,16},{28,20},{1,9},{5... | collective-permute-start | bytes 589832 | tf_op jit(solution)/shard_map/ppermute | solution.py:35
  337.0 22.7 %collective-permute-start.18 = (bf16[2,64,768]{2,1,0:T(8,128)(2,1)S(1)}, bf16[2,64,768]{2,1,0:T(8,128)(2,1)S(1)}, u32[]{:S(2)}, u32[]{:S(2)}) collective-permute-start(bf16[2,64,768]{2,1,0:T(8,128)(2,1)S(1)} %get-tuple-element.32), channel_id=1, source_target_pairs={{0,16},{4,20},{8,24},{12,28},{16,0},{20,4},{24,8},{28,12},{1,17},{... | collective-permute-start | bytes 589832 | tf_op jit(solution)/shard_map/ppermute | solution.py:35
  338.5 25.9 %collective-permute-start.19 = (bf16[2,64,768]{2,1,0:T(8,128)(2,1)S(1)}, bf16[2,64,768]{2,1,0:T(8,128)(2,1)S(1)}, u32[]{:S(2)}, u32[]{:S(2)}) collective-permute-start(bf16[2,64,768]{2,1,0:T(8,128)(2,1)S(1)} %get-tuple-element.31), channel_id=1, source_target_pairs={{0,24},{4,28},{8,16},{12,20},{16,8},{20,12},{24,0},{28,4},{1,25},{... | collective-permute-start | bytes 589832 | tf_op jit(solution)/shard_map/ppermute | solution.py:35
  370.4 7.4 %collective-permute-start.23 = (f32[3,768]{1,0:T(4,128)S(1)}, f32[3,768]{1,0:T(4,128)S(1)}, u32[]{:S(2)}, u32[]{:S(2)}) collective-permute-start(f32[3,768]{1,0:T(4,128)S(1)} %add.134), channel_id=1, source_target_pairs={{0,16},{4,20},{8,24},{12,28},{16,0},{20,4},{24,8},{28,12},{1,17},{... | collective-permute-start | bytes 27656 | tf_op jit(solution)/shard_map/ppermute | solution.py:35
  (33 other events, 604.1 us)

commit v3 on v2

v3 whole, which is shorter than its diff:
```python
import jax
import jax.numpy as jnp
from jax import lax
from jax.experimental import pallas as pl
from jax.experimental.pallas import tpu as pltpu
from jax.sharding import PartitionSpec as P

HEAD_DIM = 128
SCALE = HEAD_DIM ** (-0.5)
LOG2E = 1.4426950408889634
BLOCK = 16
HIDDEN = -1e30
ROW_TILE = 256
VMEM = 24
COST = 1.15e9
CHUNKS = 2
BF16 = jnp.bfloat16
F32 = jnp.float32
ANY = pl.BlockSpec(memory_space=pl.ANY)
SMEM = pl.BlockSpec(memory_space=pltpu.SMEM)
LIMIT = pltpu.CompilerParams(vmem_limit_bytes=VMEM * 2**20)


def lasting(us):
    return pl.CostEstimate(flops=int(us * COST), bytes_accessed=0, transcendentals=0)


def dot(a, b):
    return lax.dot_general(a, b, (((1,), (0,)), ((), ())), preferred_element_type=F32)


def dot_nt(a, b):
    return lax.dot_general(a, b, (((1,), (1,)), ((), ())), preferred_element_type=F32)


def dot_tn(a, b):
    return lax.dot_general(a, b, (((0,), (0,)), ((), ())), preferred_element_type=F32)


def swap(value, s):
    count = lax.axis_size("frame")
    return lax.ppermute(value, "frame", [(i, i ^ s) for i in range(count)])


def collect(own, count, deps):
    pieces = [own] + [swap(own, s) for s in range(2, count, 2)]

    def kernel(*refs):
        for t in range(len(pieces)):
            refs[-1][t] = refs[t][...]

    even = pl.pallas_call(
        kernel,
        in_specs=[pl.BlockSpec(memory_space=pltpu.VMEM)] * len(pieces) + [ANY] * len(deps),
        out_specs=pl.BlockSpec(memory_space=pltpu.VMEM),
        out_shape=jax.ShapeDtypeStruct((len(pieces), *own.shape), own.dtype),
        compiler_params=LIMIT,
        cost_estimate=lasting(1.2),
    )(*pieces, *deps)
    return even, swap(even, 1)


def reduce_pieces(even, odd, deps):
    sums = after(even, *deps) + swap(odd.astype(BF16), 1).astype(F32)
    total = sums[0]
    for t in range(1, even.shape[0]):
        total = total + swap(sums[t].astype(BF16), 2 * t).astype(F32)
    return total


def to_positions(arrays, chunk, count):
    frames, spatial, channels = arrays[0].shape
    size = spatial // CHUNKS
    split = [
        lax.slice_in_dim(a, chunk * size, (chunk + 1) * size, axis=1)
        .reshape(frames, count, 1, size // count, channels)
        .transpose(1, 2, 0, 3, 4)
        for a in arrays
    ]
    return jnp.concatenate(split, axis=1)


def after(value, *others):
    return lax.optimization_barrier((value, *others))[0]


def travel(value):
    return lax.all_to_all(value, "frame", split_axis=0, concat_axis=0, tiled=True)


def to_frames(values):
    count, frames, part, channels = values[0].shape
    return jnp.concatenate(
        [v.transpose(1, 0, 2, 3).reshape(frames, count * part, channels) for v in values], axis=1
    )


def temporal_bias(rate_scale, rate_reach, starts):
    places = jnp.arange(starts.shape[0], dtype=jnp.int32)
    distance = jnp.abs(places[:, None] - places[None, :]).astype(F32)
    penalty = -rate_scale[:, None, None] * jnp.log1p(rate_reach[:, None, None] * distance[None])
    allowed = (places[:, None] <= places[None, :]) & (places[:, None] >= starts[None, :])
    return jnp.repeat(jnp.where(allowed[None], penalty * LOG2E, HIDDEN), BLOCK, axis=2)


def widen(bias):
    frames, rows = bias.shape
    wide = jnp.broadcast_to(bias[:, None, :], (frames, BLOCK, rows)).reshape(rows, rows)
    key_place = lax.broadcasted_iota(jnp.int32, (rows, rows), 0) % BLOCK
    query_place = lax.broadcasted_iota(jnp.int32, (rows, rows), 1) % BLOCK
    return jnp.where(key_place == query_place, wide, HIDDEN)


def weights_of(scores):
    raised = jnp.exp2(scores - jnp.max(scores, axis=0, keepdims=True))
    return raised, 1.0 / jnp.sum(raised, axis=0, keepdims=True)


def stacked(ref, index):
    value = ref[:, index]
    return value.reshape(value.shape[0] * value.shape[1], HEAD_DIM)


def attend(video, even, odd, bias, deps=()):
    count, _, frames, part, channels = video.shape
    tokens = even.shape[2]
    heads = channels // HEAD_DIM
    rows = count * frames * BLOCK
    number = part // BLOCK
    all_tokens = tokens * count

    def kernel(video_ref, even_ref, odd_ref, bias_ref, *rest):
        out_ref, near_ref, far_ref, inverse_ref, parts_ref = rest[-5:]
        ref_key = jnp.concatenate([stacked(even_ref, 0), stacked(odd_ref, 0)], axis=0)
        ref_value_t = jnp.concatenate([stacked(even_ref, 1), stacked(odd_ref, 1)], axis=0).T
        wide = widen(bias_ref[0])
        for b in range(number):
            at = slice(b * BLOCK, (b + 1) * BLOCK)
            query, key, value = (video_ref[:, a, :, at, :].reshape(rows, HEAD_DIM) for a in range(3))
            total = None
            for k, (scores, value_t, keep) in enumerate(
                (
                    (dot_nt(key, query) * (SCALE * LOG2E) + wide, value.T, near_ref),
                    (dot_nt(ref_key, query) * (SCALE * LOG2E), ref_value_t, far_ref),
                )
            ):
                raised, inverse = weights_of(scores)
                raised = raised.astype(BF16)
                keep[0, b] = raised
                inverse_ref[0, b, k : k + 1, :] = inverse
                term = dot(value_t, raised) * inverse
                parts_ref[0, b, k] = term.astype(BF16)
                total = term if total is None else total + term
            out_ref[:, :, at, :] = total.T.astype(BF16).reshape(count, frames, BLOCK, HEAD_DIM)

    all_rows = count * frames * part
    saved = [
        ((number, rows, rows), BF16),
        ((number, all_tokens, rows), BF16),
        ((number, 2, rows), F32),
        ((number, 2, HEAD_DIM, rows), BF16),
    ]
    return pl.pallas_call(
        kernel,
        grid=(heads,),
        in_specs=[pl.BlockSpec((count, 3, frames, part, HEAD_DIM), lambda h: (0, 0, 0, 0, h))]
        + [pl.BlockSpec((count // 2, 2, tokens, HEAD_DIM), lambda h: (0, 0, 0, h))] * 2
        + [pl.BlockSpec((1, count * frames, rows), lambda h: (h, 0, 0))]
        + [ANY] * len(deps),
        out_specs=[pl.BlockSpec((count, frames, part, HEAD_DIM), lambda h: (0, 0, 0, h))]
        + [by_head(shape) for shape, _ in saved],
        out_shape=[jax.ShapeDtypeStruct((count, frames, part, channels), BF16)]
        + [jax.ShapeDtypeStruct((heads, *shape), kind) for shape, kind in saved],
        compiler_params=LIMIT,
        cost_estimate=lasting(8),
    )(video, even, odd, bias, *deps)


def by_head(shape):
    return pl.BlockSpec((1, *shape), lambda h: (h,) + (0,) * len(shape))


def attend_back(video, even, odd, saved, grad, deps=()):
    count, _, frames, part, channels = video.shape
    tokens = even.shape[2]
    heads = channels // HEAD_DIM
    rows = count * frames * BLOCK
    half = tokens * count // 2

    def kernel(video_ref, even_ref, odd_ref, near_ref, far_ref, inverse_ref, parts_ref, grad_ref, *rest):
        out_ref, even_out, odd_out = rest[-3:]
        ref_key = jnp.concatenate([stacked(even_ref, 0), stacked(odd_ref, 0)], axis=0)
        ref_value = jnp.concatenate([stacked(even_ref, 1), stacked(odd_ref, 1)], axis=0)
        ref_key_t = ref_key.T
        sums = [None, None]
        for b in range(part // BLOCK):
            at = slice(b * BLOCK, (b + 1) * BLOCK)
            query, key, value = (video_ref[:, a, :, at, :].reshape(rows, HEAD_DIM) for a in range(3))
            grad_t = grad_ref[:, :, at, :].reshape(rows, HEAD_DIM).T.astype(F32)
            results = []
            for k, (raised, keys_t, values) in enumerate(
                ((near_ref[0, b], key.T, value), (far_ref[0, b], ref_key_t, ref_value))
            ):
                inverse = inverse_ref[0, b, k : k + 1, :]
                scaled_t = (grad_t * inverse).astype(BF16)
                centre = jnp.sum(grad_t * parts_ref[0, b, k].astype(F32), axis=0, keepdims=True) * inverse
                slopes = raised * (dot(values, scaled_t) - centre).astype(BF16)
                results.append((dot(keys_t, slopes), dot(slopes, query), dot_nt(raised, scaled_t)))
            near, far = results
            for a in range(2):
                sums[a] = far[a + 1] if sums[a] is None else sums[a] + far[a + 1]
            outs = ((near[0] + far[0]).T * SCALE, near[1] * SCALE, near[2])
            for a, result in enumerate(outs):
                out_ref[:, a, :, at, :] = result.astype(BF16).reshape(count, frames, BLOCK, HEAD_DIM)
        sums[0] = sums[0] * SCALE
        for a in range(2):
            even_out[:, a] = sums[a][:half].reshape(count // 2, tokens, HEAD_DIM)
            odd_out[:, a] = sums[a][half:].reshape(count // 2, tokens, HEAD_DIM)

    all_rows = count * frames * part
    video_spec = pl.BlockSpec((count, 3, frames, part, HEAD_DIM), lambda h: (0, 0, 0, 0, h))
    ref_specs = [pl.BlockSpec((count // 2, 2, tokens, HEAD_DIM), lambda h: (0, 0, 0, h))] * 2
    out_ref_specs = [pl.BlockSpec((count // 2, 2, tokens, HEAD_DIM), lambda h: (0, 0, 0, h))] * 2
    return pl.pallas_call(
        kernel,
        grid=(heads,),
        in_specs=[video_spec, *ref_specs]
        + [by_head(array.shape[1:]) for array in saved]
        + [pl.BlockSpec((count, frames, part, HEAD_DIM), lambda h: (0, 0, 0, h))]
        + [ANY] * len(deps),
        out_specs=[video_spec, *out_ref_specs],
        out_shape=[jax.ShapeDtypeStruct(video.shape, BF16)]
        + [jax.ShapeDtypeStruct((*even.shape[:3], channels), F32)] * 2,
        compiler_params=LIMIT,
        cost_estimate=lasting(10),
    )(video, even, odd, *saved, grad, *deps)


def mix_back(cot, taps):
    full, held, channels = cot.shape
    reach = taps.shape[0]

    def kernel(taps_ref, cot_ref, out_ref):
        line = [cot_ref[f].astype(F32) for f in range(full)]
        for f in range(full):
            total = taps_ref[0:1, :] * line[f]
            for k in range(1, min(reach, full - f)):
                total = total + taps_ref[k : k + 1, :] * line[f + k]
            out_ref[f] = total.astype(BF16)

    block = pl.BlockSpec((full, held, HEAD_DIM), lambda h: (0, 0, h))
    return pl.pallas_call(
        kernel,
        grid=(channels // HEAD_DIM,),
        in_specs=[pl.BlockSpec((reach, HEAD_DIM), lambda h: (0, h)), block],
        out_specs=block,
        out_shape=jax.ShapeDtypeStruct(cot.shape, BF16),
        compiler_params=LIMIT,
        cost_estimate=lasting(1.5),
    )(taps, cot)


def mix(mixed, cot, taps, count, deps=()):
    full, part, channels = cot.shape
    reach = taps.shape[0]
    frames = full // count
    extra = -(-2 * reach // 16) * 16

    def kernel(taps_ref, mixed_ref, cot_ref, *rest):
        out_ref = rest[-1]
        line = []
        sums = [jnp.zeros((part, HEAD_DIM), F32) for _ in range(reach)]
        for f in range(full):
            line.append(mixed_ref[f].astype(F32))
            cot_line = cot_ref[f].astype(F32)
            total = jnp.zeros((part, HEAD_DIM), F32)
            for k in range(min(reach, f + 1)):
                total = total + taps_ref[k : k + 1, :] * line[f - k]
                sums[k] = sums[k] + cot_line * line[f - k]
            d, u = f // frames, f % frames
            out_ref[d, u * part : (u + 1) * part] = total.astype(BF16)
        sums = jnp.concatenate([jnp.sum(s, axis=0, keepdims=True) for s in sums], axis=0)
        high = sums.astype(BF16).astype(F32)
        zeros = jnp.zeros((extra - 2 * reach, HEAD_DIM), F32)
        rows = jnp.concatenate([high, sums - high, zeros], axis=0).astype(BF16)
        for d in range(count):
            out_ref[d, frames * part :] = rows

    block = pl.BlockSpec((full, part, HEAD_DIM), lambda h: (0, 0, h))
    return pl.pallas_call(
        kernel,
        grid=(channels // HEAD_DIM,),
        in_specs=[pl.BlockSpec((reach, HEAD_DIM), lambda h: (0, h)), block, block] + [ANY] * len(deps),
        out_specs=pl.BlockSpec((count, frames * part + extra, HEAD_DIM), lambda h: (0, 0, h)),
        out_shape=jax.ShapeDtypeStruct((count, frames * part + extra, channels), BF16),
        compiler_params=LIMIT,
        cost_estimate=lasting(3),
    )(taps, mixed, cot, *deps)


def project(attended, weight, deps=()):
    rows, channels = attended.shape
    depth = lax.axis_size("head")

    def kernel(attended_ref, weight_ref, *rest):
        for start in range(0, rows, ROW_TILE):
            at = slice(start, start + ROW_TILE)
            rest[-1][0, at] = dot(attended_ref[at], weight_ref[...]).astype(BF16)

    return pl.pallas_call(
        kernel,
        grid=(depth,),
        in_specs=[
            pl.BlockSpec((rows, channels), lambda j: (0, 0)),
            pl.BlockSpec((channels, channels), lambda j: (0, j)),
        ]
        + [ANY] * len(deps),
        out_specs=pl.BlockSpec((1, rows, channels), lambda j: (j, 0, 0)),
        out_shape=jax.ShapeDtypeStruct((depth, rows, channels), BF16),
        compiler_params=LIMIT,
        cost_estimate=lasting(4),
    )(attended, weight, *deps)


def project_back(blocks, weight, deps=()):
    depth, rows, channels = blocks.shape

    def kernel(blocks_ref, weight_ref, *rest):
        out_ref, total = rest[-2:]
        j = pl.program_id(0)
        for start in range(0, rows, ROW_TILE):
            at = slice(start, start + ROW_TILE)
            term = dot_nt(blocks_ref[0, at], weight_ref[...])

            @pl.when(j == 0)
            def _():
                total[at] = term

            @pl.when((j > 0) & (j < depth - 1))
            def _():
                total[at] += term

            @pl.when(j == depth - 1)
            def _():
                out_ref[at] = (total[at] + term).astype(BF16)

    return pl.pallas_call(
        kernel,
        grid=(depth,),
        in_specs=[
            pl.BlockSpec((1, rows, channels), lambda j: (j, 0, 0)),
            pl.BlockSpec((channels, channels), lambda j: (0, j)),
        ]
        + [ANY] * len(deps),
        out_specs=pl.BlockSpec((rows, channels), lambda j: (0, 0)),
        out_shape=jax.ShapeDtypeStruct((rows, channels), BF16),
        scratch_shapes=[pltpu.VMEM((rows, channels), F32)],
        compiler_params=LIMIT,
        cost_estimate=lasting(6),
    )(blocks, weight, *deps)


def weight_terms(attended, blocks, count, deps=()):
    chunks = len(attended)
    depth, rows, channels = blocks[0].shape
    parts = count // depth
    columns = channels // parts

    def kernel(*refs):
        out_ref, turned = refs[-2:]

        @pl.when(pl.program_id(0) == 0)
        def _():
            for c in range(chunks):
                turned[c] = refs[c][...].T

        total = None
        for c in range(chunks):
            term = dot(turned[c], refs[chunks + c][0])
            total = term if total is None else total + term
        for p in range(parts):
            out_ref[0, p] = total[:, p * columns : (p + 1) * columns].astype(BF16)

    return pl.pallas_call(
        kernel,
        grid=(depth,),
        in_specs=[pl.BlockSpec((rows, channels), lambda j: (0, 0))] * chunks
        + [pl.BlockSpec((1, rows, channels), lambda j: (j, 0, 0))] * chunks
        + [ANY] * len(deps),
        out_specs=pl.BlockSpec((1, parts, channels, columns), lambda j: (j, 0, 0, 0)),
        out_shape=jax.ShapeDtypeStruct((depth, parts, channels, columns), BF16),
        scratch_shapes=[pltpu.VMEM((chunks, channels, rows), BF16)],
        compiler_params=LIMIT,
        cost_estimate=lasting(7),
    )(*attended, *blocks, *deps)


def core_sums(terms, near, core, deps=()):
    chips, _, channels, columns = terms.shape

    def kernel(core_ref, terms_ref, near_ref, *rest):
        rest[-1][...] = (terms_ref[:, 0].astype(F32) + near_ref[...].astype(F32)).astype(BF16)

    block = pl.BlockSpec((1, channels, columns), lambda i, core: (i, 0, 0))
    return pl.pallas_call(
        kernel,
        grid_spec=pltpu.PrefetchScalarGridSpec(
            num_scalar_prefetch=1,
            grid=(chips,),
            in_specs=[pl.BlockSpec((1, 1, channels, columns), lambda i, core: (i, core[0], 0, 0)), block]
            + [ANY] * len(deps),
            out_specs=block,
        ),
        out_shape=jax.ShapeDtypeStruct((chips, channels, columns), BF16),
        compiler_params=LIMIT,
        cost_estimate=lasting(2.6),
    )(core.reshape(1).astype(jnp.int32), terms, near, *deps)


def per_device(
    queries,
    keys,
    values,
    ref_keys,
    ref_values,
    rate_scale,
    rate_reach,
    window_start,
    out_weight,
    conv_taps,
    cotangent,
):
    frames, spatial, channels = queries.shape
    count, depth = lax.axis_size("frame"), lax.axis_size("head")
    place = lax.axis_index("frame")
    part = spatial // count // CHUNKS
    rows = count * frames * part
    reach = conv_taps.shape[0]
    line = (count * frames, part, channels)

    cot, own, blocks = [], [], []
    for c in range(CHUNKS):
        packed = to_positions([cotangent], c, count)
        cot.append(travel(packed if c == 0 else after(packed, own[-1])).reshape(line))
        own.append(mix_back(cot[c], conv_taps))
        blocks.append(lax.all_gather(own[c].reshape(rows, channels), "head", axis=0))

    even, odd = collect(after(jnp.stack([ref_keys, ref_values]), own[0]), count, [own[-1]])
    bias = temporal_bias(rate_scale, rate_reach, window_start)

    video, before = [], even
    for c in range(CHUNKS):
        packed = to_positions([queries, keys, values], c, count)
        video.append(travel(after(packed, before)))
        before = video[-1]

    last = []
    attended, saved, mixed, back, finals = [], [], [], [], []

    def forward(c):
        nonlocal last
        out, *kept = attend(video[c], even, odd, bias, last)
        attended.append(out.reshape(rows, channels))
        saved.append(kept)
        shares = project(attended[c], out_weight)
        mixed.append(lax.psum_scatter(shares, "head", scatter_dimension=0, tiled=False))
        last = [shares]

    def pull(c):
        nonlocal last
        grad = project_back(blocks[c], out_weight, last)
        last = [grad]
        return grad.reshape(count, frames, part, channels)

    def backward(c, grad):
        nonlocal last
        results = attend_back(video[c], even, odd, saved[c], grad, last)
        last = [results[1]]
        back.append((travel(results[0]), results[1], results[2]))

    def finish(c):
        nonlocal last
        final = mix(mixed[c].reshape(line), cot[c], conv_taps, count, last)
        last = [final]
        return final

    forward(0)
    backward(0, pull(0))
    for c in range(1, CHUNKS):
        forward(c)

    last = [*last, back[0][0]]
    terms = weight_terms(attended, blocks, count, last)
    last = [terms]
    by_chip = terms.reshape(count // 2, 2, channels, terms.shape[3])
    core = place % 2
    near = swap(lax.dynamic_index_in_dim(by_chip, 1 - core, 1, keepdims=False), 1)
    grads = [pull(c) for c in range(1, CHUNKS)]
    sums = core_sums(by_chip, near, core, last)
    last = [sums]
    groups = [list(range(k, count, 2)) for k in range(2)]
    far = lax.all_to_all(sums, "frame", split_axis=0, concat_axis=0, axis_index_groups=groups, tiled=True)
    for c in range(1, CHUNKS):
        backward(c, grads[c - 1])

    last = [*last, far]
    for c in range(CHUNKS):
        finals.append(travel(finish(c)))
        last = [*last, back[c][0]] if c == 0 else last
    ref_even, ref_odd = (sum(b[k] for b in back) for k in (1, 2))
    ref_grads = reduce_pieces(ref_even, ref_odd, last)
    grad_weight = jnp.sum(far.astype(F32), axis=0)

    grads = [to_frames([b[0][:, a] for b in back]) for a in range(3)]
    held_rows = frames * part
    out = to_frames([f[:, :held_rows].reshape(count, frames, part, channels) for f in finals])
    taps_parts = jnp.sum(sum(f[:, held_rows : held_rows + 2 * reach].astype(F32) for f in finals), axis=0)
    taps_sum = taps_parts[:reach] + taps_parts[reach:]
    return (out, *grads, ref_grads[0], ref_grads[1], grad_weight, taps_sum)


def solution(mesh):
    video = P("frame", None, "head")
    tokens = P("frame", "head")
    return jax.shard_map(
        per_device,
        mesh=mesh,
        in_specs=(
            video,
            video,
            video,
            tokens,
            tokens,
            P("head"),
            P("head"),
            P(),
            P("head", None),
            P(None, "head"),
            video,
        ),
        out_specs=(video, video, video, video, tokens, tokens, P("head", "frame"), P(None, "head")),
        check_vma=False,
    )
```

time: 382 us -> 333 us (0.87)
  waiting for transfers between devices: 160 us -> 67.7 us
  local copies, waits for them, and re-layouts: 22.4 us -> 85.6 us
  matrix products: 29.3 us -> 0 us
  starting transfers between devices: 59.8 us -> 35.5 us
  Pallas kernels: 58.8 us -> 74.9 us
  between operations: 1.22 us -> 14.4 us
  blocking collectives: 25.9 us -> 32.5 us
    ppermute x12 -> x0, waiting for transfers between devices: 124 us -> none  [the longest x3 59.9 us: per_device(): up = lax.ppermute(send_up, 'head', [(i, i + 1) for i in range(depth - far)])]
    unnamed x58 -> x142, local copies, waits for them, and re-layouts: 3.74 us -> 69 us
    all_to_all x3 -> x6, waiting for transfers between devices: 0.01 us -> 46.6 us  [travel(): lax.all_to_all(value, 'frame', split_axis=0, concat_axis=0, tiled=True)]
    ppermute x12 -> x0, starting transfers between devices: 33.5 us -> none  [the longest x3 17.2 us: per_device(): up = lax.ppermute(send_up, 'head', [(i, i + 1) for i in range(depth - far)])]
    ppermute x12 -> x9, waiting for transfers between devices: 36.2 us -> 5.18 us  [swap(): return lax.ppermute(value, 'frame', [(i, i ^ s) for i in range(count)])]
    dot_general x6 -> x0, matrix products: 29.3 us -> none  [the longest x5 22 us: dot_nt(): lax.dot_general(a, b, (((1,), (1,)), ((), ())), preferred_element_type=F32)]
    reduce_scatter x0 -> x2, waiting for transfers between devices: none -> 14.2 us  [forward(): lax.psum_scatter(shares, 'head', scatter_dimension=0, tiled=False)]
    pallas_call x3 -> x11, Pallas kernels: 41.4 us -> 53.5 us  [the longest x2 22.1 us: attend_back(): pl.pallas_call(kernel, grid=(heads,), in_specs=[video_spec, *ref_specs] +...]
  transfers between devices with their start and end apart: 28 -> 20, of which waited for: 13 -> 9; matrix products, arithmetic and copies ran while one was open for 17% -> 10% of each run, Pallas kernels for 13% -> 22%
where the time goes in v3:
time: 333 us; the launch traced here: 330 us
  local copies, waits for them, and re-layouts  85.6 us (26%)
  Pallas kernels  74.9 us (22%)
  waiting for transfers between devices  67.7 us (20%)
  starting transfers between devices  35.5 us (11%)
  blocking collectives  32.5 us (10%)
  other arithmetic  19.7 us (6%)
  between operations  14.4 us (4%)
    unnamed x142, local copies, waits for them, and re-layouts  69 us
    all_to_all x6, waiting for transfers between devices, travel(): lax.all_to_all(value, 'frame', split_axis=0, concat_axis=0, tiled=True)  46.6 us
    all_to_all x2, blocking collectives, travel(): lax.all_to_all(value, 'frame', split_axis=0, concat_axis=0, tiled=True)  32.5 us
    all_to_all x6, starting transfers between devices, travel(): lax.all_to_all(value, 'frame', split_axis=0, concat_axis=0, tiled=True)  22.7 us
    pallas_call x2, Pallas kernels, attend_back(): pl.pallas_call(kernel, grid=(heads,), in_specs=[video_spec, *ref_specs] +...  22.1 us
    pallas_call x2, Pallas kernels, attend(): pl.pallas_call(kernel, grid=(heads,), in_specs=[pl.BlockSpec((count, 3, f...  16.7 us
    reduce_scatter x2, waiting for transfers between devices, forward(): lax.psum_scatter(shares, 'head', scatter_dimension=0, tiled=False)  14.2 us
    pallas_call x2, Pallas kernels, project_back(): pl.pallas_call(kernel, grid=(depth,), in_specs=[pl.BlockSpec((1, rows, ch...  11.4 us
  transfers between devices with their start and end apart: 20, of which 9 were waited for; matrix products, arithmetic and copies ran while one was open for 10% of the time, Pallas kernels for 22%

profile of v3, /device:TPU:0, one launch (start us, length us, event | category | flops | bytes accessed | tf_op | source)
XLA Modules:
  0.0 330.4 jit_solution(16477104082908634073)
XLA Ops:
  8.8 17.5 %all_to_all.45 = bf16[8,1,2,32,768]{4,3,2,1,0:T(8,128)(2,1)S(1)} all-to-all(bf16[8,1,2,32,768]{4,3,2,1,0:T(8,128)(2,1)S(1)} %copy.56), channel_id=1, replica_groups=mesh['frame'=8,'head'=4] {'frame'}, dimensions={0} | all-to-all | bytes 1572864 | tf_op jit(solution)/shard_map/all_to_all | solution.py:88
  28.8 15.0 %all_to_all.46 = bf16[8,1,2,32,768]{4,3,2,1,0:T(8,128)(2,1)S(1)} all-to-all(bf16[8,1,2,32,768]{4,3,2,1,0:T(8,128)(2,1)S(1)} %copy.57), channel_id=1, replica_groups=mesh['frame'=8,'head'=4] {'frame'}, dimensions={0} | all-to-all | bytes 1572864 | tf_op jit(solution)/shard_map/all_to_all | solution.py:88
  61.5 3.7 %all-to-all-start.2 = ((bf16[8,3,2,32,768]{4,3,2,1,0:T(8,128)(2,1)}), bf16[8,3,2,32,768]{4,3,2,1,0:T(8,128)(2,1)S(1)}, u32[]{:S(2)}, u32[]{:S(2)}) async-start(bf16[8,3,2,32,768]{4,3,2,1,0:T(8,128)(2,1)} %pad_maximum_fusion), calls=%async_computation.2 | async-start | bytes 4718592 | tf_op jit(solution)/shard_map/all_to_all | solution.py:88
  68.4 26.2 %all-to-all-done.2.video_ref = bf16[8,3,2,32,768]{4,3,2,1,0:T(8,128)(2,1)S(1)} async-done(((bf16[8,3,2,32,768]{4,3,2,1,0:T(8,128)(2,1)}), bf16[8,3,2,32,768]{4,3,2,1,0:T(8,128)(2,1)S(1)}, u32[]{:S(2)}, u32[]{:S(2)}) %all-to-all-start.2) | async-done | bytes 2359328 | tf_op jit(solution)/shard_map/all_to_all | solution.py:88
  95.8 8.4 %shard_map.173 = (bf16[8,2,32,768]{3,2,1,0:T(8,128)(2,1)S(1)}, bf16[6,2,256,256]{3,2,1,0:T(8,128)(2,1)S(1)}, bf16[6,2,512,256]{3,2,1,0:T(8,128)(2,1)S(1)}, f32[6...) custom-call(bf16[8,3,2,32,768]{4,3,2,1,0:T(8,128)(2,1)S(1)} %all-to-all-done.2.video_ref, ...), custom_call_target="tpu_custom_call" | custom-call | flops 9200000000 | tf_op jit(solution)/shard_map/pallas_call | solution.py:163
  110.6 4.4 %shard_map.174.rest_0_ = bf16[4,512,768]{2,1,0:T(8,128)(2,1)} custom-call(bf16[512,768]{1,0:T(8,128)(2,1)S(1)} %bitcast.105, bf16[768,3072]{1,0:T(8,128)(2,1)S(1)} %copy-done.23), custom_call_target="tpu_custom_call" | custom-call | flops 4600000000 | tf_op jit(solution)/shard_map/pallas_call | solution.py:310
  119.2 3.6 %all-to-all-start.3 = ((bf16[8,3,2,32,768]{4,3,2,1,0:T(8,128)(2,1)}), bf16[8,3,2,32,768]{4,3,2,1,0:T(8,128)(2,1)S(1)}, u32[]{:S(2)}, u32[]{:S(2)}) async-start(bf16[8,3,2,32,768]{4,3,2,1,0:T(8,128)(2,1)} %pad_maximum_fusion.1), calls=%async_computation.4 | async-start | bytes 4718592 | tf_op jit(solution)/shard_map/all_to_all | solution.py:88
  127.2 5.7 %shard_map.175.rest_0_ = bf16[512,768]{1,0:T(8,128)(2,1)S(1)} custom-call(bf16[4,512,768]{2,1,0:T(8,128)(2,1)S(1)} %copy-done.27, bf16[768,3072]{1,0:T(8,128)(2,1)S(1)} %copy-done.24, bf16[4,512,768]{2,1,0:T(8,128)(2,1)} %shard_map.174.rest_0_), custom_call_target="tpu_custom_call" | custom-call | flops 6899999744 | tf_op jit(solution)/shard_map/pallas_call | solution.py:347
  132.9 11.1 %shard_map.176 = (bf16[8,3,2,32,768]{4,3,2,1,0:T(8,128)(2,1)S(1)}, f32[4,2,64,768]{3,2,1,0:T(8,128)S(1)}, f32[4,2,64,768]{3,2,1,0:T(8,128)S(1)}) custom-call(bf16[8,3,2,32,768]{4,3,2,1,0:T(8,128)(2,1)S(1)} %copy-done.7, bf16[4,2,64,768]{3,2,1,0:T(8,128)(2,1)S(1)} %copy-done.34, bf16[4,2,64,768]{3,2,1,0:T(8,128)(2,1)} %collective-permute-done.3.odd_ref, ...), custom_call_target="tpu_custom_call" | custom-call | flops 11500000256 | tf_op jit(solution)/shard_map/pallas_call | solution.py:224
  147.7 4.5 %all-to-all-done.3.video_ref = bf16[8,3,2,32,768]{4,3,2,1,0:T(8,128)(2,1)S(1)} async-done(((bf16[8,3,2,32,768]{4,3,2,1,0:T(8,128)(2,1)}), bf16[8,3,2,32,768]{4,3,2,1,0:T(8,128)(2,1)S(1)}, u32[]{:S(2)}, u32[]{:S(2)}) %all-to-all-start.3) | async-done | bytes 2359328 | tf_op jit(solution)/shard_map/all_to_all | solution.py:88
  153.7 3.6 %all-to-all-start.4 = ((bf16[8,3,2,32,768]{4,3,2,1,0:T(8,128)(2,1)}), bf16[8,3,2,32,768]{4,3,2,1,0:T(8,128)(2,1)S(1)}, u32[]{:S(2)}, u32[]{:S(2)}) async-start(bf16[8,3,2,32,768]{4,3,2,1,0:T(8,128)(2,1)} %copy-done.5), calls=%async_computation.5 | async-start | bytes 4718592 | tf_op jit(solution)/shard_map/all_to_all | solution.py:88
  161.8 8.3 %shard_map.177 = (bf16[8,2,32,768]{3,2,1,0:T(8,128)(2,1)S(1)}, bf16[6,2,256,256]{3,2,1,0:T(8,128)(2,1)S(1)}, bf16[6,2,512,256]{3,2,1,0:T(8,128)(2,1)S(1)}, f32[6...) custom-call(bf16[8,3,2,32,768]{4,3,2,1,0:T(8,128)(2,1)S(1)} %copy-done.3, bf16[4,2,64,768]{3,2,1,0:T(8,128)(2,1)S(1)} %copy-done.35, ...), custom_call_target="tpu_custom_call" | custom-call | flops 9200000000 | tf_op jit(solution)/shard_map/pallas_call | solution.py:163
  176.3 3.5 %shard_map.178.refs_4_ = bf16[4,512,768]{2,1,0:T(8,128)(2,1)S(1)} custom-call(bf16[512,768]{1,0:T(8,128)(2,1)S(1)} %bitcast.107, bf16[768,3072]{1,0:T(8,128)(2,1)S(1)} %copy-done.25), custom_call_target="tpu_custom_call" | custom-call | flops 4600000000 | tf_op jit(solution)/shard_map/pallas_call | solution.py:310
  182.5 4.2 %all-to-all-done.4.refs_5_.rest_1_ = bf16[8,3,2,32,768]{4,3,2,1,0:T(8,128)(2,1)S(1)} async-done(((bf16[8,3,2,32,768]{4,3,2,1,0:T(8,128)(2,1)}), bf16[8,3,2,32,768]{4,3,2,1,0:T(8,128)(2,1)S(1)}, u32[]{:S(2)}, u32[]{:S(2)}) %all-to-all-start.4) | async-done | bytes 2359328 | tf_op jit(solution)/shard_map/all_to_all | solution.py:88
  194.7 6.0 %shard_map.179.rest_0_.terms_ref = bf16[4,2,768,384]{3,2,1,0:T(8,128)(2,1)S(1)} custom-call(bf16[512,768]{1,0:T(8,128)(2,1)S(1)} %bitcast.106, bf16[512,768]{1,0:T(8,128)(2,1)S(1)} %bitcast.108, bf16[4,512,768]{2,1,0:T(8,128)(2,1)S(1)} %copy-done.28, bf16[4,512,768]{2,1,0:T(8,128)(2,1)S(1)} %copy-done.29, bf16[4,512,768]{2,1,0:T(8,128)(2,1)S(1)} %copy-done.1, ...), custom_call_target="tpu_custom_call" | custom-call | flops 8049999872 | tf_op jit(solution)/shard_map/pallas_call | solution.py:384
  205.0 5.7 %shard_map.180.rest_0_ = bf16[512,768]{1,0:T(8,128)(2,1)S(1)} custom-call(bf16[4,512,768]{2,1,0:T(8,128)(2,1)S(1)} %copy-done.30, bf16[768,3072]{1,0:T(8,128)(2,1)S(1)} %copy-done.26, bf16[4,2,768,384]{3,2,1,0:T(8,128)(2,1)S(1)} %shard_map.179.rest_0_.terms_ref), custom_call_target="tpu_custom_call" | custom-call | flops 6899999744 | tf_op jit(solution)/shard_map/pallas_call | solution.py:347
  213.7 4.5 %all-to-all-start.5 = ((bf16[4,768,384]{2,1,0:T(8,128)(2,1)}), bf16[4,768,384]{2,1,0:T(8,128)(2,1)}, u32[]{:S(2)}, u32[]{:S(2)}) async-start(bf16[4,768,384]{2,1,0:T(8,128)(2,1)} %copy-done.9), calls=%async_computation.6 | async-start | bytes 4718592 | tf_op jit(solution)/shard_map/all_to_all | solution.py:502
  229.1 11.0 %shard_map.182 = (bf16[8,3,2,32,768]{4,3,2,1,0:T(8,128)(2,1)S(1)}, f32[4,2,64,768]{3,2,1,0:T(8,128)S(1)}, f32[4,2,64,768]{3,2,1,0:T(8,128)S(1)}) custom-call(bf16[8,3,2,32,768]{4,3,2,1,0:T(8,128)(2,1)S(1)} %copy-done.4, bf16[4,2,64,768]{3,2,1,0:T(8,128)(2,1)S(1)} %copy-done.36, bf16[4,2,64,768]{3,2,1,0:T(8,128)(2,1)} %collective-permute-done.3.odd_ref, ...), custom_call_target="tpu_custom_call" | custom-call | flops 11500000256 | tf_op jit(solution)/shard_map/pallas_call | solution.py:224
  245.4 4.4 %all-to-all-start.8 = ((bf16[8,3,2,32,768]{4,3,2,1,0:T(8,128)(2,1)}), bf16[8,3,2,32,768]{4,3,2,1,0:T(8,128)(2,1)}, u32[]{:S(2)}, u32[]{:S(2)}) async-start(bf16[8,3,2,32,768]{4,3,2,1,0:T(8,128)(2,1)} %copy-done.8), calls=%async_computation.10 | async-start | bytes 4718592 | tf_op jit(solution)/shard_map/all_to_all | solution.py:88
  265.0 14.2 %reduce-scatter.5.cloned.1.call-done = bf16[1,512,768]{2,1,0:T(8,128)(2,1)} async-done(((bf16[4,512,768]{2,1,0:T(8,128)(2,1)}), bf16[1,512,768]{2,1,0:T(8,128)(2,1)}) %reduce-scatter.5.cloned.1.call-update) | async-done | bytes 786448 | tf_op jit(solution)/shard_map/reduce_scatter | solution.py:466
  284.3 3.8 %all-to-all-start.6 = ((bf16[8,80,768]{2,1,0:T(8,128)(2,1)}), bf16[8,80,768]{2,1,0:T(8,128)(2,1)S(1)}, u32[]{:S(2)}, u32[]{:S(2)}) async-start(bf16[8,80,768]{2,1,0:T(8,128)(2,1)} %shard_map.183.rest_0_), calls=%async_computation.7 | async-start | bytes 1966080 | tf_op jit(solution)/shard_map/all_to_all | solution.py:88
  297.9 5.4 %all-to-all-done.6 = bf16[8,80,768]{2,1,0:T(8,128)(2,1)S(1)} async-done(((bf16[8,80,768]{2,1,0:T(8,128)(2,1)}), bf16[8,80,768]{2,1,0:T(8,128)(2,1)S(1)}, u32[]{:S(2)}, u32[]{:S(2)}) %all-to-all-start.6) | async-done | bytes 983072 | tf_op jit(solution)/shard_map/all_to_all | solution.py:88
  303.3 3.6 %all-to-all-start.7 = ((bf16[8,80,768]{2,1,0:T(8,128)(2,1)}), bf16[8,80,768]{2,1,0:T(8,128)(2,1)S(1)}, u32[]{:S(2)}, u32[]{:S(2)}) async-start(bf16[8,80,768]{2,1,0:T(8,128)(2,1)} %shard_map.184), calls=%async_computation.9 | async-start | bytes 1966080 | tf_op jit(solution)/shard_map/all_to_all | solution.py:88
  315.6 6.2 %all-to-all-done.7 = bf16[8,80,768]{2,1,0:T(8,128)(2,1)S(1)} async-done(((bf16[8,80,768]{2,1,0:T(8,128)(2,1)}), bf16[8,80,768]{2,1,0:T(8,128)(2,1)S(1)}, u32[]{:S(2)}, u32[]{:S(2)}) %all-to-all-start.7) | async-done | bytes 983072 | tf_op jit(solution)/shard_map/all_to_all | solution.py:88
  (224 shorter events, 131.4 us)
Async XLA Ops:
  7.2 115.7 %all-gather.3.cloned.1.call-start = ((), (), s32[]{:S(2)}) async-start(), calls=%async_computation.12 | async-start | bytes 3932160 | tf_op jit(solution)/shard_map/all_gather | solution.py:446
  8.7 17.6 %copy-start.38 = (f32[3,768]{1,0:T(4,128)S(1)}, f32[3,768]{1,0:T(4,128)}, u32[]{:S(2)}) copy-start(f32[3,768]{1,0:T(4,128)} %taps_ref.7) | copy-start | bytes 27652
  28.7 153.8 %all-gather.5.cloned.1.call-start = ((), (), s32[]{:S(2)}) async-start(), calls=%async_computation.13 | async-start | bytes 3932160 | tf_op jit(solution)/shard_map/all_gather | solution.py:446
  49.1 7.9 %collective-permute-start = (bf16[2,64,768]{2,1,0:T(8,128)(2,1)S(1)}, bf16[2,64,768]{2,1,0:T(8,128)(2,1)S(1)}, u32[]{:S(2)}, u32[]{:S(2)}) collective-permute-start(bf16[2,64,768]{2,1,0:T(8,128)(2,1)S(1)} %pad_maximum_fusion.6.refs_0_), channel_id=1, source_target_pairs={{0,8},{4,12},{8,0},{12,4},{16,24},{20,28},{24,16},{28,20},{1,9},{5... | collective-permute-start | bytes 589832 | tf_op jit(solution)/shard_map/ppermute | solution.py:42
  49.7 10.8 %collective-permute-start.1 = (bf16[2,64,768]{2,1,0:T(8,128)(2,1)S(1)}, bf16[2,64,768]{2,1,0:T(8,128)(2,1)S(1)}, u32[]{:S(2)}, u32[]{:S(2)}) collective-permute-start(bf16[2,64,768]{2,1,0:T(8,128)(2,1)S(1)} %pad_maximum_fusion.6.refs_0_), channel_id=1, source_target_pairs={{0,16},{4,20},{8,24},{12,28},{16,0},{20,4},{24,8},{28,12},{1,17},{... | collective-permute-start | bytes 589832 | tf_op jit(solution)/shard_map/ppermute | solution.py:42
  50.3 10.2 %collective-permute-start.2 = (bf16[2,64,768]{2,1,0:T(8,128)(2,1)S(1)}, bf16[2,64,768]{2,1,0:T(8,128)(2,1)S(1)}, u32[]{:S(2)}, u32[]{:S(2)}) collective-permute-start(bf16[2,64,768]{2,1,0:T(8,128)(2,1)S(1)} %pad_maximum_fusion.6.refs_0_), channel_id=1, source_target_pairs={{0,24},{4,28},{8,16},{12,20},{16,8},{20,12},{24,0},{28,4},{1,25},{... | collective-permute-start | bytes 589832 | tf_op jit(solution)/shard_map/ppermute | solution.py:42
  61.5 33.1 %all-to-all-start.2 = ((bf16[8,3,2,32,768]{4,3,2,1,0:T(8,128)(2,1)}), bf16[8,3,2,32,768]{4,3,2,1,0:T(8,128)(2,1)S(1)}, u32[]{:S(2)}, u32[]{:S(2)}) async-start(bf16[8,3,2,32,768]{4,3,2,1,0:T(8,128)(2,1)} %pad_maximum_fusion), calls=%async_computation.2 | async-start | bytes 4718592 | tf_op jit(solution)/shard_map/all_to_all | solution.py:88
  65.2 194.6 %reduce-scatter.3.cloned.1.call-start = ((), (), s32[]{:S(2)}) async-start(), calls=%async_computation.11 | async-start | bytes 3932160 | tf_op jit(solution)/shard_map/reduce_scatter | solution.py:466
  65.3 3.1 collective-permute-start.3
  95.8 8.4 %copy-start.6 = (bf16[8,3,2,32,768]{4,3,2,1,0:T(8,128)(2,1)}, bf16[8,3,2,32,768]{4,3,2,1,0:T(8,128)(2,1)S(1)}, u32[]{:S(2)}) copy-start(bf16[8,3,2,32,768]{4,3,2,1,0:T(8,128)(2,1)S(1)} %all-to-all-done.2.video_ref) | copy-start | bytes 7077892
  119.2 33.0 %all-to-all-start.3 = ((bf16[8,3,2,32,768]{4,3,2,1,0:T(8,128)(2,1)}), bf16[8,3,2,32,768]{4,3,2,1,0:T(8,128)(2,1)S(1)}, u32[]{:S(2)}, u32[]{:S(2)}) async-start(bf16[8,3,2,32,768]{4,3,2,1,0:T(8,128)(2,1)} %pad_maximum_fusion.1), calls=%async_computation.4 | async-start | bytes 4718592 | tf_op jit(solution)/shard_map/all_to_all | solution.py:88
  127.2 5.7 %copy-start.54 = (bf16[6,2,256,256]{3,2,1,0:T(8,128)(2,1)S(1)}, bf16[6,2,256,256]{3,2,1,0:T(8,128)(2,1)}, u32[]{:S(2)}) copy-start(bf16[6,2,256,256]{3,2,1,0:T(8,128)(2,1)} %copy-done.53) | copy-start | bytes 4718596
  127.2 5.8 %copy-start.56 = (bf16[6,2,2,128,256]{4,3,2,1,0:T(8,128)(2,1)S(1)}, bf16[6,2,2,128,256]{4,3,2,1,0:T(8,128)(2,1)}, u32[]{:S(2)}) copy-start(bf16[6,2,2,128,256]{4,3,2,1,0:T(8,128)(2,1)} %copy-done.55) | copy-start | bytes 4718596
  153.7 33.0 %all-to-all-start.4 = ((bf16[8,3,2,32,768]{4,3,2,1,0:T(8,128)(2,1)}), bf16[8,3,2,32,768]{4,3,2,1,0:T(8,128)(2,1)S(1)}, u32[]{:S(2)}, u32[]{:S(2)}) async-start(bf16[8,3,2,32,768]{4,3,2,1,0:T(8,128)(2,1)} %copy-done.5), calls=%async_computation.5 | async-start | bytes 4718592 | tf_op jit(solution)/shard_map/all_to_all | solution.py:88
  157.3 121.9 %reduce-scatter.5.cloned.1.call-start = ((), (), s32[]{:S(2)}) async-start(), calls=%async_computation.14 | async-start | bytes 3932160 | tf_op jit(solution)/shard_map/reduce_scatter | solution.py:466
  201.0 9.7 %collective-permute-start.4 = (bf16[4,768,384]{2,1,0:T(8,128)(2,1)S(1)}, bf16[4,768,384]{2,1,0:T(8,128)(2,1)S(1)}, u32[]{:S(2)}, u32[]{:S(2)}) collective-permute-start(bf16[4,768,384]{2,1,0:T(8,128)(2,1)S(1)} %dynamic-slice_bitcast_fusion), channel_id=1, source_target_pairs={{0,4},{4,0},{8,12},{12,8},{16,20},{20,16},{24,28},{28,24},{1,5},{5... | collective-permute-start | bytes 7077896 | tf_op jit(solution)/shard_map/ppermute | solution.py:42
  213.7 31.7 %all-to-all-start.5 = ((bf16[4,768,384]{2,1,0:T(8,128)(2,1)}), bf16[4,768,384]{2,1,0:T(8,128)(2,1)}, u32[]{:S(2)}, u32[]{:S(2)}) async-start(bf16[4,768,384]{2,1,0:T(8,128)(2,1)} %copy-done.9), calls=%async_computation.6 | async-start | bytes 4718592 | tf_op jit(solution)/shard_map/all_to_all | solution.py:502
  245.4 38.9 %all-to-all-start.8 = ((bf16[8,3,2,32,768]{4,3,2,1,0:T(8,128)(2,1)}), bf16[8,3,2,32,768]{4,3,2,1,0:T(8,128)(2,1)}, u32[]{:S(2)}, u32[]{:S(2)}) async-start(bf16[8,3,2,32,768]{4,3,2,1,0:T(8,128)(2,1)} %copy-done.8), calls=%async_computation.10 | async-start | bytes 4718592 | tf_op jit(solution)/shard_map/all_to_all | solution.py:88
  256.3 31.7 %collective-permute-start.5 = (bf16[4,2,64,768]{3,2,1,0:T(8,128)(2,1)}, bf16[4,2,64,768]{3,2,1,0:T(8,128)(2,1)}, u32[]{:S(2)}, u32[]{:S(2)}) collective-permute-start(bf16[4,2,64,768]{3,2,1,0:T(8,128)(2,1)} %add_convert_fusion), channel_id=1, source_target_pairs={{0,4},{4,0},{8,12},{12,8},{16,20},{20,16},{24,28},{28,24},{1,5},{5... | collective-permute-start | bytes 2359304 | tf_op jit(solution)/shard_map/ppermute | solution.py:42
  284.3 19.1 %all-to-all-start.6 = ((bf16[8,80,768]{2,1,0:T(8,128)(2,1)}), bf16[8,80,768]{2,1,0:T(8,128)(2,1)S(1)}, u32[]{:S(2)}, u32[]{:S(2)}) async-start(bf16[8,80,768]{2,1,0:T(8,128)(2,1)} %shard_map.183.rest_0_), calls=%async_computation.7 | async-start | bytes 1966080 | tf_op jit(solution)/shard_map/all_to_all | solution.py:88
  290.7 22.8 %collective-permute-start.8 = (bf16[2,64,768]{2,1,0:T(8,128)(2,1)S(1)}, bf16[2,64,768]{2,1,0:T(8,128)(2,1)S(1)}, u32[]{:S(2)}, u32[]{:S(2)}) collective-permute-start(bf16[2,64,768]{2,1,0:T(8,128)(2,1)S(1)} %get-tuple-element.67), channel_id=1, source_target_pairs={{0,24},{4,28},{8,16},{12,20},{16,8},{20,12},{24,0},{28,4},{1,25},{... | collective-permute-start | bytes 589832 | tf_op jit(solution)/shard_map/ppermute | solution.py:42
  293.6 19.8 %collective-permute-start.7 = (bf16[2,64,768]{2,1,0:T(8,128)(2,1)S(1)}, bf16[2,64,768]{2,1,0:T(8,128)(2,1)}, u32[]{:S(2)}, u32[]{:S(2)}) collective-permute-start(bf16[2,64,768]{2,1,0:T(8,128)(2,1)S(1)} %get-tuple-element.68), channel_id=1, source_target_pairs={{0,16},{4,20},{8,24},{12,28},{16,0},{20,4},{24,8},{28,12},{1,17},{... | collective-permute-start | bytes 589832 | tf_op jit(solution)/shard_map/ppermute | solution.py:42
  294.2 19.3 %collective-permute-start.6 = (bf16[2,64,768]{2,1,0:T(8,128)(2,1)S(1)}, bf16[2,64,768]{2,1,0:T(8,128)(2,1)}, u32[]{:S(2)}, u32[]{:S(2)}) collective-permute-start(bf16[2,64,768]{2,1,0:T(8,128)(2,1)S(1)} %get-tuple-element.66), channel_id=1, source_target_pairs={{0,8},{4,12},{8,0},{12,4},{16,24},{20,28},{24,16},{28,20},{1,9},{5... | collective-permute-start | bytes 589832 | tf_op jit(solution)/shard_map/ppermute | solution.py:42
  303.3 18.5 %all-to-all-start.7 = ((bf16[8,80,768]{2,1,0:T(8,128)(2,1)}), bf16[8,80,768]{2,1,0:T(8,128)(2,1)S(1)}, u32[]{:S(2)}, u32[]{:S(2)}) async-start(bf16[8,80,768]{2,1,0:T(8,128)(2,1)} %shard_map.184), calls=%async_computation.9 | async-start | bytes 1966080 | tf_op jit(solution)/shard_map/all_to_all | solution.py:88
  (67 other events, 131.2 us)
Sparse Core Ops, SparseCore 0:
  28.8 62.8 all-gather.2
  93.3 62.1 all-gather.4
  157.8 58.8 reduce-scatter.2
  218.9 60.2 reduce-scatter.4

commit v4 on v3

--- a/solution.py
+++ b/solution.py
@@ -19,6 +19,7 @@
 ANY = pl.BlockSpec(memory_space=pl.ANY)
 SMEM = pl.BlockSpec(memory_space=pltpu.SMEM)
 LIMIT = pltpu.CompilerParams(vmem_limit_bytes=VMEM * 2**20)
+BIG = pltpu.CompilerParams(vmem_limit_bytes=60 * 2**20)
 
 
 def lasting(us):
@@ -171,7 +172,7 @@
         + [by_head(shape) for shape, _ in saved],
         out_shape=[jax.ShapeDtypeStruct((count, frames, part, channels), BF16)]
         + [jax.ShapeDtypeStruct((heads, *shape), kind) for shape, kind in saved],
-        compiler_params=LIMIT,
+        compiler_params=BIG,
         cost_estimate=lasting(8),
     )(video, even, odd, bias, *deps)
 
@@ -180,7 +181,7 @@
     return pl.BlockSpec((1, *shape), lambda h: (h,) + (0,) * len(shape))
 
 
-def attend_back(video, even, odd, saved, grad, deps=()):
+def attend_back(video, even, odd, saved, grad, arrays, deps=()):
     count, _, frames, part, channels = video.shape
     tokens = even.shape[2]
     heads = channels // HEAD_DIM
@@ -229,9 +230,9 @@
         + [pl.BlockSpec((count, frames, part, HEAD_DIM), lambda h: (0, 0, 0, h))]
         + [ANY] * len(deps),
         out_specs=[video_spec, *out_ref_specs],
-        out_shape=[jax.ShapeDtypeStruct(video.shape, BF16)]
+        out_shape=[jax.ShapeDtypeStruct((count, arrays, frames, part, channels), BF16)]
         + [jax.ShapeDtypeStruct((*even.shape[:3], channels), F32)] * 2,
-        compiler_params=LIMIT,
+        compiler_params=BIG,
         cost_estimate=lasting(10),
     )(video, even, odd, *saved, grad, *deps)
 
@@ -260,14 +261,14 @@
     )(taps, cot)
 
 
-def mix(mixed, cot, taps, count, deps=()):
+def mix(mixed, cot, taps, count, room=None, taps_before=None, deps=()):
     full, part, channels = cot.shape
     reach = taps.shape[0]
     frames = full // count
+    last = taps_before is not None
     extra = -(-2 * reach // 16) * 16
 
     def kernel(taps_ref, mixed_ref, cot_ref, *rest):
-        out_ref = rest[-1]
         line = []
         sums = [jnp.zeros((part, HEAD_DIM), F32) for _ in range(reach)]
         for f in range(full):
@@ -278,24 +279,46 @@
                 total = total + taps_ref[k : k + 1, :] * line[f - k]
                 sums[k] = sums[k] + cot_line * line[f - k]
             d, u = f // frames, f % frames
-            out_ref[d, u * part : (u + 1) * part] = total.astype(BF16)
+            if last:
+                rest[-1][d, u * part : (u + 1) * part] = total.astype(BF16)
+            else:
+                rest[-2][d, 0, u] = total.astype(BF16)
         sums = jnp.concatenate([jnp.sum(s, axis=0, keepdims=True) for s in sums], axis=0)
-        high = sums.astype(BF16).astype(F32)
-        zeros = jnp.zeros((extra - 2 * reach, HEAD_DIM), F32)
-        rows = jnp.concatenate([high, sums - high, zeros], axis=0).astype(BF16)
-        for d in range(count):
-            out_ref[d, frames * part :] = rows
+        if last:
+            sums = sums + rest[0][...]
+            high = sums.astype(BF16).astype(F32)
+            zeros = jnp.zeros((extra - 2 * reach, HEAD_DIM), F32)
+            rows = jnp.concatenate([high, sums - high, zeros], axis=0).astype(BF16)
+            for d in range(count):
+                rest[-1][d, frames * part :] = rows
+        else:
+            rest[-1][...] = sums
 
     block = pl.BlockSpec((full, part, HEAD_DIM), lambda h: (0, 0, h))
+    taps_block = pl.BlockSpec((reach, HEAD_DIM), lambda h: (0, h))
+    if last:
+        out_specs = pl.BlockSpec((count, frames * part + extra, HEAD_DIM), lambda h: (0, 0, h))
+        out_shape = jax.ShapeDtypeStruct((count, frames * part + extra, channels), BF16)
+    else:
+        slot = room.shape[1] - 1
+        out_specs = [
+            pl.BlockSpec((count, 1, frames, part, HEAD_DIM), lambda h: (0, slot, 0, 0, h)),
+            taps_block,
+        ]
+        out_shape = [
+            jax.ShapeDtypeStruct(room.shape, BF16),
+            jax.ShapeDtypeStruct(taps.shape, F32),
+        ]
     return pl.pallas_call(
         kernel,
         grid=(channels // HEAD_DIM,),
-        in_specs=[pl.BlockSpec((reach, HEAD_DIM), lambda h: (0, h)), block, block] + [ANY] * len(deps),
-        out_specs=pl.BlockSpec((count, frames * part + extra, HEAD_DIM), lambda h: (0, 0, h)),
-        out_shape=jax.ShapeDtypeStruct((count, frames * part + extra, channels), BF16),
+        in_specs=[taps_block, block, block, taps_block if last else ANY] + [ANY] * len(deps),
+        input_output_aliases={} if last else {3: 0},
+        out_specs=out_specs,
+        out_shape=out_shape,
         compiler_params=LIMIT,
         cost_estimate=lasting(3),
-    )(taps, mixed, cot, *deps)
+    )(taps, mixed, cot, taps_before if last else room, *deps)
 
 
 def project(attended, weight, deps=()):
@@ -317,7 +340,7 @@
         + [ANY] * len(deps),
         out_specs=pl.BlockSpec((1, rows, channels), lambda j: (j, 0, 0)),
         out_shape=jax.ShapeDtypeStruct((depth, rows, channels), BF16),
-        compiler_params=LIMIT,
+        compiler_params=BIG,
         cost_estimate=lasting(4),
     )(attended, weight, *deps)
 
@@ -355,7 +378,7 @@
         out_specs=pl.BlockSpec((rows, channels), lambda j: (0, 0)),
         out_shape=jax.ShapeDtypeStruct((rows, channels), BF16),
         scratch_shapes=[pltpu.VMEM((rows, channels), F32)],
-        compiler_params=LIMIT,
+        compiler_params=BIG,
         cost_estimate=lasting(6),
     )(blocks, weight, *deps)
 
@@ -390,7 +413,7 @@
         out_specs=pl.BlockSpec((1, parts, channels, columns), lambda j: (j, 0, 0, 0)),
         out_shape=jax.ShapeDtypeStruct((depth, parts, channels, columns), BF16),
         scratch_shapes=[pltpu.VMEM((chunks, channels, rows), BF16)],
-        compiler_params=LIMIT,
+        compiler_params=BIG,
         cost_estimate=lasting(7),
     )(*attended, *blocks, *deps)
 
@@ -455,7 +478,7 @@
         before = video[-1]
 
     last = []
-    attended, saved, mixed, back, finals = [], [], [], [], []
+    attended, saved, mixed = [], [], []
 
     def forward(c):
         nonlocal last
@@ -472,49 +495,40 @@
         last = [grad]
         return grad.reshape(count, frames, part, channels)
 
-    def backward(c, grad):
+    def backward(c, grad, arrays):
         nonlocal last
-        results = attend_back(video[c], even, odd, saved[c], grad, last)
+        results = attend_back(video[c], even, odd, saved[c], grad, arrays, last)
         last = [results[1]]
-        back.append((travel(results[0]), results[1], results[2]))
-
-    def finish(c):
-        nonlocal last
-        final = mix(mixed[c].reshape(line), cot[c], conv_taps, count, last)
-        last = [final]
-        return final
+        return results
 
     forward(0)
-    backward(0, pull(0))
-    for c in range(1, CHUNKS):
-        forward(c)
-
-    last = [*last, back[0][0]]
-    terms = weight_terms(attended, blocks, count, last)
-    last = [terms]
+    first_back, even_first, odd_first = backward(0, pull(0), 3)
+    first_back = travel(first_back)
+    forward(1)
+
+    terms = weight_terms(attended, blocks, count, [*last, first_back])
     by_chip = terms.reshape(count // 2, 2, channels, terms.shape[3])
     core = place % 2
     near = swap(lax.dynamic_index_in_dim(by_chip, 1 - core, 1, keepdims=False), 1)
-    grads = [pull(c) for c in range(1, CHUNKS)]
-    sums = core_sums(by_chip, near, core, last)
+    sums = core_sums(by_chip, near, core)
     last = [sums]
     groups = [list(range(k, count, 2)) for k in range(2)]
     far = lax.all_to_all(sums, "frame", split_axis=0, concat_axis=0, axis_index_groups=groups, tiled=True)
-    for c in range(1, CHUNKS):
-        backward(c, grads[c - 1])
-
-    last = [*last, far]
-    for c in range(CHUNKS):
-        finals.append(travel(finish(c)))
-        last = [*last, back[c][0]] if c == 0 else last
-    ref_even, ref_odd = (sum(b[k] for b in back) for k in (1, 2))
-    ref_grads = reduce_pieces(ref_even, ref_odd, last)
+
+    second_back, even_second, odd_second = backward(1, pull(1), 4)
+    second_back, taps_first = mix(
+        mixed[0].reshape(line), cot[0], conv_taps, count, room=second_back, deps=[*last, far]
+    )
+    second_back = travel(second_back)
+    ref_grads = reduce_pieces(even_first + even_second, odd_first + odd_second, [second_back])
+    final = mix(mixed[1].reshape(line), cot[1], conv_taps, count, taps_before=taps_first, deps=[ref_grads])
+    final = travel(final)
     grad_weight = jnp.sum(far.astype(F32), axis=0)
 
-    grads = [to_frames([b[0][:, a] for b in back]) for a in range(3)]
+    grads = [to_frames([first_back[:, a], second_back[:, a]]) for a in range(3)]
     held_rows = frames * part
-    out = to_frames([f[:, :held_rows].reshape(count, frames, part, channels) for f in finals])
-    taps_parts = jnp.sum(sum(f[:, held_rows : held_rows + 2 * reach].astype(F32) for f in finals), axis=0)
+    out = to_frames([second_back[:, 3], final[:, :held_rows].reshape(count, frames, part, channels)])
+    taps_parts = jnp.sum(final[:, held_rows : held_rows + 2 * reach].astype(F32), axis=0)
     taps_sum = taps_parts[:reach] + taps_parts[reach:]
     return (out, *grads, ref_grads[0], ref_grads[1], grad_weight, taps_sum)
 

time: 333 us -> 319 us (0.958)
  local copies, waits for them, and re-layouts: 85.6 us -> 32 us
  waiting for transfers between devices: 67.7 us -> 98.7 us
  Pallas kernels: 74.9 us -> 89.2 us
    unnamed x142 -> x52, local copies, waits for them, and re-layouts: 69 us -> 15.7 us
    all_to_all x6 -> x5, waiting for transfers between devices: 46.6 us -> 73.1 us  [travel(): lax.all_to_all(value, 'frame', split_axis=0, concat_axis=0, tiled=True)]
    reduce_scatter x2, waiting for transfers between devices: 14.2 us -> 1.77 us  [forward(): lax.psum_scatter(shares, 'head', scatter_dimension=0, tiled=False)]
    ppermute x9, waiting for transfers between devices: 5.18 us -> 15.7 us  [swap(): return lax.ppermute(value, 'frame', [(i, i ^ s) for i in range(count)])]
    pallas_call x2, Pallas kernels: 7.85 us -> 12.9 us  [project(): pl.pallas_call(kernel, grid=(depth,), in_specs=[pl.BlockSpec((rows, chann...]
    pallas_call x2, Pallas kernels: 11.4 us -> 15.9 us  [project_back(): pl.pallas_call(kernel, grid=(depth,), in_specs=[pl.BlockSpec((1, rows, ch...]
    all_to_all x1, waiting for transfers between devices: 1.6 us -> 6.06 us  [per_device(): lax.all_to_all(sums, 'frame', split_axis=0, concat_axis=0, axis_index_gro...]
    pallas_call x1, Pallas kernels: 6.05 us -> 9.51 us  [weight_terms(): pl.pallas_call(kernel, grid=(depth,), in_specs=[pl.BlockSpec((rows, chann...]
  transfers between devices with their start and end apart: 20 -> 19, of which waited for: 9 -> 13; matrix products, arithmetic and copies ran while one was open for 10% -> 9% of each run, Pallas kernels for 22% -> 27%
where the time goes in v4:
time: 319 us; the launch traced here: 317 us
  waiting for transfers between devices  98.7 us (31%)
  Pallas kernels  89.2 us (28%)
  starting transfers between devices  33.2 us (10%)
  blocking collectives  32.5 us (10%)
  local copies, waits for them, and re-layouts  32 us (10%)
  other arithmetic  16.9 us (5%)
  between operations  14.2 us (4%)
    all_to_all x5, waiting for transfers between devices, travel(): lax.all_to_all(value, 'frame', split_axis=0, concat_axis=0, tiled=True)  73.1 us
    all_to_all x2, blocking collectives, travel(): lax.all_to_all(value, 'frame', split_axis=0, concat_axis=0, tiled=True)  32.5 us
    pallas_call x2, Pallas kernels, attend_back(): pl.pallas_call(kernel, grid=(heads,), in_specs=[video_spec, *ref_specs] +...  24 us
    all_to_all x5, starting transfers between devices, travel(): lax.all_to_all(value, 'frame', split_axis=0, concat_axis=0, tiled=True)  21.3 us
    pallas_call x2, Pallas kernels, attend(): pl.pallas_call(kernel, grid=(heads,), in_specs=[pl.BlockSpec((count, 3, f...  17.8 us
    pallas_call x2, Pallas kernels, project_back(): pl.pallas_call(kernel, grid=(depth,), in_specs=[pl.BlockSpec((1, rows, ch...  15.9 us
    unnamed x52, local copies, waits for them, and re-layouts  15.7 us
    ppermute x9, waiting for transfers between devices, swap(): return lax.ppermute(value, 'frame', [(i, i ^ s) for i in range(count)])  15.7 us
  transfers between devices with their start and end apart: 19, of which 13 were waited for; matrix products, arithmetic and copies ran while one was open for 9% of the time, Pallas kernels for 27%

profile of v4, /device:TPU:0, one launch (start us, length us, event | category | flops | bytes accessed | tf_op | source)
XLA Modules:
  0.0 316.6 jit_solution(16910878104140189939)
XLA Ops:
  8.8 17.5 %all_to_all.40 = bf16[8,1,2,32,768]{4,3,2,1,0:T(8,128)(2,1)S(1)} all-to-all(bf16[8,1,2,32,768]{4,3,2,1,0:T(8,128)(2,1)S(1)} %copy.56), channel_id=1, replica_groups=mesh['frame'=8,'head'=4] {'frame'}, dimensions={0} | all-to-all | bytes 1572864 | tf_op jit(solution)/shard_map/all_to_all | solution.py:89
  28.9 15.0 %all_to_all.41 = bf16[8,1,2,32,768]{4,3,2,1,0:T(8,128)(2,1)S(1)} all-to-all(bf16[8,1,2,32,768]{4,3,2,1,0:T(8,128)(2,1)S(1)} %copy.57), channel_id=1, replica_groups=mesh['frame'=8,'head'=4] {'frame'}, dimensions={0} | all-to-all | bytes 1572864 | tf_op jit(solution)/shard_map/all_to_all | solution.py:89
  57.0 3.5 %collective-permute-done.1.refs_2_ = bf16[2,64,768]{2,1,0:T(8,128)(2,1)S(1)} collective-permute-done((bf16[2,64,768]{2,1,0:T(8,128)(2,1)S(1)}, bf16[2,64,768]{2,1,0:T(8,128)(2,1)S(1)}, u32[]{:S(2)}, u32[]{:S(2)}) %collective-permute-start.1) | collective-permute-done | bytes 196640 | tf_op jit(solution)/shard_map/ppermute | solution.py:43
  60.6 4.5 %all-to-all-start.2 = ((bf16[8,3,2,32,768]{4,3,2,1,0:T(8,128)(2,1)}), bf16[8,3,2,32,768]{4,3,2,1,0:T(8,128)(2,1)}, u32[]{:S(2)}, u32[]{:S(2)}) async-start(bf16[8,3,2,32,768]{4,3,2,1,0:T(8,128)(2,1)} %pad_maximum_fusion), calls=%async_computation.2 | async-start | bytes 4718592 | tf_op jit(solution)/shard_map/all_to_all | solution.py:89
  70.2 24.4 %all-to-all-done.2.video_ref = bf16[8,3,2,32,768]{4,3,2,1,0:T(8,128)(2,1)} async-done(((bf16[8,3,2,32,768]{4,3,2,1,0:T(8,128)(2,1)}), bf16[8,3,2,32,768]{4,3,2,1,0:T(8,128)(2,1)}, u32[]{:S(2)}, u32[]{:S(2)}) %all-to-all-start.2) | async-done | bytes 2359328 | tf_op jit(solution)/shard_map/all_to_all | solution.py:89
  94.6 4.4 %all-to-all-start.3 = ((bf16[8,3,2,32,768]{4,3,2,1,0:T(8,128)(2,1)}), bf16[8,3,2,32,768]{4,3,2,1,0:T(8,128)(2,1)}, u32[]{:S(2)}, u32[]{:S(2)}) async-start(bf16[8,3,2,32,768]{4,3,2,1,0:T(8,128)(2,1)} %pad_maximum_fusion.1), calls=%async_computation.4 | async-start | bytes 4718592 | tf_op jit(solution)/shard_map/all_to_all | solution.py:89
  99.1 8.9 %shard_map.173 = (bf16[8,2,32,768]{3,2,1,0:T(8,128)(2,1)}, bf16[6,2,256,256]{3,2,1,0:T(8,128)(2,1)}, bf16[6,2,512,256]{3,2,1,0:T(8,128)(2,1)}, f32[6,2,2,256]{3,2,1,0:T(2,128)}, bf16[6,2,2,128,256]{4,3,2,1,0:T(8,128)(2,1)}) custom-call(bf16[8,3,2,32,768]{4,3,2,1,0:T(8,128)(2,1)} %all-to-all-done.2.video_ref, bf16[4,2,64,768]{3,2,1,0:T(8,128)(2,1)} %copy-done.8, ...), custom_call_target="tpu_custom_call" | custom-call | flops 9200000000 | tf_op jit(solution)/shard_map/pallas_call | solution.py:164
  108.0 6.4 %shard_map.174.rest_0_ = bf16[4,512,768]{2,1,0:T(8,128)(2,1)} custom-call(bf16[512,768]{1,0:T(8,128)(2,1)} %bitcast.127, bf16[768,3072]{1,0:T(8,128)(2,1)} %weight_ref.7), custom_call_target="tpu_custom_call" | custom-call | flops 4600000000 | tf_op jit(solution)/shard_map/pallas_call | solution.py:333
  114.5 8.0 %shard_map.175.rest_0_ = bf16[512,768]{1,0:T(8,128)(2,1)} custom-call(bf16[4,512,768]{2,1,0:T(8,128)(2,1)} %all-gather.3.cloned.1.call-done.blocks_ref.refs_2_, bf16[768,3072]{1,0:T(8,128)(2,1)} %weight_ref.7, bf16[4,512,768]{2,1,0:T(8,128)(2,1)} %shard_map.174.rest_0_), custom_call_target="tpu_custom_call" | custom-call | flops 6899999744 | tf_op jit(solution)/shard_map/pallas_call | solution.py:370
  122.4 11.6 %shard_map.176 = (bf16[8,3,2,32,768]{4,3,2,1,0:T(8,128)(2,1)}, f32[4,2,64,768]{3,2,1,0:T(8,128)}, f32[4,2,64,768]{3,2,1,0:T(8,128)}) custom-call(bf16[8,3,2,32,768]{4,3,2,1,0:T(8,128)(2,1)} %all-to-all-done.2.video_ref, bf16[4,2,64,768]{3,2,1,0:T(8,128)(2,1)} %copy-done.8, bf16[4,2,64,768]{3,2,1,0:T(8,128)(2,1)} %collective-permute-done.3.odd_ref, ...), custom_call_target="tpu_custom_call" | custom-call | flops 11500000256 | tf_op jit(solution)/shard_map/pallas_call | solution.py:225
  134.1 4.1 %all-to-all-start.4 = ((bf16[8,3,2,32,768]{4,3,2,1,0:T(8,128)(2,1)}), bf16[8,3,2,32,768]{4,3,2,1,0:T(8,128)(2,1)S(1)}, u32[]{:S(2)}, u32[]{:S(2)}) async-start(bf16[8,3,2,32,768]{4,3,2,1,0:T(8,128)(2,1)} %get-tuple-element.46), calls=%async_computation.5 | async-start | bytes 4718592 | tf_op jit(solution)/shard_map/all_to_all | solution.py:89
  138.2 8.8 %shard_map.177 = (bf16[8,2,32,768]{3,2,1,0:T(8,128)(2,1)}, bf16[6,2,256,256]{3,2,1,0:T(8,128)(2,1)}, bf16[6,2,512,256]{3,2,1,0:T(8,128)(2,1)}, f32[6,2,2,256]{3,2,1,0:T(2,128)}, bf16[6,2,2,128,256]{4,3,2,1,0:T(8,128)(2,1)}) custom-call(bf16[8,3,2,32,768]{4,3,2,1,0:T(8,128)(2,1)} %all-to-all-done.3.video_ref, bf16[4,2,64,768]{3,2,1,0:T(8,128)(2,1)} %copy-done.8, ...), custom_call_target="tpu_custom_call" | custom-call | flops 9200000000 | tf_op jit(solution)/shard_map/pallas_call | solution.py:164
  147.0 6.5 %shard_map.178.refs_4_ = bf16[4,512,768]{2,1,0:T(8,128)(2,1)} custom-call(bf16[512,768]{1,0:T(8,128)(2,1)} %bitcast.129, bf16[768,3072]{1,0:T(8,128)(2,1)} %weight_ref.7), custom_call_target="tpu_custom_call" | custom-call | flops 4600000000 | tf_op jit(solution)/shard_map/pallas_call | solution.py:333
  155.5 12.1 %all-to-all-done.4.refs_5_ = bf16[8,3,2,32,768]{4,3,2,1,0:T(8,128)(2,1)S(1)} async-done(((bf16[8,3,2,32,768]{4,3,2,1,0:T(8,128)(2,1)}), bf16[8,3,2,32,768]{4,3,2,1,0:T(8,128)(2,1)S(1)}, u32[]{:S(2)}, u32[]{:S(2)}) %all-to-all-start.4) | async-done | bytes 2359328 | tf_op jit(solution)/shard_map/all_to_all | solution.py:89
  169.1 9.5 %shard_map.179.terms_ref = bf16[4,2,768,384]{3,2,1,0:T(8,128)(2,1)} custom-call(bf16[512,768]{1,0:T(8,128)(2,1)} %bitcast.128, bf16[512,768]{1,0:T(8,128)(2,1)} %bitcast.130, bf16[4,512,768]{2,1,0:T(8,128)(2,1)} %all-gather.3.cloned.1.call-done.blocks_ref.refs_2_, bf16[4,512,768]{2,1,0:T(8,128)(2,1)} %all-gather.5.cloned.1.call-done.refs_3_.blocks_ref, ...), custom_call_target="tpu_custom_call" | custom-call | flops 8049999872 | tf_op jit(solution)/shard_map/pallas_call | solution.py:407
  181.9 4.7 %collective-permute-done.4.near_ref = bf16[4,768,384]{2,1,0:T(8,128)(2,1)S(1)} collective-permute-done((bf16[4,768,384]{2,1,0:T(8,128)(2,1)}, bf16[4,768,384]{2,1,0:T(8,128)(2,1)S(1)}, u32[]{:S(2)}, u32[]{:S(2)}) %collective-permute-start.4) | collective-permute-done | bytes 2359328 | tf_op jit(solution)/shard_map/ppermute | solution.py:43
  191.0 3.8 %all-to-all-start.5 = ((bf16[4,768,384]{2,1,0:T(8,128)(2,1)}), bf16[4,768,384]{2,1,0:T(8,128)(2,1)S(1)}, u32[]{:S(2)}, u32[]{:S(2)}) async-start(bf16[4,768,384]{2,1,0:T(8,128)(2,1)} %copy-done.2), calls=%async_computation.6 | async-start | bytes 4718592 | tf_op jit(solution)/shard_map/all_to_all | solution.py:516
  194.8 7.9 %shard_map.181.rest_0_ = bf16[512,768]{1,0:T(8,128)(2,1)} custom-call(bf16[4,512,768]{2,1,0:T(8,128)(2,1)} %all-gather.5.cloned.1.call-done.refs_3_.blocks_ref, bf16[768,3072]{1,0:T(8,128)(2,1)} %weight_ref.7, bf16[4,768,384]{2,1,0:T(8,128)(2,1)} %copy-done.2), custom_call_target="tpu_custom_call" | custom-call | flops 6899999744 | tf_op jit(solution)/shard_map/pallas_call | solution.py:370
  202.7 12.3 %shard_map.182 = (bf16[8,4,2,32,768]{4,3,2,1,0:T(8,128)(2,1)}, f32[4,2,64,768]{3,2,1,0:T(8,128)}, f32[4,2,64,768]{3,2,1,0:T(8,128)}) custom-call(bf16[8,3,2,32,768]{4,3,2,1,0:T(8,128)(2,1)} %all-to-all-done.3.video_ref, bf16[4,2,64,768]{3,2,1,0:T(8,128)(2,1)} %copy-done.8, bf16[4,2,64,768]{3,2,1,0:T(8,128)(2,1)} %collective-permute-done.3.odd_ref, ...), custom_call_target="tpu_custom_call" | custom-call | flops 11500000256 | tf_op jit(solution)/shard_map/pallas_call | solution.py:225
  216.8 6.1 %all-to-all-done.5.rest_2_ = bf16[4,768,384]{2,1,0:T(8,128)(2,1)S(1)} async-done(((bf16[4,768,384]{2,1,0:T(8,128)(2,1)}), bf16[4,768,384]{2,1,0:T(8,128)(2,1)S(1)}, u32[]{:S(2)}, u32[]{:S(2)}) %all-to-all-start.5) | async-done | bytes 2359328 | tf_op jit(solution)/shard_map/all_to_all | solution.py:516
  231.4 4.4 %all-to-all-start.6 = ((bf16[8,4,2,32,768]{4,3,2,1,0:T(8,128)(2,1)}), bf16[8,4,2,32,768]{4,3,2,1,0:T(8,128)(2,1)}, u32[]{:S(2)}, u32[]{:S(2)}) async-start(bf16[8,4,2,32,768]{4,3,2,1,0:T(8,128)(2,1)} %copy-done.1), calls=%async_computation.7 | async-start | bytes 6291456 | tf_op jit(solution)/shard_map/all_to_all | solution.py:89
  243.7 30.0 %all-to-all-done.6 = bf16[8,4,2,32,768]{4,3,2,1,0:T(8,128)(2,1)} async-done(((bf16[8,4,2,32,768]{4,3,2,1,0:T(8,128)(2,1)}), bf16[8,4,2,32,768]{4,3,2,1,0:T(8,128)(2,1)}, u32[]{:S(2)}, u32[]{:S(2)}) %all-to-all-start.6) | async-done | bytes 3145760 | tf_op jit(solution)/shard_map/all_to_all | solution.py:89
  289.4 4.0 %all-to-all-start.7 = ((bf16[8,80,768]{2,1,0:T(8,128)(2,1)}), bf16[8,80,768]{2,1,0:T(8,128)(2,1)S(1)}, u32[]{:S(2)}, u32[]{:S(2)}) async-start(bf16[8,80,768]{2,1,0:T(8,128)(2,1)} %shard_map.184), calls=%async_computation.9 | async-start | bytes 1966080 | tf_op jit(solution)/shard_map/all_to_all | solution.py:89
  301.4 6.7 %all-to-all-done.7 = bf16[8,80,768]{2,1,0:T(8,128)(2,1)S(1)} async-done(((bf16[8,80,768]{2,1,0:T(8,128)(2,1)}), bf16[8,80,768]{2,1,0:T(8,128)(2,1)S(1)}, u32[]{:S(2)}, u32[]{:S(2)}) %all-to-all-start.7) | async-done | bytes 983072 | tf_op jit(solution)/shard_map/all_to_all | solution.py:89
  (131 shorter events, 77.4 us)
Async XLA Ops:
  7.2 107.3 %all-gather.3.cloned.1.call-start = ((), (), s32[]{:S(2)}) async-start(), calls=%async_computation.11 | async-start | bytes 3932160 | tf_op jit(solution)/shard_map/all_gather | solution.py:469
  8.7 17.6 %copy-start.11 = (f32[3,768]{1,0:T(4,128)S(1)}, f32[3,768]{1,0:T(4,128)}, u32[]{:S(2)}) copy-start(f32[3,768]{1,0:T(4,128)} %taps_ref.7) | copy-start | bytes 27652
  28.8 126.8 %all-gather.5.cloned.1.call-start = ((), (), s32[]{:S(2)}) async-start(), calls=%async_computation.12 | async-start | bytes 3932160 | tf_op jit(solution)/shard_map/all_gather | solution.py:469
  49.1 7.9 %collective-permute-start = (bf16[2,64,768]{2,1,0:T(8,128)(2,1)S(1)}, bf16[2,64,768]{2,1,0:T(8,128)(2,1)S(1)}, u32[]{:S(2)}, u32[]{:S(2)}) collective-permute-start(bf16[2,64,768]{2,1,0:T(8,128)(2,1)S(1)} %pad_maximum_fusion.6.refs_0_), channel_id=1, source_target_pairs={{0,8},{4,12},{8,0},{12,4},{16,24},{20,28},{24,16},{28,20},{1,9},{5... | collective-permute-start | bytes 589832 | tf_op jit(solution)/shard_map/ppermute | solution.py:43
  49.8 10.8 %collective-permute-start.1 = (bf16[2,64,768]{2,1,0:T(8,128)(2,1)S(1)}, bf16[2,64,768]{2,1,0:T(8,128)(2,1)S(1)}, u32[]{:S(2)}, u32[]{:S(2)}) collective-permute-start(bf16[2,64,768]{2,1,0:T(8,128)(2,1)S(1)} %pad_maximum_fusion.6.refs_0_), channel_id=1, source_target_pairs={{0,16},{4,20},{8,24},{12,28},{16,0},{20,4},{24,8},{28,12},{1,17},{... | collective-permute-start | bytes 589832 | tf_op jit(solution)/shard_map/ppermute | solution.py:43
  50.3 10.2 %collective-permute-start.2 = (bf16[2,64,768]{2,1,0:T(8,128)(2,1)S(1)}, bf16[2,64,768]{2,1,0:T(8,128)(2,1)S(1)}, u32[]{:S(2)}, u32[]{:S(2)}) collective-permute-start(bf16[2,64,768]{2,1,0:T(8,128)(2,1)S(1)} %pad_maximum_fusion.6.refs_0_), channel_id=1, source_target_pairs={{0,24},{4,28},{8,16},{12,20},{16,8},{20,12},{24,0},{28,4},{1,25},{... | collective-permute-start | bytes 589832 | tf_op jit(solution)/shard_map/ppermute | solution.py:43
  60.6 4.7 %copy-start.8 = (bf16[4,2,64,768]{3,2,1,0:T(8,128)(2,1)}, bf16[4,2,64,768]{3,2,1,0:T(8,128)(2,1)S(1)}, u32[]{:S(2)}) copy-start(bf16[4,2,64,768]{3,2,1,0:T(8,128)(2,1)S(1)} %shard_map.172.even_ref) | copy-start | bytes 2359300
  60.6 4.6 %copy-start.25 = (f32[6]{0:T(128)S(1)}, f32[6]{0:T(128)}, u32[]{:S(2)}) copy-start(f32[6]{0:T(128)} %param.16) | copy-start | bytes 76
  60.6 4.6 %copy-start.24 = (s32[16]{0:T(128)S(1)}, s32[16]{0:T(128)}, u32[]{:S(2)}) copy-start(s32[16]{0:T(128)} %param.18) | copy-start | bytes 196
  60.6 5.1 %copy-start.23 = (f32[6]{0:T(128)S(1)}, f32[6]{0:T(128)}, u32[]{:S(2)}) copy-start(f32[6]{0:T(128)} %param.17) | copy-start | bytes 76
  60.6 34.0 %all-to-all-start.2 = ((bf16[8,3,2,32,768]{4,3,2,1,0:T(8,128)(2,1)}), bf16[8,3,2,32,768]{4,3,2,1,0:T(8,128)(2,1)}, u32[]{:S(2)}, u32[]{:S(2)}) async-start(bf16[8,3,2,32,768]{4,3,2,1,0:T(8,128)(2,1)} %pad_maximum_fusion), calls=%async_computation.2 | async-start | bytes 4718592 | tf_op jit(solution)/shard_map/all_to_all | solution.py:89
  65.3 33.8 %collective-permute-start.3 = (bf16[4,2,64,768]{3,2,1,0:T(8,128)(2,1)S(1)}, bf16[4,2,64,768]{3,2,1,0:T(8,128)(2,1)}, u32[]{:S(2)}, u32[]{:S(2)}) collective-permute-start(bf16[4,2,64,768]{3,2,1,0:T(8,128)(2,1)S(1)} %shard_map.172.even_ref), channel_id=1, source_target_pairs={{0,4},{4,0},{8,12},{12,8},{16,20},{20,16},{24,28},{28,24},{1,5},{5... | collective-permute-start | bytes 2359304 | tf_op jit(solution)/shard_map/ppermute | solution.py:43
  94.6 39.5 %all-to-all-start.3 = ((bf16[8,3,2,32,768]{4,3,2,1,0:T(8,128)(2,1)}), bf16[8,3,2,32,768]{4,3,2,1,0:T(8,128)(2,1)}, u32[]{:S(2)}, u32[]{:S(2)}) async-start(bf16[8,3,2,32,768]{4,3,2,1,0:T(8,128)(2,1)} %pad_maximum_fusion.1), calls=%async_computation.4 | async-start | bytes 4718592 | tf_op jit(solution)/shard_map/all_to_all | solution.py:89
  99.0 117.8 %reduce-scatter.3.cloned.1.call-start = ((), (), s32[]{:S(2)}) async-start(), calls=%async_computation.10 | async-start | bytes 3932160 | tf_op jit(solution)/shard_map/reduce_scatter | solution.py:489
  134.1 33.5 %all-to-all-start.4 = ((bf16[8,3,2,32,768]{4,3,2,1,0:T(8,128)(2,1)}), bf16[8,3,2,32,768]{4,3,2,1,0:T(8,128)(2,1)S(1)}, u32[]{:S(2)}, u32[]{:S(2)}) async-start(bf16[8,3,2,32,768]{4,3,2,1,0:T(8,128)(2,1)} %get-tuple-element.46), calls=%async_computation.5 | async-start | bytes 4718592 | tf_op jit(solution)/shard_map/all_to_all | solution.py:89
  138.1 147.5 %reduce-scatter.5.cloned.1.call-start = ((), (), s32[]{:S(2)}) async-start(), calls=%async_computation.13 | async-start | bytes 3932160 | tf_op jit(solution)/shard_map/reduce_scatter | solution.py:489
  181.9 4.7 %collective-permute-start.4 = (bf16[4,768,384]{2,1,0:T(8,128)(2,1)}, bf16[4,768,384]{2,1,0:T(8,128)(2,1)S(1)}, u32[]{:S(2)}, u32[]{:S(2)}) collective-permute-start(bf16[4,768,384]{2,1,0:T(8,128)(2,1)} %dynamic-slice_bitcast_fusion), channel_id=1, source_target_pairs={{0,4},{4,0},{8,12},{12,8},{16,20},{20,16},{24,28},{28,24},{1,5},{5... | collective-permute-start | bytes 7077896 | tf_op jit(solution)/shard_map/ppermute | solution.py:43
  191.0 31.9 %all-to-all-start.5 = ((bf16[4,768,384]{2,1,0:T(8,128)(2,1)}), bf16[4,768,384]{2,1,0:T(8,128)(2,1)S(1)}, u32[]{:S(2)}, u32[]{:S(2)}) async-start(bf16[4,768,384]{2,1,0:T(8,128)(2,1)} %copy-done.2), calls=%async_computation.6 | async-start | bytes 4718592 | tf_op jit(solution)/shard_map/all_to_all | solution.py:516
  231.4 42.3 %all-to-all-start.6 = ((bf16[8,4,2,32,768]{4,3,2,1,0:T(8,128)(2,1)}), bf16[8,4,2,32,768]{4,3,2,1,0:T(8,128)(2,1)}, u32[]{:S(2)}, u32[]{:S(2)}) async-start(bf16[8,4,2,32,768]{4,3,2,1,0:T(8,128)(2,1)} %copy-done.1), calls=%async_computation.7 | async-start | bytes 6291456 | tf_op jit(solution)/shard_map/all_to_all | solution.py:89
  239.0 34.8 %collective-permute-start.5 = (bf16[4,2,64,768]{3,2,1,0:T(8,128)(2,1)}, bf16[4,2,64,768]{3,2,1,0:T(8,128)(2,1)}, u32[]{:S(2)}, u32[]{:S(2)}) collective-permute-start(bf16[4,2,64,768]{3,2,1,0:T(8,128)(2,1)} %add_convert_fusion), channel_id=1, source_target_pairs={{0,4},{4,0},{8,12},{12,8},{16,20},{20,16},{24,28},{28,24},{1,5},{5... | collective-permute-start | bytes 2359304 | tf_op jit(solution)/shard_map/ppermute | solution.py:43
  275.6 8.1 %collective-permute-start.8 = (bf16[2,64,768]{2,1,0:T(8,128)(2,1)S(1)}, bf16[2,64,768]{2,1,0:T(8,128)(2,1)S(1)}, u32[]{:S(2)}, u32[]{:S(2)}) collective-permute-start(bf16[2,64,768]{2,1,0:T(8,128)(2,1)S(1)} %get-tuple-element.72), channel_id=1, source_target_pairs={{0,24},{4,28},{8,16},{12,20},{16,8},{20,12},{24,0},{28,4},{1,25},{... | collective-permute-start | bytes 589832 | tf_op jit(solution)/shard_map/ppermute | solution.py:43
  276.3 9.0 %collective-permute-start.7 = (bf16[2,64,768]{2,1,0:T(8,128)(2,1)S(1)}, bf16[2,64,768]{2,1,0:T(8,128)(2,1)S(1)}, u32[]{:S(2)}, u32[]{:S(2)}) collective-permute-start(bf16[2,64,768]{2,1,0:T(8,128)(2,1)S(1)} %get-tuple-element.73), channel_id=1, source_target_pairs={{0,16},{4,20},{8,24},{12,28},{16,0},{20,4},{24,8},{28,12},{1,17},{... | collective-permute-start | bytes 589832 | tf_op jit(solution)/shard_map/ppermute | solution.py:43
  277.6 7.9 %collective-permute-start.6 = (bf16[2,64,768]{2,1,0:T(8,128)(2,1)S(1)}, bf16[2,64,768]{2,1,0:T(8,128)(2,1)S(1)}, u32[]{:S(2)}, u32[]{:S(2)}) collective-permute-start(bf16[2,64,768]{2,1,0:T(8,128)(2,1)S(1)} %get-tuple-element.71), channel_id=1, source_target_pairs={{0,8},{4,12},{8,0},{12,4},{16,24},{20,28},{24,16},{28,20},{1,9},{5... | collective-permute-start | bytes 589832 | tf_op jit(solution)/shard_map/ppermute | solution.py:43
  289.4 18.7 %all-to-all-start.7 = ((bf16[8,80,768]{2,1,0:T(8,128)(2,1)}), bf16[8,80,768]{2,1,0:T(8,128)(2,1)S(1)}, u32[]{:S(2)}, u32[]{:S(2)}) async-start(bf16[8,80,768]{2,1,0:T(8,128)(2,1)} %shard_map.184), calls=%async_computation.9 | async-start | bytes 1966080 | tf_op jit(solution)/shard_map/all_to_all | solution.py:89
  (21 other events, 40.2 us)
Sparse Core Ops, SparseCore 0:
  28.9 62.8 all-gather.2
  93.4 62.1 all-gather.4
  157.8 58.8 reduce-scatter.2
  218.9 60.2 reduce-scatter.4

commit v5 on v4

--- a/solution.py
+++ b/solution.py
@@ -12,7 +12,7 @@
 HIDDEN = -1e30
 ROW_TILE = 256
 VMEM = 24
-COST = 1.15e9
+COST = 2.3e+09
 CHUNKS = 2
 BF16 = jnp.bfloat16
 F32 = jnp.float32

time: 319 us -> 315 us (0.987)
  blocking collectives: 32.5 us -> 17.5 us
  local copies, waits for them, and re-layouts: 32 us -> 36.8 us
  waiting for transfers between devices: 98.7 us -> 102 us
    all_to_all x2 -> x1, blocking collectives: 32.5 us -> 17.5 us  [travel(): lax.all_to_all(value, 'frame', split_axis=0, concat_axis=0, tiled=True)]
    slice x4, local copies, waits for them, and re-layouts: 3.54 us -> 6.83 us  [to_positions(): lax.slice_in_dim(a, chunk * size, (chunk + 1) * size, axis=1)]
    all_to_all x5 -> x6, starting transfers between devices: 21.3 us -> 24.2 us  [travel(): lax.all_to_all(value, 'frame', split_axis=0, concat_axis=0, tiled=True)]
    all_to_all x5 -> x6, waiting for transfers between devices: 73.1 us -> 74.4 us  [travel(): lax.all_to_all(value, 'frame', split_axis=0, concat_axis=0, tiled=True)]
    unnamed x52 -> x56, local copies, waits for them, and re-layouts: 15.7 us -> 15.3 us
  transfers between devices with their start and end apart: 19 -> 20, of which waited for: 13 -> 14; matrix products, arithmetic and copies ran while one was open for 9% -> 11% of each run, Pallas kernels for 27% -> 27%
where the time goes in v5:
time: 315 us; the launch traced here: 313 us
  waiting for transfers between devices  102 us (32%)
  Pallas kernels  89.3 us (28%)
  local copies, waits for them, and re-layouts  36.8 us (12%)
  starting transfers between devices  36 us (11%)
  blocking collectives  17.5 us (6%)
  other arithmetic  16.7 us (5%)
  between operations  14.3 us (5%)
    all_to_all x6, waiting for transfers between devices, travel(): lax.all_to_all(value, 'frame', split_axis=0, concat_axis=0, tiled=True)  74.4 us
    all_to_all x6, starting transfers between devices, travel(): lax.all_to_all(value, 'frame', split_axis=0, concat_axis=0, tiled=True)  24.2 us
    pallas_call x2, Pallas kernels, attend_back(): pl.pallas_call(kernel, grid=(heads,), in_specs=[video_spec, *ref_specs] +...  23.9 us
    pallas_call x2, Pallas kernels, attend(): pl.pallas_call(kernel, grid=(heads,), in_specs=[pl.BlockSpec((count, 3, f...  17.8 us
    all_to_all x1, blocking collectives, travel(): lax.all_to_all(value, 'frame', split_axis=0, concat_axis=0, tiled=True)  17.5 us
    pallas_call x2, Pallas kernels, project_back(): pl.pallas_call(kernel, grid=(depth,), in_specs=[pl.BlockSpec((1, rows, ch...  16 us
    unnamed x56, local copies, waits for them, and re-layouts  15.3 us
    ppermute x9, waiting for transfers between devices, swap(): return lax.ppermute(value, 'frame', [(i, i ^ s) for i in range(count)])  15.2 us
  transfers between devices with their start and end apart: 20, of which 14 were waited for; matrix products, arithmetic and copies ran while one was open for 11% of the time, Pallas kernels for 27%

profile of v5, /device:TPU:0, one launch (start us, length us, event | category | flops | bytes accessed | tf_op | source)
XLA Modules:
  0.0 312.9 jit_solution(5742873622759591004)
XLA Ops:
  8.8 17.5 %all_to_all.40 = bf16[8,1,2,32,768]{4,3,2,1,0:T(8,128)(2,1)S(1)} all-to-all(bf16[8,1,2,32,768]{4,3,2,1,0:T(8,128)(2,1)S(1)} %copy.56), channel_id=1, replica_groups=mesh['frame'=8,'head'=4] {'frame'}, dimensions={0} | all-to-all | bytes 1572864 | tf_op jit(solution)/shard_map/all_to_all | solution.py:89
  45.5 4.1 %all-to-all-done.1 = bf16[8,1,2,32,768]{4,3,2,1,0:T(8,128)(2,1)S(1)} async-done(((bf16[8,1,2,32,768]{4,3,2,1,0:T(8,128)(2,1)}), bf16[8,1,2,32,768]{4,3,2,1,0:T(8,128)(2,1)S(1)}, u32[]{:S(2)}, u32[]{:S(2)}) %all-to-all-start.1) | async-done | bytes 786464 | tf_op jit(solution)/shard_map/all_to_all | solution.py:89
  52.9 4.7 %collective-permute-done.2.refs_3_ = bf16[2,64,768]{2,1,0:T(8,128)(2,1)S(1)} collective-permute-done((bf16[2,64,768]{2,1,0:T(8,128)(2,1)S(1)}, bf16[2,64,768]{2,1,0:T(8,128)(2,1)S(1)}, u32[]{:S(2)}, u32[]{:S(2)}) %collective-permute-start.2) | collective-permute-done | bytes 196640 | tf_op jit(solution)/shard_map/ppermute | solution.py:43
  57.6 4.5 %all-to-all-start.2 = ((bf16[8,3,2,32,768]{4,3,2,1,0:T(8,128)(2,1)}), bf16[8,3,2,32,768]{4,3,2,1,0:T(8,128)(2,1)}, u32[]{:S(2)}, u32[]{:S(2)}) async-start(bf16[8,3,2,32,768]{4,3,2,1,0:T(8,128)(2,1)} %pad_maximum_fusion), calls=%async_computation.2 | async-start | bytes 4718592 | tf_op jit(solution)/shard_map/all_to_all | solution.py:89
  67.3 24.4 %all-to-all-done.2.video_ref = bf16[8,3,2,32,768]{4,3,2,1,0:T(8,128)(2,1)} async-done(((bf16[8,3,2,32,768]{4,3,2,1,0:T(8,128)(2,1)}), bf16[8,3,2,32,768]{4,3,2,1,0:T(8,128)(2,1)}, u32[]{:S(2)}, u32[]{:S(2)}) %all-to-all-start.2) | async-done | bytes 2359328 | tf_op jit(solution)/shard_map/all_to_all | solution.py:89
  95.3 9.0 %shard_map.173 = (bf16[8,2,32,768]{3,2,1,0:T(8,128)(2,1)}, bf16[6,2,256,256]{3,2,1,0:T(8,128)(2,1)}, bf16[6,2,512,256]{3,2,1,0:T(8,128)(2,1)}, f32[6,2,2,256]{3,2,1,0:T(2,128)}, bf16[6,2,2,128,256]{4,3,2,1,0:T(8,128)(2,1)}) custom-call(bf16[8,3,2,32,768]{4,3,2,1,0:T(8,128)(2,1)} %all-to-all-done.2.video_ref, bf16[4,2,64,768]{3,2,1,0:T(8,128)(2,1)} %copy-done.10, ...), custom_call_target="tpu_custom_call" | custom-call | flops 18400000000 | tf_op jit(solution)/shard_map/pallas_call | solution.py:164
  104.3 6.4 %shard_map.174.rest_0_ = bf16[4,512,768]{2,1,0:T(8,128)(2,1)} custom-call(bf16[512,768]{1,0:T(8,128)(2,1)} %bitcast.127, bf16[768,3072]{1,0:T(8,128)(2,1)} %weight_ref.7), custom_call_target="tpu_custom_call" | custom-call | flops 9200000000 | tf_op jit(solution)/shard_map/pallas_call | solution.py:333
  110.8 8.0 %shard_map.175.rest_0_ = bf16[512,768]{1,0:T(8,128)(2,1)} custom-call(bf16[4,512,768]{2,1,0:T(8,128)(2,1)} %all-gather.3.cloned.1.call-done.blocks_ref.refs_2_, bf16[768,3072]{1,0:T(8,128)(2,1)} %weight_ref.7, bf16[4,512,768]{2,1,0:T(8,128)(2,1)} %shard_map.174.rest_0_), custom_call_target="tpu_custom_call" | custom-call | flops 13799999488 | tf_op jit(solution)/shard_map/pallas_call | solution.py:370
  118.8 11.6 %shard_map.176 = (bf16[8,3,2,32,768]{4,3,2,1,0:T(8,128)(2,1)}, f32[4,2,64,768]{3,2,1,0:T(8,128)}, f32[4,2,64,768]{3,2,1,0:T(8,128)}) custom-call(bf16[8,3,2,32,768]{4,3,2,1,0:T(8,128)(2,1)} %all-to-all-done.2.video_ref, bf16[4,2,64,768]{3,2,1,0:T(8,128)(2,1)} %copy-done.10, bf16[4,2,64,768]{3,2,1,0:T(8,128)(2,1)} %collective-permute-done.3.odd_ref, ...), custom_call_target="tpu_custom_call" | custom-call | flops 23000000512 | tf_op jit(solution)/shard_map/pallas_call | solution.py:225
  131.9 4.1 %all-to-all-start.4 = ((bf16[8,3,2,32,768]{4,3,2,1,0:T(8,128)(2,1)}), bf16[8,3,2,32,768]{4,3,2,1,0:T(8,128)(2,1)S(1)}, u32[]{:S(2)}, u32[]{:S(2)}) async-start(bf16[8,3,2,32,768]{4,3,2,1,0:T(8,128)(2,1)} %get-tuple-element.46), calls=%async_computation.5 | async-start | bytes 4718592 | tf_op jit(solution)/shard_map/all_to_all | solution.py:89
  136.0 8.8 %shard_map.177 = (bf16[8,2,32,768]{3,2,1,0:T(8,128)(2,1)}, bf16[6,2,256,256]{3,2,1,0:T(8,128)(2,1)}, bf16[6,2,512,256]{3,2,1,0:T(8,128)(2,1)}, f32[6,2,2,256]{3,2,1,0:T(2,128)}, bf16[6,2,2,128,256]{4,3,2,1,0:T(8,128)(2,1)}) custom-call(bf16[8,3,2,32,768]{4,3,2,1,0:T(8,128)(2,1)} %copy-done.20, bf16[4,2,64,768]{3,2,1,0:T(8,128)(2,1)} %copy-done.10, ...), custom_call_target="tpu_custom_call" | custom-call | flops 18400000000 | tf_op jit(solution)/shard_map/pallas_call | solution.py:164
  144.8 6.5 %shard_map.178.refs_4_ = bf16[4,512,768]{2,1,0:T(8,128)(2,1)} custom-call(bf16[512,768]{1,0:T(8,128)(2,1)} %bitcast.129, bf16[768,3072]{1,0:T(8,128)(2,1)} %weight_ref.7), custom_call_target="tpu_custom_call" | custom-call | flops 9200000000 | tf_op jit(solution)/shard_map/pallas_call | solution.py:333
  151.3 4.8 %all-gather.5.cloned.1.call-done.refs_3_.blocks_ref = bf16[4,512,768]{2,1,0:T(8,128)(2,1)} async-done(((bf16[1,512,768]{2,1,0:T(8,128)(2,1)}), bf16[4,512,768]{2,1,0:T(8,128)(2,1)}) %all-gather.5.cloned.1.call-update) | async-done | bytes 3145744 | tf_op jit(solution)/shard_map/all_gather | solution.py:469
  156.1 9.3 %all-to-all-done.4.refs_5_ = bf16[8,3,2,32,768]{4,3,2,1,0:T(8,128)(2,1)S(1)} async-done(((bf16[8,3,2,32,768]{4,3,2,1,0:T(8,128)(2,1)}), bf16[8,3,2,32,768]{4,3,2,1,0:T(8,128)(2,1)S(1)}, u32[]{:S(2)}, u32[]{:S(2)}) %all-to-all-start.4) | async-done | bytes 2359328 | tf_op jit(solution)/shard_map/all_to_all | solution.py:89
  166.9 9.5 %shard_map.179.terms_ref = bf16[4,2,768,384]{3,2,1,0:T(8,128)(2,1)} custom-call(bf16[512,768]{1,0:T(8,128)(2,1)} %bitcast.128, bf16[512,768]{1,0:T(8,128)(2,1)} %bitcast.130, bf16[4,512,768]{2,1,0:T(8,128)(2,1)} %all-gather.3.cloned.1.call-done.blocks_ref.refs_2_, bf16[4,512,768]{2,1,0:T(8,128)(2,1)} %all-gather.5.cloned.1.call-done.refs_3_.blocks_ref, ...), custom_call_target="tpu_custom_call" | custom-call | flops 16099999744 | tf_op jit(solution)/shard_map/pallas_call | solution.py:407
  179.6 4.7 %collective-permute-done.4.near_ref = bf16[4,768,384]{2,1,0:T(8,128)(2,1)S(1)} collective-permute-done((bf16[4,768,384]{2,1,0:T(8,128)(2,1)}, bf16[4,768,384]{2,1,0:T(8,128)(2,1)S(1)}, u32[]{:S(2)}, u32[]{:S(2)}) %collective-permute-start.4) | collective-permute-done | bytes 2359328 | tf_op jit(solution)/shard_map/ppermute | solution.py:43
  188.8 3.8 %all-to-all-start.5 = ((bf16[4,768,384]{2,1,0:T(8,128)(2,1)}), bf16[4,768,384]{2,1,0:T(8,128)(2,1)S(1)}, u32[]{:S(2)}, u32[]{:S(2)}) async-start(bf16[4,768,384]{2,1,0:T(8,128)(2,1)} %copy-done.2), calls=%async_computation.6 | async-start | bytes 4718592 | tf_op jit(solution)/shard_map/all_to_all | solution.py:516
  192.6 8.0 %shard_map.181.rest_0_ = bf16[512,768]{1,0:T(8,128)(2,1)} custom-call(bf16[4,512,768]{2,1,0:T(8,128)(2,1)} %all-gather.5.cloned.1.call-done.refs_3_.blocks_ref, bf16[768,3072]{1,0:T(8,128)(2,1)} %weight_ref.7, bf16[4,768,384]{2,1,0:T(8,128)(2,1)} %copy-done.2), custom_call_target="tpu_custom_call" | custom-call | flops 13799999488 | tf_op jit(solution)/shard_map/pallas_call | solution.py:370
  200.6 12.3 %shard_map.182 = (bf16[8,4,2,32,768]{4,3,2,1,0:T(8,128)(2,1)}, f32[4,2,64,768]{3,2,1,0:T(8,128)}, f32[4,2,64,768]{3,2,1,0:T(8,128)}) custom-call(bf16[8,3,2,32,768]{4,3,2,1,0:T(8,128)(2,1)} %copy-done.20, bf16[4,2,64,768]{3,2,1,0:T(8,128)(2,1)} %copy-done.10, bf16[4,2,64,768]{3,2,1,0:T(8,128)(2,1)} %collective-permute-done.3.odd_ref, ...), custom_call_target="tpu_custom_call" | custom-call | flops 23000000512 | tf_op jit(solution)/shard_map/pallas_call | solution.py:225
  212.9 4.5 %reduce-scatter.3.cloned.1.call-done = bf16[1,512,768]{2,1,0:T(8,128)(2,1)} async-done(((bf16[4,512,768]{2,1,0:T(8,128)(2,1)}), bf16[1,512,768]{2,1,0:T(8,128)(2,1)}) %reduce-scatter.3.cloned.1.call-update) | async-done | bytes 786448 | tf_op jit(solution)/shard_map/reduce_scatter | solution.py:489
  227.8 4.5 %all-to-all-start.6 = ((bf16[8,4,2,32,768]{4,3,2,1,0:T(8,128)(2,1)}), bf16[8,4,2,32,768]{4,3,2,1,0:T(8,128)(2,1)}, u32[]{:S(2)}, u32[]{:S(2)}) async-start(bf16[8,4,2,32,768]{4,3,2,1,0:T(8,128)(2,1)} %copy-done.1), calls=%async_computation.7 | async-start | bytes 6291456 | tf_op jit(solution)/shard_map/all_to_all | solution.py:89
  240.1 30.0 %all-to-all-done.6 = bf16[8,4,2,32,768]{4,3,2,1,0:T(8,128)(2,1)} async-done(((bf16[8,4,2,32,768]{4,3,2,1,0:T(8,128)(2,1)}), bf16[8,4,2,32,768]{4,3,2,1,0:T(8,128)(2,1)}, u32[]{:S(2)}, u32[]{:S(2)}) %all-to-all-start.6) | async-done | bytes 3145760 | tf_op jit(solution)/shard_map/all_to_all | solution.py:89
  285.7 4.0 %all-to-all-start.7 = ((bf16[8,80,768]{2,1,0:T(8,128)(2,1)}), bf16[8,80,768]{2,1,0:T(8,128)(2,1)S(1)}, u32[]{:S(2)}, u32[]{:S(2)}) async-start(bf16[8,80,768]{2,1,0:T(8,128)(2,1)} %shard_map.184), calls=%async_computation.9 | async-start | bytes 1966080 | tf_op jit(solution)/shard_map/all_to_all | solution.py:89
  297.7 6.7 %all-to-all-done.7 = bf16[8,80,768]{2,1,0:T(8,128)(2,1)S(1)} async-done(((bf16[8,80,768]{2,1,0:T(8,128)(2,1)}), bf16[8,80,768]{2,1,0:T(8,128)(2,1)S(1)}, u32[]{:S(2)}, u32[]{:S(2)}) %all-to-all-start.7) | async-done | bytes 983072 | tf_op jit(solution)/shard_map/all_to_all | solution.py:89
  (136 shorter events, 87.1 us)
Async XLA Ops:
  7.2 103.6 %all-gather.3.cloned.1.call-start = ((), (), s32[]{:S(2)}) async-start(), calls=%async_computation.11 | async-start | bytes 3932160 | tf_op jit(solution)/shard_map/all_gather | solution.py:469
  8.7 17.6 %copy-start.13 = (f32[3,768]{1,0:T(4,128)S(1)}, f32[3,768]{1,0:T(4,128)}, u32[]{:S(2)}) copy-start(f32[3,768]{1,0:T(4,128)} %taps_ref.7) | copy-start | bytes 27652
  33.0 16.6 %all-to-all-start.1 = ((bf16[8,1,2,32,768]{4,3,2,1,0:T(8,128)(2,1)}), bf16[8,1,2,32,768]{4,3,2,1,0:T(8,128)(2,1)S(1)}, u32[]{:S(2)}, u32[]{:S(2)}) async-start(bf16[8,1,2,32,768]{4,3,2,1,0:T(8,128)(2,1)} %copy.57), calls=%async_computation.1 | async-start | bytes 1572864 | tf_op jit(solution)/shard_map/all_to_all | solution.py:89
  36.5 119.6 %all-gather.5.cloned.1.call-start = ((), (), s32[]{:S(2)}) async-start(), calls=%async_computation.12 | async-start | bytes 3932160 | tf_op jit(solution)/shard_map/all_gather | solution.py:469
  42.0 10.9 %collective-permute-start = (bf16[2,64,768]{2,1,0:T(8,128)(2,1)S(1)}, bf16[2,64,768]{2,1,0:T(8,128)(2,1)S(1)}, u32[]{:S(2)}, u32[]{:S(2)}) collective-permute-start(bf16[2,64,768]{2,1,0:T(8,128)(2,1)S(1)} %pad_maximum_fusion.6.refs_0_), channel_id=1, source_target_pairs={{0,8},{4,12},{8,0},{12,4},{16,24},{20,28},{24,16},{28,20},{1,9},{5... | collective-permute-start | bytes 589832 | tf_op jit(solution)/shard_map/ppermute | solution.py:43
  43.9 9.0 %collective-permute-start.1 = (bf16[2,64,768]{2,1,0:T(8,128)(2,1)S(1)}, bf16[2,64,768]{2,1,0:T(8,128)(2,1)S(1)}, u32[]{:S(2)}, u32[]{:S(2)}) collective-permute-start(bf16[2,64,768]{2,1,0:T(8,128)(2,1)S(1)} %pad_maximum_fusion.6.refs_0_), channel_id=1, source_target_pairs={{0,16},{4,20},{8,24},{12,28},{16,0},{20,4},{24,8},{28,12},{1,17},{... | collective-permute-start | bytes 589832 | tf_op jit(solution)/shard_map/ppermute | solution.py:43
  45.3 12.2 %collective-permute-start.2 = (bf16[2,64,768]{2,1,0:T(8,128)(2,1)S(1)}, bf16[2,64,768]{2,1,0:T(8,128)(2,1)S(1)}, u32[]{:S(2)}, u32[]{:S(2)}) collective-permute-start(bf16[2,64,768]{2,1,0:T(8,128)(2,1)S(1)} %pad_maximum_fusion.6.refs_0_), channel_id=1, source_target_pairs={{0,24},{4,28},{8,16},{12,20},{16,8},{20,12},{24,0},{28,4},{1,25},{... | collective-permute-start | bytes 589832 | tf_op jit(solution)/shard_map/ppermute | solution.py:43
  57.6 34.0 %all-to-all-start.2 = ((bf16[8,3,2,32,768]{4,3,2,1,0:T(8,128)(2,1)}), bf16[8,3,2,32,768]{4,3,2,1,0:T(8,128)(2,1)}, u32[]{:S(2)}, u32[]{:S(2)}) async-start(bf16[8,3,2,32,768]{4,3,2,1,0:T(8,128)(2,1)} %pad_maximum_fusion), calls=%async_computation.2 | async-start | bytes 4718592 | tf_op jit(solution)/shard_map/all_to_all | solution.py:89
  62.3 33.0 %collective-permute-start.3 = (bf16[4,2,64,768]{3,2,1,0:T(8,128)(2,1)S(1)}, bf16[4,2,64,768]{3,2,1,0:T(8,128)(2,1)}, u32[]{:S(2)}, u32[]{:S(2)}) collective-permute-start(bf16[4,2,64,768]{3,2,1,0:T(8,128)(2,1)S(1)} %shard_map.172.even_ref), channel_id=1, source_target_pairs={{0,4},{4,0},{8,12},{12,8},{16,20},{20,16},{24,28},{28,24},{1,5},{5... | collective-permute-start | bytes 2359304 | tf_op jit(solution)/shard_map/ppermute | solution.py:43
  91.6 38.8 %all-to-all-start.3 = ((bf16[8,3,2,32,768]{4,3,2,1,0:T(8,128)(2,1)}), bf16[8,3,2,32,768]{4,3,2,1,0:T(8,128)(2,1)S(1)}, u32[]{:S(2)}, u32[]{:S(2)}) async-start(bf16[8,3,2,32,768]{4,3,2,1,0:T(8,128)(2,1)} %pad_maximum_fusion.1), calls=%async_computation.4 | async-start | bytes 4718592 | tf_op jit(solution)/shard_map/all_to_all | solution.py:89
  95.2 122.1 %reduce-scatter.3.cloned.1.call-start = ((), (), s32[]{:S(2)}) async-start(), calls=%async_computation.10 | async-start | bytes 3932160 | tf_op jit(solution)/shard_map/reduce_scatter | solution.py:489
  131.9 33.6 %all-to-all-start.4 = ((bf16[8,3,2,32,768]{4,3,2,1,0:T(8,128)(2,1)}), bf16[8,3,2,32,768]{4,3,2,1,0:T(8,128)(2,1)S(1)}, u32[]{:S(2)}, u32[]{:S(2)}) async-start(bf16[8,3,2,32,768]{4,3,2,1,0:T(8,128)(2,1)} %get-tuple-element.46), calls=%async_computation.5 | async-start | bytes 4718592 | tf_op jit(solution)/shard_map/all_to_all | solution.py:89
  136.0 145.9 %reduce-scatter.5.cloned.1.call-start = ((), (), s32[]{:S(2)}) async-start(), calls=%async_computation.13 | async-start | bytes 3932160 | tf_op jit(solution)/shard_map/reduce_scatter | solution.py:489
  179.6 4.7 %collective-permute-start.4 = (bf16[4,768,384]{2,1,0:T(8,128)(2,1)}, bf16[4,768,384]{2,1,0:T(8,128)(2,1)S(1)}, u32[]{:S(2)}, u32[]{:S(2)}) collective-permute-start(bf16[4,768,384]{2,1,0:T(8,128)(2,1)} %dynamic-slice_bitcast_fusion), channel_id=1, source_target_pairs={{0,4},{4,0},{8,12},{12,8},{16,20},{20,16},{24,28},{28,24},{1,5},{5... | collective-permute-start | bytes 7077896 | tf_op jit(solution)/shard_map/ppermute | solution.py:43
  188.8 31.9 %all-to-all-start.5 = ((bf16[4,768,384]{2,1,0:T(8,128)(2,1)}), bf16[4,768,384]{2,1,0:T(8,128)(2,1)S(1)}, u32[]{:S(2)}, u32[]{:S(2)}) async-start(bf16[4,768,384]{2,1,0:T(8,128)(2,1)} %copy-done.2), calls=%async_computation.6 | async-start | bytes 4718592 | tf_op jit(solution)/shard_map/all_to_all | solution.py:516
  200.6 20.1 %copy-start.9 = (bf16[8,1,2,32,768]{4,3,2,1,0:T(8,128)(2,1)S(1)}, bf16[8,1,2,32,768]{4,3,2,1,0:T(8,128)(2,1)}, u32[]{:S(2)}) copy-start(bf16[8,1,2,32,768]{4,3,2,1,0:T(8,128)(2,1)} %copy-done.8) | copy-start | bytes 2359300
  200.6 20.1 %copy-start.14 = (f32[3,768]{1,0:T(4,128)S(1)}, f32[3,768]{1,0:T(4,128)}, u32[]{:S(2)}) copy-start(f32[3,768]{1,0:T(4,128)} %taps_ref.7) | copy-start | bytes 27652
  227.8 42.4 %all-to-all-start.6 = ((bf16[8,4,2,32,768]{4,3,2,1,0:T(8,128)(2,1)}), bf16[8,4,2,32,768]{4,3,2,1,0:T(8,128)(2,1)}, u32[]{:S(2)}, u32[]{:S(2)}) async-start(bf16[8,4,2,32,768]{4,3,2,1,0:T(8,128)(2,1)} %copy-done.1), calls=%async_computation.7 | async-start | bytes 6291456 | tf_op jit(solution)/shard_map/all_to_all | solution.py:89
  235.4 34.8 %collective-permute-start.5 = (bf16[4,2,64,768]{3,2,1,0:T(8,128)(2,1)}, bf16[4,2,64,768]{3,2,1,0:T(8,128)(2,1)S(1)}, u32[]{:S(2)}, u32[]{:S(2)}) collective-permute-start(bf16[4,2,64,768]{3,2,1,0:T(8,128)(2,1)} %add_convert_fusion), channel_id=1, source_target_pairs={{0,4},{4,0},{8,12},{12,8},{16,20},{20,16},{24,28},{28,24},{1,5},{5... | collective-permute-start | bytes 2359304 | tf_op jit(solution)/shard_map/ppermute | solution.py:43
  271.9 8.2 %collective-permute-start.8 = (bf16[2,64,768]{2,1,0:T(8,128)(2,1)S(1)}, bf16[2,64,768]{2,1,0:T(8,128)(2,1)S(1)}, u32[]{:S(2)}, u32[]{:S(2)}) collective-permute-start(bf16[2,64,768]{2,1,0:T(8,128)(2,1)S(1)} %get-tuple-element.72), channel_id=1, source_target_pairs={{0,24},{4,28},{8,16},{12,20},{16,8},{20,12},{24,0},{28,4},{1,25},{... | collective-permute-start | bytes 589832 | tf_op jit(solution)/shard_map/ppermute | solution.py:43
  272.5 9.0 %collective-permute-start.7 = (bf16[2,64,768]{2,1,0:T(8,128)(2,1)S(1)}, bf16[2,64,768]{2,1,0:T(8,128)(2,1)S(1)}, u32[]{:S(2)}, u32[]{:S(2)}) collective-permute-start(bf16[2,64,768]{2,1,0:T(8,128)(2,1)S(1)} %get-tuple-element.73), channel_id=1, source_target_pairs={{0,16},{4,20},{8,24},{12,28},{16,0},{20,4},{24,8},{28,12},{1,17},{... | collective-permute-start | bytes 589832 | tf_op jit(solution)/shard_map/ppermute | solution.py:43
  273.9 8.0 %copy-start.7 = (bf16[8,1,2,32,768]{4,3,2,1,0:T(8,128)(2,1)S(1)}, bf16[8,1,2,32,768]{4,3,2,1,0:T(8,128)(2,1)}, u32[]{:S(2)}) copy-start(bf16[8,1,2,32,768]{4,3,2,1,0:T(8,128)(2,1)} %copy-done.6) | copy-start | bytes 2359300
  273.9 7.9 %collective-permute-start.6 = (bf16[2,64,768]{2,1,0:T(8,128)(2,1)S(1)}, bf16[2,64,768]{2,1,0:T(8,128)(2,1)S(1)}, u32[]{:S(2)}, u32[]{:S(2)}) collective-permute-start(bf16[2,64,768]{2,1,0:T(8,128)(2,1)S(1)} %get-tuple-element.71), channel_id=1, source_target_pairs={{0,8},{4,12},{8,0},{12,4},{16,24},{20,28},{24,16},{28,20},{1,9},{5... | collective-permute-start | bytes 589832 | tf_op jit(solution)/shard_map/ppermute | solution.py:43
  285.7 18.7 %all-to-all-start.7 = ((bf16[8,80,768]{2,1,0:T(8,128)(2,1)}), bf16[8,80,768]{2,1,0:T(8,128)(2,1)S(1)}, u32[]{:S(2)}, u32[]{:S(2)}) async-start(bf16[8,80,768]{2,1,0:T(8,128)(2,1)} %shard_map.184), calls=%async_computation.9 | async-start | bytes 1966080 | tf_op jit(solution)/shard_map/all_to_all | solution.py:89
  (24 other events, 57.4 us)
Sparse Core Ops, SparseCore 0:
  28.9 62.8 all-gather.2
  93.9 62.1 all-gather.4
  158.4 58.8 reduce-scatter.2
  219.5 60.2 reduce-scatter.4
